TPU v7x, 256 devices: a whole 4x4x8 slice. The times are simulated.
256 devices in a mesh: particle: 32 (over x, z), token: 8 (over y, core).
Axes of the slice: x: 4, y: 4, z: 8, core: 2. Of those that a mesh axis runs over, the one named last changes fastest.
Arguments:
- states: bfloat16 [64, 512, 768], P('particle', 'token'), may hold values from -6 to 6
- ancestors: int32 [64], P('particle'), may hold values from 0 to 63, as said below
- pair_bias: bfloat16 [16, 512, 512], P(None, 'token'), may hold values from -3 to 300, as said below
- key_mask: int32 [512], replicated, may hold values from 0 to 1, as said below
- gain_attn: float32 [768], replicated, may hold values from 0.1 to 1.9
- w_qkv: bfloat16 [768, 2304], replicated, may hold values from -0.21875 to 0.21875
- w_o: bfloat16 [768, 768], replicated, may hold values from -0.21875 to 0.21875
- gain_ff: float32 [768], replicated, may hold values from 0.1 to 1.9
- w_in: bfloat16 [2, 768, 1536], P(None, 'particle'), may hold values from -0.21875 to 0.21875
- w_out: bfloat16 [768, 1536], P('particle'), may hold values from -0.15625 to 0.15625
Outputs:
- new_states: bfloat16 [64, 512, 768], P('particle', 'token')
Inputs may be any that keep to these rules, and one draw needn't show every extreme that they name: `ancestors`: any particle may be the ancestor of any number of particles. `pair_bias`: real values; rows of some heads may hold a few large entries. `key_mask`: 1 on a prefix of 256 or more tokens and 0 after it; the last token is always 0.
All inputs are finite; a program needn't handle non-finite values.
Results may differ from a plain program's by a relative error of at most 0.0085.
Values may be sent and summed in bfloat16 or wider, within the bound.
No kernel may reach another device: no remote copies, remote signals or barrier semaphores. Data moves between devices by JAX's collectives and lax.ppermute only.
A program may use at most 64 MiB of HBM per device.

v0:
```python
import math

import jax
import jax.numpy as jnp
from jax import lax
from jax.sharding import PartitionSpec as P


def rms_norm(stream, gain_vec):
    return stream * lax.rsqrt(jnp.mean(stream * stream, axis=-1, keepdims=True) + 1e-05) * gain_vec


def attend_portion(running_sum, queries, key_part, value_part, pair_bias, key_mask):
    running, totals, summed = running_sum
    part_count, row_count, model_width = queries.shape
    head_count = pair_bias.shape[0]
    head_size = model_width // head_count
    number = key_part.shape[1]
    query_heads = queries.reshape(part_count, row_count, head_count, head_size)
    key_heads = key_part.reshape(part_count, number, head_count, head_size)
    value_heads = value_part.reshape(part_count, number, head_count, head_size)
    scores = jnp.einsum(
        "prhe,pnhe->phrn", query_heads, key_heads, preferred_element_type=jnp.float32
    )
    bias_part = pair_bias.astype(jnp.float32)
    scores = scores + bias_part[None]
    usable = (key_mask > 0)[None, None, None, :]
    new_max = jnp.maximum(running, jnp.max(jnp.where(usable, scores, -1e30), axis=3))
    weights = jnp.where(usable, jnp.exp(scores - new_max[..., None]), 0.0)
    totals = jnp.sum(weights, axis=3)
    summed = jnp.einsum(
        "phrn,pnhe->phre",
        weights.astype(jnp.bfloat16),
        value_heads,
        preferred_element_type=jnp.float32,
    )
    return (new_max, totals, summed)


def run_block(states, pair_bias, key_mask, gain_attn, w_qkv, w_o, gain_ff, w_in, w_out):
    part_count, row_count, model_width = states.shape
    head_count = pair_bias.shape[0]
    head_size = model_width // head_count
    score_scale = 1.0 / math.sqrt(head_size)
    stream = states.astype(jnp.float32)
    normed = rms_norm(stream, gain_attn).astype(jnp.bfloat16)
    start_carry = (
        jnp.full((part_count, head_count, row_count), -1e30, jnp.float32),
        jnp.zeros((part_count, head_count, row_count), jnp.float32),
        jnp.zeros((part_count, head_count, row_count, head_size), jnp.float32),
    )
    projected = jnp.einsum("prd,de->pre", normed, w_qkv, preferred_element_type=jnp.float32)
    queries = (projected[..., :model_width] * score_scale).astype(jnp.bfloat16)
    key_local = projected[..., model_width : 2 * model_width].astype(jnp.bfloat16)
    value_local = projected[..., 2 * model_width :].astype(jnp.bfloat16)
    portion = (
        lax.all_gather(key_local, "token", axis=1, tiled=True),
        lax.all_gather(value_local, "token", axis=1, tiled=True),
    )
    running, totals, summed = attend_portion(
        start_carry, queries, portion[0], portion[1], pair_bias, key_mask
    )
    attended = (
        (summed / totals[..., None])
        .transpose(0, 2, 1, 3)
        .reshape(part_count, row_count, model_width)
        .astype(jnp.bfloat16)
    )
    stream = stream + jnp.einsum("prd,de->pre", attended, w_o, preferred_element_type=jnp.float32)
    normed_ff = rms_norm(stream, gain_ff).astype(jnp.bfloat16)
    portion = lax.all_gather(w_in, "particle", axis=1, tiled=True)
    gate_sum = jnp.einsum("prd,df->prf", normed_ff, portion[0], preferred_element_type=jnp.float32)
    up_sum = jnp.einsum("prd,df->prf", normed_ff, portion[1], preferred_element_type=jnp.float32)
    hidden = (jax.nn.silu(gate_sum) * up_sum).astype(jnp.bfloat16)
    update = jnp.einsum(
        "prf,nf->prn",
        hidden,
        lax.all_gather(w_out, "particle", axis=0, tiled=True),
        preferred_element_type=jnp.float32,
    )
    return (stream + update).astype(jnp.bfloat16)


def select_rows(ancestors, portion):
    number = portion.shape[0]
    indices = lax.iota(jnp.int32, number)
    onehot = (ancestors[:, None] == indices[None, :]).astype(jnp.bfloat16)
    return jnp.einsum("jp,prd->jrd", onehot, portion, preferred_element_type=jnp.float32)


def body(states, ancestors, pair_bias, key_mask, gain_attn, w_qkv, w_o, gain_ff, w_in, w_out):
    chosen = select_rows(ancestors, lax.all_gather(states, "particle", axis=0, tiled=True)).astype(
        jnp.bfloat16
    )
    return run_block(chosen, pair_bias, key_mask, gain_attn, w_qkv, w_o, gain_ff, w_in, w_out)


def solution(mesh):
    placed = (
        P("particle", "token", None),
        P("particle"),
        P(None, "token", None),
        P(),
        P(),
        P(),
        P(),
        P(),
        P(None, "particle", None),
        P("particle", None),
    )
    return jax.shard_map(
        body, mesh=mesh, in_specs=placed, out_specs=P("particle", "token", None), check_vma=False
    )
```

profile of v0, /device:TPU:1, one launch (start us, length us, event | category | flops | bytes accessed | tf_op | source)
XLA Modules:
  0.0 342.5 jit_solution(17704252850291132048)
XLA Ops:
  6.5 0.0 copy-start
  6.5 0.0 copy-start.7
  6.5 0.0 all-gather.6.cloned.1.call-start
  6.5 0.7 all-gather.6.cloned.1.call-update
  7.3 0.0 all-gather.8.cloned.1.call-start
  7.3 94.8 %all-gather.6.cloned.1.call-done = bf16[64,64,768]{2,1,0:T(8,128)(2,1)} async-done(((bf16[2,64,768]{2,1,0:T(8,128)(2,1)}), bf16[64,64,768]{2,1,0:T(8,128)(2,1)}) %all-gather.6.cloned.1.call-update) | async-done | bytes 6291472 | tf_op jit(solution)/shard_map/all_gather | solution.py:92
  102.1 9.6 %multiply_reduce_fusion.1 = (f32[2,64]{0,1:T(8,128)S(1)}, f32[2,64,768]{2,0,1:T(2,128)S(1)}) fusion(bf16[64,64,768]{2,1,0:T(8,128)(2,1)} %all-gather.6.cloned.1.call-done, s32[2]{0:T(128)} %param.11), kind=kOutput, calls=%fused_computation.41 | convolution fusion | flops 12976128 | bytes 6685192 | tf_op jit(solution)/shard_map/jp,prd->jrd/dot_general | solution.py:88
  111.7 0.0 copy-start.2
  111.7 0.0 copy-done.7
  111.7 0.2 multiply_convert_fusion.1
  112.0 0.0 copy-done
  112.0 1.7 fusion.52
  113.7 0.0 copy-done.2
  113.7 0.0 copy-start.9
  113.7 0.8 fusion.51
  114.5 0.0 all-gather.8.cloned.1.call-update
  114.5 0.0 all-gather.10.cloned.1.call-start
  114.6 0.7 all-gather.10.cloned.1.call-update
  115.3 0.0 all-gather.12.cloned.1.call-start
  115.3 0.5 all-gather.12.cloned.1.call-update
  115.9 0.2 all-gather.14.cloned.1.call-start
  116.1 0.4 all-gather.14.cloned.1.call-update
  116.4 2.9 convert_element_type.40
  119.3 0.0 copy-done.9
  119.3 1.7 fusion.38
  121.0 1.9 copy.71
  122.9 16.5 %all-gather.8.cloned.1.call-done = bf16[2,512,768]{2,1,0:T(8,128)(2,1)} async-done(((bf16[2,64,768]{2,1,0:T(8,128)(2,1)}), bf16[2,512,768]{2,1,0:T(8,128)(2,1)}) %all-gather.8.cloned.1.call-update) | async-done | bytes 1572880 | tf_op jit(solution)/shard_map/all_gather | solution.py:57
  139.4 2.6 copy.59
  142.0 26.4 %all-gather.10.cloned.1.call-done = bf16[2,512,768]{2,1,0:T(8,128)(2,1)} async-done(((bf16[2,64,768]{2,1,0:T(8,128)(2,1)}), bf16[2,512,768]{2,1,0:T(8,128)(2,1)}) %all-gather.10.cloned.1.call-update) | async-done | bytes 1572880 | tf_op jit(solution)/shard_map/all_gather | solution.py:58
  168.4 2.6 copy.61
  171.0 0.0 copy-start.1
  171.0 3.2 select_reduce_fusion
  174.1 0.0 copy-start.5
  174.2 0.0 copy-done.1
  174.2 1.2 fusion.4
  175.4 0.2 copy-done.5
  175.5 0.0 copy-start.6
  175.5 0.0 copy-start.3
  175.6 0.0 copy-start.8
  175.6 1.2 fusion.30
  176.7 0.1 copy-done.6
  176.8 0.4 fusion.19
  177.2 0.0 copy-done.3
  177.2 0.0 copy-start.4
  177.2 0.4 multiply_reduce_fusion
  177.6 0.4 copy-done.4
  178.0 0.0 copy-done.8
  178.0 1.1 multiply_convert_fusion
  179.1 72.3 %all-gather.12.cloned.1.call-done = bf16[2,768,1536]{2,1,0:T(8,128)(2,1)} async-done(((bf16[2,24,1536]{2,1,0:T(8,128)(2,1)}), bf16[2,768,1536]{2,1,0:T(8,128)(2,1)}) %all-gather.12.cloned.1.call-update) | async-done | bytes 4718608 | tf_op jit(solution)/shard_map/all_gather | solution.py:71
  251.4 3.1 fusion.7
  254.5 74.2 %all-gather.14.cloned.1.call-done = bf16[768,1536]{1,0:T(8,128)(2,1)} async-done(((bf16[24,1536]{1,0:T(8,128)(2,1)}), bf16[768,1536]{1,0:T(8,128)(2,1)}) %all-gather.14.cloned.1.call-update) | async-done | bytes 2359312 | tf_op jit(solution)/shard_map/all_gather | solution.py:78
  328.7 4.8 %fusion.8 = f32[2,64,768]{2,1,0:T(8,128)} fusion(bf16[768,1536]{1,0:T(8,128)(2,1)} %all-gather.14.cloned.1.call-done, bf16[2,768,1536]{2,1,0:T(8,128)(2,1)} %all-gather.12.cloned.1.call-done, f32[2,64,1536]{2,1,0:T(8,128)} %fusion.7, bf16[2,64,768]{2,0,1:T(2,128)(2,1)} %multiply_convert_fusion), kind=kOutput, calls=%fused_computation.13 | convolution fusion | flops 605159424 | bytes 6094848 | tf_op jit(solution)/shard_map/prf,nf->prn/dot_general | solution.py:75
  333.4 1.8 fusion.39
  335.3 0.7 copy.69
  (4 shorter events, 0.0 us)
Async XLA Ops:
  6.5 105.5 %copy-start = (bf16[768,2304]{1,0:T(8,128)(2,1)S(1)}, bf16[768,2304]{1,0:T(8,128)(2,1)}, u32[]{:S(2)}) copy-start(bf16[768,2304]{1,0:T(8,128)(2,1)} %param.15) | copy-start | bytes 10616836
  6.5 105.2 %copy-start.7 = (f32[768]{0:T(1024)S(1)}, f32[768]{0:T(1024)}, u32[]{:S(2)}) copy-start(f32[768]{0:T(1024)} %param.14) | copy-start | bytes 9220
  6.5 95.5 %all-gather.6.cloned.1.call-start = ((), (), s32[]{:S(2)}) async-start(), calls=%async_computation | async-start | bytes 6488064 | tf_op jit(solution)/shard_map/all_gather | solution.py:92
  7.3 132.1 %all-gather.8.cloned.1.call-start = ((), (), s32[]{:S(2)}) async-start(), calls=%async_computation.1 | async-start | bytes 1769472 | tf_op jit(solution)/shard_map/all_gather | solution.py:57
  111.7 2.0 copy-start.2
  113.7 5.6 %copy-start.9 = (s32[512]{0:T(512)S(1)}, s32[512]{0:T(512)}, u32[]{:S(2)}) copy-start(s32[512]{0:T(512)} %param.13) | copy-start | bytes 6148
  114.5 53.8 %all-gather.10.cloned.1.call-start = ((), (), s32[]{:S(2)}) async-start(), calls=%async_computation.2 | async-start | bytes 1769472 | tf_op jit(solution)/shard_map/all_gather | solution.py:58
  115.3 136.1 %all-gather.12.cloned.1.call-start = ((), (), s32[]{:S(2)}) async-start(), calls=%async_computation.3 | async-start | bytes 4866048 | tf_op jit(solution)/shard_map/all_gather | solution.py:71
  115.9 212.8 %all-gather.14.cloned.1.call-start = ((), (), s32[]{:S(2)}) async-start(), calls=%async_computation.4 | async-start | bytes 2433024 | tf_op jit(solution)/shard_map/all_gather | solution.py:78
  171.0 3.2 copy-start.1
  174.1 1.4 copy-start.5
  175.5 1.3 copy-start.6
  175.5 1.6 copy-start.3
  175.6 2.4 copy-start.8
  177.2 0.8 copy-start.4
Sparse Core Ops, SparseCore 0:
  9.9 92.0 all-gather.5
  114.7 24.6 all-gather.7
  141.2 27.1 all-gather.9
  170.8 80.5 all-gather.11
  253.8 74.8 all-gather.13
where the time goes:
time: 345 us; the launch traced here: 342 us
  waiting for transfers between devices  286 us (83%)
  matrix products  24 us (7%)
  between operations  13.2 us (4%)
  other arithmetic  9.43 us (3%)
  local copies, waits for them, and re-layouts  9.19 us (3%)
    all_gather x1, waiting for transfers between devices, body(): lax.all_gather(states, 'particle', axis=0, tiled=True)  94.8 us
    all_gather x1, waiting for transfers between devices, run_block(): lax.all_gather(w_out, 'particle', axis=0, tiled=True)  74.2 us
    all_gather x1, waiting for transfers between devices, run_block(): portion = lax.all_gather(w_in, 'particle', axis=1, tiled=True)  72.3 us
    all_gather x1, waiting for transfers between devices, run_block(): lax.all_gather(value_local, 'token', axis=1, tiled=True)  26.4 us
    all_gather x1, waiting for transfers between devices, run_block(): lax.all_gather(key_local, 'token', axis=1, tiled=True)  16.5 us
    dot_general x1, matrix products, select_rows(): jnp.einsum('jp,prd->jrd', onehot, portion, preferred_element_type=jnp.flo...  9.63 us
  transfers between devices with their start and end apart: 5, of which 5 were waited for; matrix products, arithmetic and copies ran while one was open for 6% of the time, Pallas kernels for 0%

commit v1 on v0

v1 whole, which is shorter than its diff:
```python
import functools
import math

import jax
import jax.numpy as jnp
from jax import lax
from jax.experimental import pallas as pl
from jax.experimental.pallas import tpu as pltpu
from jax.sharding import Mesh
from jax.sharding import PartitionSpec as P

NX, NZ, NY, NC = 4, 8, 4, 2
PARTICLE = ("x", "z")
HEADS = 16
EPS = 1e-05
VMEM = pl.BlockSpec(memory_space=pltpu.VMEM)
SMEM = pl.BlockSpec(memory_space=pltpu.SMEM)


def rms_norm(stream, gain_vec):
    return stream * lax.rsqrt(jnp.mean(stream * stream, axis=-1, keepdims=True) + EPS) * gain_vec


def attention_kernel(
    place, n0, n1, n2, n3, x, w_qkv, bias_own, bias_other, mask, w_o, gain_ff,
    stream_ref, normed_ff_ref, rows_all, keys, values, queries, attended,
):
    y, c = place[0], place[1]
    row_count, width = x.shape
    half = row_count // 2
    head_size = width // HEADS
    for k, block in enumerate((n0, n1, n2, n3)):
        at = pl.multiple_of(lax.rem(y + (NY - k), NY) * row_count, row_count)
        rows_all[pl.ds(at, row_count), :] = block[...]
    own = pl.multiple_of(c * half, half)
    other = pl.multiple_of((1 - c) * half, half)
    own_rows = jnp.concatenate([n0[pl.ds(own, half), :], n0[pl.ds(other, half), :]], axis=0)
    scale = 1.0 / math.sqrt(head_size)
    queries[...] = (
        jnp.dot(own_rows, w_qkv[:, :width], preferred_element_type=jnp.float32) * scale
    ).astype(jnp.bfloat16)
    step = 256
    for part, dest in ((1, keys), (2, values)):
        for at in range(0, width, step):
            dest[:, at : at + step] = jnp.dot(
                rows_all[...],
                w_qkv[:, part * width + at : part * width + at + step],
                preferred_element_type=jnp.float32,
            ).astype(jnp.bfloat16)
    unusable = jnp.where(mask[...] > 0, 0.0, -1e30)
    attended[...] = jnp.zeros_like(attended)
    for h in range(HEADS):
        first, last = h * head_size, (h + 1) * head_size
        lo, hi = first // 128 * 128, -(-last // 128) * 128
        lanes = lax.broadcasted_iota(jnp.int32, (1, hi - lo), 1) + lo
        inside = (lanes >= first) & (lanes < last)
        query_head = jnp.where(inside, queries[:, lo:hi], jnp.zeros((), jnp.bfloat16))
        scores = lax.dot_general(
            query_head, keys[:, lo:hi], (((1,), (1,)), ((), ())), preferred_element_type=jnp.float32
        )
        bias = jnp.concatenate([bias_own[h], bias_other[h]], axis=0).astype(jnp.float32)
        scores = scores + bias + unusable
        weights = jnp.exp(scores - jnp.max(scores, axis=1, keepdims=True))
        total = jnp.sum(weights, axis=1, keepdims=True)
        mixture = jnp.dot(
            weights.astype(jnp.bfloat16), values[:, lo:hi], preferred_element_type=jnp.float32
        )
        attended[:, lo:hi] += jnp.where(inside, mixture / total, 0.0)
    x_rows = jnp.concatenate([x[pl.ds(own, half), :], x[pl.ds(other, half), :]], axis=0)
    stream = x_rows.astype(jnp.float32) + jnp.dot(
        attended[...].astype(jnp.bfloat16), w_o[...], preferred_element_type=jnp.float32
    )
    stream_ref[...] = stream
    normed_ff_ref[...] = rms_norm(stream, gain_ff[...]).astype(jnp.bfloat16)


def transition_kernel(place, own, other, stream, weights, keep_ref, send_ref):
    c = place[1]
    half = own.shape[0] // 2
    rows = jnp.concatenate([own[...], other[...]], axis=0)
    gate = jnp.dot(rows, weights[0], preferred_element_type=jnp.float32)
    up = jnp.dot(rows, weights[1], preferred_element_type=jnp.float32)
    hidden = (gate / (1.0 + jnp.exp(-gate)) * up).astype(jnp.bfloat16)
    update = lax.dot_general(
        hidden, weights[2], (((1,), (1,)), ((), ())), preferred_element_type=jnp.float32
    )
    keep_ref[c] = update[:half] + stream[:half]
    send_ref[c] = update[half : 2 * half] + stream[half:]
    send_ref[1 - c] = update[2 * half : 3 * half]
    keep_ref[1 - c] = update[3 * half :]


def swap_cores(value):
    return lax.ppermute(value, "c", [(0, 1), (1, 0)])


def body(states, ancestors, pair_bias, key_mask, gain_attn, w_qkv, w_o, gain_ff, w_in, w_out):
    part_count, block_rows, width = states.shape
    groups = NX * NZ
    each = block_rows // groups
    rows = block_rows * NC
    c = lax.axis_index("c")
    place = jnp.stack([lax.axis_index("y"), c]).astype(jnp.int32)

    hidden_half = w_out.shape[1] // NC
    local = jnp.concatenate([w_in, w_out[None]], axis=0)
    local = lax.dynamic_slice_in_dim(local, c * hidden_half, hidden_half, axis=2)
    ff_weights = lax.all_gather(local, PARTICLE, axis=1, tiled=True)
    bias_other = swap_cores(pair_bias)

    spread = states.reshape(part_count, groups, each, width).transpose(1, 0, 2, 3)
    names = jnp.broadcast_to(
        ancestors.astype(jnp.bfloat16)[None, :, None, None], (groups, part_count, each, 128)
    )
    spread = jnp.concatenate([spread, names], axis=3).reshape(groups, part_count * each, width + 128)
    spread = lax.all_to_all(spread, PARTICLE, 0, 0)
    wanted = spread[:, ::each, width].astype(jnp.int32).T.reshape(-1)
    source = lax.iota(jnp.int32, groups * part_count)
    onehot = (wanted[:, None] == source[None, :]).astype(jnp.bfloat16)
    picked = jnp.einsum(
        "ds,sre->dre",
        onehot,
        spread[:, :, :width].reshape(groups * part_count, each, width),
        preferred_element_type=jnp.float32,
    ).astype(jnp.bfloat16)
    chosen = lax.all_to_all(picked, ("c",) + PARTICLE, 0, 0).reshape(rows, width)

    normed = rms_norm(chosen.astype(jnp.float32), gain_attn).astype(jnp.bfloat16)
    blocks = [normed] + [
        lax.ppermute(normed, "y", [(i, (i + k) % NY) for i in range(NY)]) for k in range(1, NY)
    ]
    stream, normed_ff = pl.pallas_call(
        attention_kernel,
        out_shape=(
            jax.ShapeDtypeStruct((rows, width), jnp.float32),
            jax.ShapeDtypeStruct((rows, width), jnp.bfloat16),
        ),
        in_specs=[SMEM] + [VMEM] * 11,
        out_specs=(VMEM, VMEM),
        scratch_shapes=[
            pltpu.VMEM((rows * NY, width), jnp.bfloat16),
            pltpu.VMEM((rows * NY, width), jnp.bfloat16),
            pltpu.VMEM((rows * NY, width), jnp.bfloat16),
            pltpu.VMEM((rows, width), jnp.bfloat16),
            pltpu.VMEM((rows, width), jnp.float32),
        ],
        compiler_params=pltpu.CompilerParams(vmem_limit_bytes=32 * 2**20),
        name="attention",
    )(
        place, *blocks, chosen, w_qkv, pair_bias, bias_other, key_mask[None], w_o, gain_ff[None]
    )
    keep, send = pl.pallas_call(
        transition_kernel,
        out_shape=(jax.ShapeDtypeStruct((part_count, block_rows, width), jnp.float32),) * 2,
        in_specs=[SMEM] + [VMEM] * 4,
        out_specs=(VMEM, VMEM),
        compiler_params=pltpu.CompilerParams(vmem_limit_bytes=32 * 2**20),
        name="transition",
    )(place, normed_ff, swap_cores(normed_ff), stream, ff_weights)
    return (keep + swap_cores(send)).astype(jnp.bfloat16)


def solution(mesh):
    fine = Mesh(mesh.devices.reshape(NX, NZ, NY, NC), ("x", "z", "y", "c"))
    token = ("y", "c")
    placed = (
        P(PARTICLE, token, None),
        P(PARTICLE),
        P(None, token, None),
        P(),
        P(),
        P(),
        P(),
        P(),
        P(None, PARTICLE, None),
        P(PARTICLE, None),
    )
    return jax.shard_map(
        body, mesh=fine, in_specs=placed, out_specs=P(PARTICLE, token, None), check_vma=False
    )
```

time: 345 us -> 112 us (0.32)
  waiting for transfers between devices: 286 us -> 20.4 us
  matrix products: 24 us -> 1.17 us
  blocking collectives: 0 us -> 21.2 us
  starting transfers between devices: 0.34 us -> 17.4 us
  local copies, waits for them, and re-layouts: 9.19 us -> 22.1 us
  Pallas kernels: 0 us -> 8.94 us
    all_gather x5 -> x1, waiting for transfers between devices: 284 us -> 0.01 us  [body(): ff_weights = lax.all_gather(local, PARTICLE, axis=1, tiled=True)]
    dot_general x7 -> x1, matrix products: 24 us -> 1.17 us  [body(): jnp.einsum('ds,sre->dre', onehot, spread[:, :, :width].reshape(groups * p...]
    all_to_all x0 -> x1, blocking collectives: none -> 21.2 us  [body(): spread = lax.all_to_all(spread, PARTICLE, 0, 0)]
    unnamed x20 -> x32, local copies, waits for them, and re-layouts: 0.66 us -> 13 us
    all_to_all x0 -> x1, waiting for transfers between devices: none -> 11.5 us  [body(): lax.all_to_all(picked, ('c',) + PARTICLE, 0, 0).reshape(rows, width)]
    ppermute x0 -> x6, starting transfers between devices: none -> 9.08 us  [the longest x3 5.25 us: body(): lax.ppermute(normed, 'y', [(i, (i + k) % NY) for i in range(NY)])]
    pallas_call x0 -> x2, Pallas kernels: none -> 8.94 us  [the longest x1 7.16 us: body(): pl.pallas_call(attention_kernel, out_shape=(jax.ShapeDtypeStruct((rows, w...]
    ppermute x0 -> x6, waiting for transfers between devices: none -> 8.83 us  [the longest x3 7.08 us: body(): lax.ppermute(normed, 'y', [(i, (i + k) % NY) for i in range(NY)])]
  transfers between devices with their start and end apart: 5 -> 8, of which waited for: 5 -> 5; matrix products, arithmetic and copies ran while one was open for 6% -> 15% of each run, Pallas kernels for 0% -> 6%
where the time goes in v1:
time: 112 us; the launch traced here: 111 us
  local copies, waits for them, and re-layouts  22.1 us (20%)
  blocking collectives  21.2 us (19%)
  waiting for transfers between devices  20.4 us (18%)
  starting transfers between devices  17.4 us (16%)
  between operations  13.5 us (12%)
  Pallas kernels  8.94 us (8%)
  other arithmetic  6.72 us (6%)
  matrix products  1.17 us (1%)
    all_to_all x1, blocking collectives, body(): spread = lax.all_to_all(spread, PARTICLE, 0, 0)  21.2 us
    unnamed x32, local copies, waits for them, and re-layouts  13 us
    all_to_all x1, waiting for transfers between devices, body(): lax.all_to_all(picked, ('c',) + PARTICLE, 0, 0).reshape(rows, width)  11.5 us
    all_to_all x1, starting transfers between devices, body(): lax.all_to_all(picked, ('c',) + PARTICLE, 0, 0).reshape(rows, width)  8.28 us
    pallas_call x1, Pallas kernels, body(): pl.pallas_call(attention_kernel, out_shape=(jax.ShapeDtypeStruct((rows, w...  7.16 us
    ppermute x3, waiting for transfers between devices, body(): lax.ppermute(normed, 'y', [(i, (i + k) % NY) for i in range(NY)])  7.08 us
    ppermute x3, starting transfers between devices, body(): lax.ppermute(normed, 'y', [(i, (i + k) % NY) for i in range(NY)])  5.25 us
    ppermute x3, starting transfers between devices, swap_cores(): return lax.ppermute(value, 'c', [(0, 1), (1, 0)])  3.83 us
  transfers between devices with their start and end apart: 8, of which 5 were waited for; matrix products, arithmetic and copies ran while one was open for 15% of the time, Pallas kernels for 6%

profile of v1, /device:TPU:1, one launch (start us, length us, event | category | flops | bytes accessed | tf_op | source)
XLA Modules:
  0.0 111.4 jit_solution(3225171912745520643)
XLA Ops:
  6.5 0.0 copy-start.13
  6.5 0.0 copy-start.14
  6.5 0.0 copy-start.11
  6.5 0.0 copy-start.1
  6.5 0.0 all-gather.2.cloned.1.call-start
  6.6 1.7 %fusion.1 = bf16[3,24,768]{2,1,0:T(8,128)(2,1)} fusion(s32[]{:T(128)S(6)} %select_n.3, bf16[2,24,1536]{2,1,0:T(8,128)(2,1)} %param.18, bf16[1,24,1536]{2,1,0:T(8,128)(2,1)} %bitcast.19), kind=kLoop, calls=%fused_computation.8 | loop fusion | flops 221184 | bytes 331780 | tf_op jit(solution)/shard_map/concatenate | solution.py:106
  8.3 0.0 all-gather.2.cloned.1.call-update
  8.3 1.1 %copy.49 = bf16[2,64,768]{2,0,1:T(2,128)(2,1)S(1)} copy(bf16[2,64,768]{2,1,0:T(8,128)(2,1)} %param.10) | data formatting | bytes 393216 | tf_op args[0]
  9.5 0.7 convert_element_type.23
  10.1 0.1 broadcast_in_dim.8
  10.2 0.2 pad_maximum_fusion
  10.5 0.1 copy.51
  10.6 21.2 %all_to_all.10 = bf16[32,4,896]{2,1,0:T(4,128)(2,1)S(1)} all-to-all(bf16[32,4,896]{2,1,0:T(4,128)(2,1)S(1)} %copy.51), channel_id=1, replica_groups=mesh['x'=4,'z'=8,'y'=4,'c'=2] {'x','z'}, dimensions={0} | all-to-all | bytes 458752 | tf_op jit(solution)/shard_map/all_to_all | solution.py:116
  31.8 0.0 copy-start.12
  31.8 0.7 copy-done.12
  32.5 0.7 slice.8
  33.2 1.7 %reshape.36 = bf16[64,2,768]{2,1,0:T(2,128)(2,1)} reshape(bf16[32,4,768]{2,1,0:T(4,128)(2,1)} %slice.8) | data formatting | bytes 393216 | tf_op jit(solution)/shard_map/reshape | solution.py:123
  34.9 1.4 %slice.6 = bf16[32,2,1]{2,1,0:T(2,128)(2,1)} slice(bf16[32,4,896]{2,1,0:T(4,128)(2,1)} %copy-done.12), slice={[0:32:1], [0:4:2], [768:769:1]} | slice | bytes 256 | tf_op jit(solution)/shard_map/slice | solution.py:117
  36.3 0.8 copy.57
  37.1 0.6 convert_bitcast_fusion
  37.7 0.8 reshape.38
  38.4 1.2 %convolution_convert_fusion = bf16[64,2,768]{2,0,1:T(8,128)(2,1)S(1)} fusion(bf16[64,2,768]{2,1,0:T(2,128)(2,1)} %reshape.36, s32[64]{0:T(128)S(1)} %reshape.38), kind=kOutput, calls=%fused_computation | convolution fusion | flops 12685312 | bytes 393472 | tf_op jit(solution)/shard_map/ds,sre->dre/dot_general | solution.py:120
  39.6 0.9 copy.54
  40.5 8.3 %all-to-all-start.1 = ((bf16[64,2,768]{2,1,0:T(2,128)(2,1)}), bf16[64,2,768]{2,1,0:T(2,128)(2,1)}, u32[]{:S(2)}, u32[]{:S(2)}) async-start(bf16[64,2,768]{2,1,0:T(2,128)(2,1)} %copy.54), calls=%async_computation.1 | async-start | bytes 393216 | tf_op jit(solution)/shard_map/all_to_all | solution.py:126
  48.8 0.5 collective-permute-start.3
  49.3 11.5 %all-to-all-done.1 = bf16[64,2,768]{2,1,0:T(2,128)(2,1)} async-done(((bf16[64,2,768]{2,1,0:T(2,128)(2,1)}), bf16[64,2,768]{2,1,0:T(2,128)(2,1)}, u32[]{:S(2)}, u32[]{:S(2)}) %all-to-all-start.1) | async-done | bytes 196640 | tf_op jit(solution)/shard_map/all_to_all | solution.py:126
  60.8 1.0 multiply_reduce_fusion
  61.9 0.7 copy.56
  62.6 0.9 rsqrt.12
  63.5 1.8 %reshape.37.x = bf16[128,768]{1,0:T(8,128)(2,1)} reshape(bf16[64,2,768]{2,1,0:T(2,128)(2,1)} %all-to-all-done.1) | data formatting | bytes 393216 | tf_op jit(solution)/shard_map/reshape | solution.py:126
  65.3 0.0 copy-done.13
  65.3 1.7 %multiply_convert_fusion.n0 = bf16[128,768]{1,0:T(8,128)(2,1)} fusion(bf16[128,768]{1,0:T(8,128)(2,1)} %reshape.37.x, f32[768]{0:T(1024)S(1)} %copy-done.13, f32[128]{0:T(128)S(1)} %rsqrt.12), kind=kLoop, calls=%fused_computation.2 | loop fusion | flops 393216 | bytes 396800 | tf_op jit(solution)/shard_map/convert_element_type | solution.py:128
  67.0 1.5 %collective-permute-start = (bf16[128,768]{1,0:T(8,128)(2,1)}, bf16[128,768]{1,0:T(8,128)(2,1)}, u32[]{:S(2)}, u32[]{:S(2)}) collective-permute-start(bf16[128,768]{1,0:T(8,128)(2,1)} %multiply_convert_fusion.n0), channel_id=1, source_target_pairs={{0,2},{2,4},{4,6},{6,0},{1,3},{3,5},{5,7},{7,1},{8,10},{10,12},{12... | collective-permute-start | bytes 589832 | tf_op jit(solution)/shard_map/ppermute | solution.py:130
  68.5 2.6 %collective-permute-start.1 = (bf16[128,768]{1,0:T(8,128)(2,1)}, bf16[128,768]{1,0:T(8,128)(2,1)}, u32[]{:S(2)}, u32[]{:S(2)}) collective-permute-start(bf16[128,768]{1,0:T(8,128)(2,1)} %multiply_convert_fusion.n0), channel_id=1, source_target_pairs={{0,4},{2,6},{4,0},{6,2},{1,5},{3,7},{5,1},{7,3},{8,12},{10,14},{12... | collective-permute-start | bytes 589832 | tf_op jit(solution)/shard_map/ppermute | solution.py:130
  71.1 1.1 collective-permute-start.2
  72.2 0.0 copy-done.14
  72.3 0.1 pad_add_fusion.place
  72.3 2.0 %collective-permute-done.n1 = bf16[128,768]{1,0:T(8,128)(2,1)} collective-permute-done((bf16[128,768]{1,0:T(8,128)(2,1)}, bf16[128,768]{1,0:T(8,128)(2,1)}, u32[]{:S(2)}, u32[]{:S(2)}) %collective-permute-start) | collective-permute-done | bytes 196640 | tf_op jit(solution)/shard_map/ppermute | solution.py:130
  74.3 5.1 %collective-permute-done.1.n2 = bf16[128,768]{1,0:T(8,128)(2,1)} collective-permute-done((bf16[128,768]{1,0:T(8,128)(2,1)}, bf16[128,768]{1,0:T(8,128)(2,1)}, u32[]{:S(2)}, u32[]{:S(2)}) %collective-permute-start.1) | collective-permute-done | bytes 196640 | tf_op jit(solution)/shard_map/ppermute | solution.py:130
  79.4 0.0 collective-permute-done.2.n3
  79.4 0.0 collective-permute-done.3.bias_other
  79.4 0.0 copy-done.11
  79.4 0.0 copy-done.1
  79.4 0.0 copy-start.2
  79.4 0.9 copy-done.2
  80.4 0.0 copy-start.3
  80.4 1.3 %copy-done.3 = bf16[768,768]{1,0:T(8,128)(2,1)S(1)} copy-done((bf16[768,768]{1,0:T(8,128)(2,1)S(1)}, bf16[768,768]{1,0:T(8,128)(2,1)}, u32[]{:S(2)}) %copy-start.3) | copy-done | bytes 1179672
  81.7 0.0 copy-start.4
  81.7 1.2 %copy-done.4 = bf16[16,64,512]{2,1,0:T(8,128)(2,1)S(1)} copy-done((bf16[16,64,512]{2,1,0:T(8,128)(2,1)S(1)}, bf16[16,64,512]{2,1,0:T(8,128)(2,1)}, u32[]{:S(2)}) %copy-start.4) | copy-done | bytes 1048600
  82.9 7.2 %attention.1 = (f32[128,768]{1,0:T(8,128)S(1)}, bf16[128,768]{1,0:T(8,128)(2,1)S(1)}) custom-call(s32[2]{0:T(128)S(1)} %pad_add_fusion.place, bf16[128,768]{1,0:T(8,128)(2,1)} %multiply_convert_fusion.n0, bf16[128,768]{1,0:T(8,128)(2,1)} %collective-permute-done.n1, bf16[128,768]{1,0:T(8,128)(2,1)} %collective-permute-done.1.n2, ...), custom_call_target="tpu_custom_call" | custom-call | tf_op jit(solution)/shard_map/attention/pallas_call | solution.py:132
  90.1 0.0 copy-start.5
  90.1 0.7 copy-done.5
  90.8 2.1 %collective-permute-start.4 = (bf16[128,768]{1,0:T(8,128)(2,1)S(1)}, bf16[128,768]{1,0:T(8,128)(2,1)S(1)}, u32[]{:S(2)}, u32[]{:S(2)}) collective-permute-start(bf16[128,768]{1,0:T(8,128)(2,1)S(1)} %get-tuple-element.9.own), channel_id=1, source_target_pairs={{0,1},{1,0},{2,3},{3,2},{4,5},{5,4},{6,7},{7,6},{8,9},{9,8},{10,11... | collective-permute-start | bytes 589832 | tf_op jit(solution)/shard_map/ppermute | solution.py:94
  92.9 0.7 copy-done.7
  93.6 0.4 collective-permute-done.4.other
  94.0 0.7 copy-done.9
  94.7 2.0 %copy-done = bf16[3,768,768]{2,1,0:T(8,128)(2,1)S(1)} copy-done((bf16[3,768,768]{2,1,0:T(8,128)(2,1)S(1)}, bf16[3,768,768]{2,1,0:T(8,128)(2,1)}, u32[]{:S(2)}) %copy-start) | copy-done | bytes 3538968
  96.7 1.0 copy-done.6
  97.7 0.9 copy-done.8
  98.6 0.9 copy-done.10
  99.5 1.8 %transition.1 = (f32[2,64,768]{2,1,0:T(8,128)S(1)}, f32[2,64,768]{2,1,0:T(8,128)S(1)}) custom-call(s32[2]{0:T(128)S(1)} %pad_add_fusion.place, bf16[128,768]{1,0:T(8,128)(2,1)S(1)} %copy-done.8, bf16[128,768]{1,0:T(8,128)(2,1)S(1)} %copy-done.10, f32[128,768]{1,0:T(8,128)S(1)} %copy-done.6, bf16[3,768,768]{2,1,0:T(8,128)(2,1)S(1)} %copy-done), custom_call_target="tpu_custom_call" | custom-call | tf_op jit(solution)/shard_map/transition/pallas_call | solution.py:152
  101.3 1.2 %collective-permute-start.5 = (f32[2,64,768]{2,1,0:T(8,128)S(1)}, f32[2,64,768]{2,1,0:T(8,128)S(1)}, u32[]{:S(2)}, u32[]{:S(2)}) collective-permute-start(f32[2,64,768]{2,1,0:T(8,128)S(1)} %get-tuple-element.12), channel_id=1, source_target_pairs={{0,1},{1,0},{2,3},{3,2},{4,5},{5,4},{6,7},{7,6},{8,9},{9,8},{10,11... | collective-permute-start | bytes 1179656 | tf_op jit(solution)/shard_map/ppermute | solution.py:94
  102.5 1.3 %collective-permute-done.5 = f32[2,64,768]{2,1,0:T(8,128)S(1)} collective-permute-done((f32[2,64,768]{2,1,0:T(8,128)S(1)}, f32[2,64,768]{2,1,0:T(8,128)S(1)}, u32[]{:S(2)}, u32[]{:S(2)}) %collective-permute-start.5) | collective-permute-done | bytes 393248 | tf_op jit(solution)/shard_map/ppermute | solution.py:94
  103.9 0.7 add_convert_fusion
  (10 shorter events, 0.0 us)
Async XLA Ops:
  6.5 58.7 %copy-start.13 = (f32[768]{0:T(1024)S(1)}, f32[768]{0:T(1024)}, u32[]{:S(2)}) copy-start(f32[768]{0:T(1024)} %param.14) | copy-start | bytes 9220
  6.5 65.7 %copy-start.14 = (f32[768]{0:T(1024)S(1)}, f32[768]{0:T(1024)}, u32[]{:S(2)}) copy-start(f32[768]{0:T(1024)} %param.17) | copy-start | bytes 9220
  6.5 72.9 %copy-start.11 = (s32[512]{0:T(512)S(1)}, s32[512]{0:T(512)}, u32[]{:S(2)}) copy-start(s32[512]{0:T(512)} %param.13) | copy-start | bytes 6148
  6.5 72.9 %copy-start.1 = (bf16[768,2304]{1,0:T(8,128)(2,1)S(1)}, bf16[768,2304]{1,0:T(8,128)(2,1)}, u32[]{:S(2)}) copy-start(bf16[768,2304]{1,0:T(8,128)(2,1)} %w_qkv.1) | copy-start | bytes 10616836
  6.5 88.1 %all-gather.2.cloned.1.call-start = ((), (), s32[]{:S(2)}) async-start(), calls=%async_computation.2 | async-start | bytes 3649536 | tf_op jit(solution)/shard_map/all_gather | solution.py:108
  31.8 0.7 copy-start.12
  40.5 20.3 %all-to-all-start.1 = ((bf16[64,2,768]{2,1,0:T(2,128)(2,1)}), bf16[64,2,768]{2,1,0:T(2,128)(2,1)}, u32[]{:S(2)}, u32[]{:S(2)}) async-start(bf16[64,2,768]{2,1,0:T(2,128)(2,1)} %copy.54), calls=%async_computation.1 | async-start | bytes 393216 | tf_op jit(solution)/shard_map/all_to_all | solution.py:126
  48.8 30.6 %collective-permute-start.3 = (bf16[16,64,512]{2,1,0:T(8,128)(2,1)}, bf16[16,64,512]{2,1,0:T(8,128)(2,1)}, u32[]{:S(2)}, u32[]{:S(2)}) collective-permute-start(bf16[16,64,512]{2,1,0:T(8,128)(2,1)} %bias_own.1), channel_id=1, source_target_pairs={{0,1},{1,0},{2,3},{3,2},{4,5},{5,4},{6,7},{7,6},{8,9},{9,8},{10,11... | collective-permute-start | bytes 3145736 | tf_op jit(solution)/shard_map/ppermute | solution.py:94
  67.0 7.3 %collective-permute-start = (bf16[128,768]{1,0:T(8,128)(2,1)}, bf16[128,768]{1,0:T(8,128)(2,1)}, u32[]{:S(2)}, u32[]{:S(2)}) collective-permute-start(bf16[128,768]{1,0:T(8,128)(2,1)} %multiply_convert_fusion.n0), channel_id=1, source_target_pairs={{0,2},{2,4},{4,6},{6,0},{1,3},{3,5},{5,7},{7,1},{8,10},{10,12},{12... | collective-permute-start | bytes 589832 | tf_op jit(solution)/shard_map/ppermute | solution.py:130
  68.5 10.9 %collective-permute-start.1 = (bf16[128,768]{1,0:T(8,128)(2,1)}, bf16[128,768]{1,0:T(8,128)(2,1)}, u32[]{:S(2)}, u32[]{:S(2)}) collective-permute-start(bf16[128,768]{1,0:T(8,128)(2,1)} %multiply_convert_fusion.n0), channel_id=1, source_target_pairs={{0,4},{2,6},{4,0},{6,2},{1,5},{3,7},{5,1},{7,3},{8,12},{10,14},{12... | collective-permute-start | bytes 589832 | tf_op jit(solution)/shard_map/ppermute | solution.py:130
  71.1 8.3 %collective-permute-start.2 = (bf16[128,768]{1,0:T(8,128)(2,1)}, bf16[128,768]{1,0:T(8,128)(2,1)}, u32[]{:S(2)}, u32[]{:S(2)}) collective-permute-start(bf16[128,768]{1,0:T(8,128)(2,1)} %multiply_convert_fusion.n0), channel_id=1, source_target_pairs={{0,6},{2,0},{4,2},{6,4},{1,7},{3,1},{5,3},{7,5},{8,14},{10,8},{12,... | collective-permute-start | bytes 589832 | tf_op jit(solution)/shard_map/ppermute | solution.py:130
  79.4 0.9 copy-start.2
  80.4 1.3 %copy-start.3 = (bf16[768,768]{1,0:T(8,128)(2,1)S(1)}, bf16[768,768]{1,0:T(8,128)(2,1)}, u32[]{:S(2)}) copy-start(bf16[768,768]{1,0:T(8,128)(2,1)} %w_o.1) | copy-start | bytes 3538948
  81.7 1.2 %copy-start.4 = (bf16[16,64,512]{2,1,0:T(8,128)(2,1)S(1)}, bf16[16,64,512]{2,1,0:T(8,128)(2,1)}, u32[]{:S(2)}) copy-start(bf16[16,64,512]{2,1,0:T(8,128)(2,1)} %bias_own.1) | copy-start | bytes 3145732
  90.1 0.8 copy-start.5
  90.8 3.2 %collective-permute-start.4 = (bf16[128,768]{1,0:T(8,128)(2,1)S(1)}, bf16[128,768]{1,0:T(8,128)(2,1)S(1)}, u32[]{:S(2)}, u32[]{:S(2)}) collective-permute-start(bf16[128,768]{1,0:T(8,128)(2,1)S(1)} %get-tuple-element.9.own), channel_id=1, source_target_pairs={{0,1},{1,0},{2,3},{3,2},{4,5},{5,4},{6,7},{7,6},{8,9},{9,8},{10,11... | collective-permute-start | bytes 589832 | tf_op jit(solution)/shard_map/ppermute | solution.py:94
  92.9 0.7 copy-start.7
  94.0 0.7 copy-start.9
  94.7 2.0 %copy-start = (bf16[3,768,768]{2,1,0:T(8,128)(2,1)S(1)}, bf16[3,768,768]{2,1,0:T(8,128)(2,1)}, u32[]{:S(2)}) copy-start(bf16[3,768,768]{2,1,0:T(8,128)(2,1)} %all-gather.2.cloned.1.call-done.weights) | copy-start | bytes 10616836
  96.7 1.0 copy-start.6
  97.7 0.9 copy-start.8
  98.6 0.9 copy-start.10
  101.3 2.5 %collective-permute-start.5 = (f32[2,64,768]{2,1,0:T(8,128)S(1)}, f32[2,64,768]{2,1,0:T(8,128)S(1)}, u32[]{:S(2)}, u32[]{:S(2)}) collective-permute-start(f32[2,64,768]{2,1,0:T(8,128)S(1)} %get-tuple-element.12), channel_id=1, source_target_pairs={{0,1},{1,0},{2,3},{3,2},{4,5},{5,4},{6,7},{7,6},{8,9},{9,8},{10,11... | collective-permute-start | bytes 1179656 | tf_op jit(solution)/shard_map/ppermute | solution.py:94
Sparse Core Ops, SparseCore 0:
  10.1 81.7 all-gather.1

commit v2 on v1

v2 whole, which is shorter than its diff:
```python
import math

import jax
import jax.numpy as jnp
import numpy as np
from jax import lax
from jax.experimental import pallas as pl
from jax.experimental.pallas import tpu as pltpu
from jax.sharding import Mesh
from jax.sharding import PartitionSpec as P

NX, NZ, NY, NC = 4, 8, 4, 2
GROUP = NX * NZ
PARTICLE = ("x", "z")
HEADS = 16
EPS = 1e-05
PIECE = 4
TILE = 8
TILES = 8
MIB = 2**20
ANY = pl.BlockSpec(memory_space=pl.ANY)
VMEM = pl.BlockSpec(memory_space=pltpu.VMEM)
SMEM = pl.BlockSpec(memory_space=pltpu.SMEM)


def rms_norm(stream, gain_vec):
    return stream * lax.rsqrt(jnp.mean(stream * stream, axis=-1, keepdims=True) + EPS) * gain_vec


def iotas(shape):
    return lax.broadcasted_iota(jnp.int32, shape, 0), lax.broadcasted_iota(jnp.int32, shape, 1)


def reorder(onehot, values):
    return jnp.dot(onehot.astype(jnp.bfloat16), values, preferred_element_type=jnp.float32)


def weight_orders(width):
    depth = width // GROUP
    tile, source, row = np.meshgrid(np.arange(3), np.arange(GROUP), np.arange(TILE), indexing="ij")
    inputs = (source * depth + tile * TILE + row).reshape(-1)
    outputs = np.concatenate([inputs[: 2 * GROUP * TILE], inputs[2 * GROUP * TILE :].reshape(GROUP, TILE).T.reshape(-1)])
    eye = np.eye(width, dtype=jnp.bfloat16)
    return eye[:, inputs], eye[outputs]


def spread_kernel(place, ancestors, states, w_in, w_out, out_ref, local):
    y, c = place[0], place[1]
    part_count, rows, width = states.shape
    half = width // 2
    both = 2 * PIECE
    out_row, in_row = iotas((part_count * rows, part_count * rows))
    group, part, row = out_row // both, out_row // PIECE % 2, out_row % PIECE
    onehot = in_row == part * rows + group * PIECE + row
    moved = reorder(onehot, states[...].reshape(part_count * rows, width))
    for h in range(2):
        out_ref[:, h, :, :half] = (
            moved[:, h * half : (h + 1) * half].reshape(-1, both, half).astype(jnp.bfloat16)
        )
    depth = w_out.shape[0]
    mine = pl.ds(pl.multiple_of(c * width, 128), width)
    local[: 2 * depth] = w_in[:, :, mine].astype(jnp.float32).reshape(2 * depth, width)
    local[2 * depth :] = w_out[:, mine].astype(jnp.float32)
    lanes = pl.ds(pl.multiple_of(lax.rem(y, 2) * half, 128), half)
    tile_row = lax.broadcasted_iota(jnp.int32, (both, 128), 0)
    names = jnp.where(tile_row == 3, ancestors[0], ancestors[1]).astype(jnp.float32)
    groups = GROUP // NX // 2
    for x in range(NX):
        e = 2 * x + y // 2
        tile = local[pl.ds(pl.multiple_of(e * TILE, TILE), TILE), lanes]
        extra = local[pl.ds(TILES * TILE + e, 1), lanes]
        last = names
        for i in range(3):
            last = jnp.where(tile_row == i, extra[:, i * 128 : (i + 1) * 128], last)
        at = slice(x * groups, (x + 1) * groups)
        shape = (groups, 2, both)
        out_ref[at, :, :, half:width] = jnp.broadcast_to(tile.astype(jnp.bfloat16), shape + (half,))
        out_ref[at, :, :, width:] = jnp.broadcast_to(last.astype(jnp.bfloat16), shape + (128,))


def pick_kernel(place, pieces, picked_ref, weights_ref):
    c = place[1]
    half = picked_ref.shape[2]
    width = 2 * half
    rows = pieces[...].astype(jnp.float32).reshape(-1, width + 128)
    count = rows.shape[0]
    last = rows[:, width:].astype(jnp.bfloat16)
    out_row, in_row = iotas((count, count))
    part = lax.rem(out_row // PIECE + c, 2)
    names = reorder(in_row == out_row // TILE * TILE + 3 + part, last)[:, :1]
    onehot = in_row == names.astype(jnp.int32) * PIECE + out_row % PIECE
    picked = reorder(onehot, rows[:, :half].astype(jnp.bfloat16))
    picked_ref[...] = picked.reshape(picked_ref.shape).astype(jnp.bfloat16)
    weights_ref[:count] = rows[:, half:width].astype(jnp.bfloat16)
    out_row, in_row = iotas((GROUP, count))
    for i in range(3):
        extra = reorder(in_row == out_row * TILE + i, last).astype(jnp.bfloat16)
        weights_ref[count:, i * 128 : (i + 1) * 128] = extra


def column_kernel(place, w0, w1, w2, w3, out_ref):
    half = w0.shape[1]
    for k, block in enumerate((w0, w1, w2, w3)):
        y = lax.rem(place[0] + (NY - k), NY)
        lanes = pl.ds(pl.multiple_of(lax.rem(y, 2) * half, 128), half)
        out_ref[y // 2, :, lanes] = block[...]


def rows_kernel(pieces, keep_ref, send_ref):
    rows, width = keep_ref.shape
    half = width // 2
    both = 2 * PIECE
    out_row, in_row = iotas((2 * rows, 2 * rows))
    part, at = out_row // rows, out_row % rows
    onehot = in_row == at // PIECE * both + part * PIECE + at % PIECE
    for h in range(2):
        values = pieces[:, h].astype(jnp.float32).reshape(2 * rows, half).astype(jnp.bfloat16)
        moved = reorder(onehot, values).astype(jnp.bfloat16)
        keep_ref[:, h * half : (h + 1) * half] = moved[:rows]
        send_ref[:, h * half : (h + 1) * half] = moved[rows:]


def norm_kernel(place, own, other, gain, normed_ref):
    c = place[1]
    rows = own.shape[0]
    for values, slot in ((own, c), (other, 1 - c)):
        at = pl.ds(pl.multiple_of(slot * rows, rows), rows)
        normed = rms_norm(values[...].astype(jnp.float32), gain[...][None, :])
        normed_ref[at, :] = normed.astype(jnp.bfloat16)


def project_kernel(place, normed, w_qkv, queries_ref, keys_ref, values_ref):
    c = place[1]
    row_count, width = normed.shape
    half = row_count // 2
    scale = 1.0 / math.sqrt(width // HEADS)
    projected = jnp.dot(normed[...], w_qkv[...], preferred_element_type=jnp.float32)
    queries = (projected[:, :width] * scale).astype(jnp.bfloat16)
    for slot, at in ((c, 0), (1 - c, half)):
        queries_ref[pl.ds(pl.multiple_of(slot * half, half), half), :] = queries[at : at + half]
    keys_ref[...] = projected[:, width : 2 * width].astype(jnp.bfloat16)
    values_ref[...] = projected[:, 2 * width :].astype(jnp.bfloat16)


def attention_kernel(
    place, n1, n2, n3, queries, key_own, value_own, x_own, x_other, w_qkv, bias_own, bias_other,
    mask, w_o, gain_ff, order, stream_ref, normed_ff_ref,
    rows_all, keys, values, attended, bias, w_o_here, order_here, arrived, loaded,
):
    y = place[0]
    row_count, width = queries.shape
    half = row_count // 2
    head_size = width // HEADS
    blocks = [
        pltpu.make_async_copy(block, rows_all.at[pl.ds(k * row_count, row_count)], arrived.at[k])
        for k, block in enumerate((n1, n2, n3))
    ]
    loads = [
        pltpu.make_async_copy(bias_own, bias.at[:, :half], loaded.at[0]),
        pltpu.make_async_copy(bias_other, bias.at[:, half:], loaded.at[1]),
        pltpu.make_async_copy(w_o, w_o_here, loaded.at[2]),
        pltpu.make_async_copy(order, order_here, loaded.at[3]),
    ]
    for copy in blocks + loads:
        copy.start()
    spots = [
        pl.ds(pl.multiple_of(lax.rem(y + (NY - k), NY) * row_count, row_count), row_count)
        for k in range(NY)
    ]
    keys[spots[0], :] = key_own[...]
    values[spots[0], :] = value_own[...]
    for copy in blocks:
        copy.wait()
    step = 256
    for part, dest in ((1, keys), (2, values)):
        for at in range(0, width, step):
            made = jnp.dot(
                rows_all[...],
                w_qkv[:, part * width + at : part * width + at + step],
                preferred_element_type=jnp.float32,
            ).astype(jnp.bfloat16)
            for k in range(1, NY):
                dest[spots[k], at : at + step] = made[(k - 1) * row_count : k * row_count]
    unusable = jnp.where(mask[...][None, :] > 0, 0.0, -1e30)
    attended[...] = jnp.zeros_like(attended)
    for copy in loads[:2]:
        copy.wait()
    for h in range(HEADS):
        first, last = h * head_size, (h + 1) * head_size
        lo, hi = first // 128 * 128, -(-last // 128) * 128
        lanes = lax.broadcasted_iota(jnp.int32, (1, hi - lo), 1) + lo
        inside = (lanes >= first) & (lanes < last)
        query_head = jnp.where(inside, queries[:, lo:hi], jnp.zeros((), jnp.bfloat16))
        scores = lax.dot_general(
            query_head, keys[:, lo:hi], (((1,), (1,)), ((), ())), preferred_element_type=jnp.float32
        )
        scores = scores + bias[h].astype(jnp.float32) + unusable
        weights = jnp.exp(scores - jnp.max(scores, axis=1, keepdims=True))
        total = jnp.sum(weights, axis=1, keepdims=True)
        mixture = jnp.dot(
            weights.astype(jnp.bfloat16), values[:, lo:hi], preferred_element_type=jnp.float32
        )
        attended[:, lo:hi] += jnp.where(inside, mixture / total, 0.0)
    x_rows = jnp.concatenate([x_own[...], x_other[...]], axis=0)
    for copy in loads[2:]:
        copy.wait()
    stream = x_rows.astype(jnp.float32) + jnp.dot(
        attended[...].astype(jnp.bfloat16), w_o_here[...], preferred_element_type=jnp.float32
    )
    stream_ref[...] = stream
    normed_ff = rms_norm(stream, gain_ff[...][None, :]).astype(jnp.bfloat16)
    normed_ff_ref[...] = jnp.dot(
        normed_ff, order_here[...], preferred_element_type=jnp.float32
    ).astype(jnp.bfloat16)


def transition_kernel(
    place, own, other, stream, order, w0, w1, w2, w3, keep_ref, send_ref, tiles, extras, arrived
):
    c, x = place[1], place[2]
    half = own.shape[0] // 2
    width = own.shape[1]
    count = tiles.shape[1]
    copies = []
    for k, block in enumerate((w0, w1, w2, w3)):
        at = pl.ds(lax.rem(x + (NX - k), NX) * 2, 2)
        copies.append(pltpu.make_async_copy(block.at[:, :count], tiles.at[at], arrived.at[2 * k]))
        copies.append(pltpu.make_async_copy(block.at[:, count:], extras.at[at], arrived.at[2 * k + 1]))
    for copy in copies:
        copy.start()
    rows = jnp.concatenate([own[...], other[...]], axis=0)
    for copy in copies:
        copy.wait()
    gate = jnp.dot(rows, tiles[0:3].reshape(width, width), preferred_element_type=jnp.float32)
    up = jnp.dot(rows, tiles[3:6].reshape(width, width), preferred_element_type=jnp.float32)
    hidden = (gate / (1.0 + jnp.exp(-gate)) * up).astype(jnp.bfloat16)
    across = (((1,), (1,)), ((), ()))
    update = jnp.concatenate(
        [
            lax.dot_general(
                hidden, tiles[6:8].reshape(2 * count, width), across, preferred_element_type=jnp.float32
            ),
            lax.dot_general(
                hidden, extras[...].reshape(-1, width), across, preferred_element_type=jnp.float32
            ),
        ],
        axis=1,
    )
    high = update.astype(jnp.bfloat16)
    low = (update - high.astype(jnp.float32)).astype(jnp.bfloat16)
    update = jnp.dot(high, order[...], preferred_element_type=jnp.float32) + jnp.dot(
        low, order[...], preferred_element_type=jnp.float32
    )
    keep_ref[c] = update[:half] + stream[:half]
    send_ref[c] = update[half : 2 * half] + stream[half:]
    send_ref[1 - c] = update[2 * half : 3 * half]
    keep_ref[1 - c] = update[3 * half :]


def swap_cores(value):
    return lax.ppermute(value, "c", [(0, 1), (1, 0)])


def others(value, axis, size):
    return [
        lax.ppermute(value, axis, [(i, (i + k) % size) for i in range(size)]) for k in range(1, size)
    ]


def kernel(f, name, specs, args, shapes, limit=8, scratch=()):
    def whole(shape):
        return pl.BlockSpec(shape, lambda i: (0,) * len(shape))

    specs = [whole(a.shape) if s is None else s for s, a in zip(specs, args, strict=True)]
    outs = tuple(jax.ShapeDtypeStruct(shape, dtype) for shape, dtype in shapes)
    return pl.pallas_call(
        f,
        grid=(1,),
        out_shape=outs,
        in_specs=specs,
        out_specs=tuple(whole(o.shape) for o in outs),
        scratch_shapes=scratch,
        compiler_params=pltpu.CompilerParams(vmem_limit_bytes=limit * MIB),
        name=name,
    )(*args)


def body(states, ancestors, pair_bias, key_mask, gain_attn, w_qkv, w_o, gain_ff, w_in, w_out):
    part_count, block_rows, width = states.shape
    rows = block_rows * NC
    half = width // 2
    both = 2 * PIECE
    depth = w_out.shape[0]
    bf16, f32 = jnp.bfloat16, jnp.float32
    place = jnp.stack([lax.axis_index(a) for a in ("y", "c", "x")]).astype(jnp.int32)
    order_in, order_out = weight_orders(width)

    bias_other = swap_cores(pair_bias)
    (pieces,) = kernel(
        spread_kernel,
        "spread",
        [SMEM, SMEM, None, None, None],
        (place, ancestors, states, w_in, w_out),
        [((GROUP // 2, 2, both, width + 128), bf16)],
        scratch=[pltpu.VMEM((3 * depth, width), f32)],
    )
    pieces = lax.all_to_all(pieces.reshape(GROUP, both, width + 128), PARTICLE, 0, 0)
    picked, piece = kernel(
        pick_kernel,
        "pick",
        [SMEM, None],
        (place, pieces),
        [((GROUP, both, half), bf16), ((GROUP * (TILE + 1), half), bf16)],
    )
    ring = [piece] + others(piece, "y", NY)
    (column,) = kernel(
        column_kernel,
        "column",
        [SMEM] + [None] * NY,
        (place, *ring),
        [((2, GROUP * (TILE + 1), width), bf16)],
    )
    columns = [column] + others(column, "x", NX)
    picked = lax.all_to_all(picked, PARTICLE, 0, 0)
    x_own, x_send = kernel(
        rows_kernel,
        "rows",
        [None],
        (picked.reshape(GROUP // 2, 2, both, half),),
        [((block_rows, width), bf16)] * 2,
    )
    x_other = swap_cores(x_send)
    (normed,) = kernel(
        norm_kernel,
        "norm",
        [SMEM, None, None, None],
        (place, x_own, x_other, gain_attn),
        [((rows, width), bf16)],
    )
    blocks = others(normed, "y", NY)
    queries, key_own, value_own = kernel(
        project_kernel,
        "project",
        [SMEM, None, VMEM],
        (place, normed, w_qkv),
        [((rows, width), bf16)] * 3,
    )
    stream, normed_ff = kernel(
        attention_kernel,
        "attention",
        [SMEM] + [ANY] * 3 + [None] * 5 + [VMEM, ANY, ANY, None, ANY, None, ANY],
        (
            place, *blocks, queries, key_own, value_own, x_own, x_other, w_qkv, pair_bias,
            bias_other, key_mask, w_o, gain_ff, order_in,
        ),
        [((rows, width), f32), ((rows, width), bf16)],
        limit=16,
        scratch=[
            pltpu.VMEM((rows * (NY - 1), width), bf16),
            pltpu.VMEM((rows * NY, width), bf16),
            pltpu.VMEM((rows * NY, width), bf16),
            pltpu.VMEM((rows, width), f32),
            pltpu.VMEM((HEADS, rows, rows * NY), bf16),
            pltpu.VMEM((width, width), bf16),
            pltpu.VMEM((width, width), bf16),
            pltpu.SemaphoreType.DMA((NY - 1,)),
            pltpu.SemaphoreType.DMA((4,)),
        ],
    )
    keep, send = kernel(
        transition_kernel,
        "transition",
        [SMEM, None, None, None, None] + [ANY] * NX,
        (place, normed_ff, swap_cores(normed_ff), stream, order_out, *columns),
        [((part_count, block_rows, width), f32)] * 2,
        limit=16,
        scratch=[
            pltpu.VMEM((TILES, GROUP * TILE, width), bf16),
            pltpu.VMEM((TILES, GROUP, width), bf16),
            pltpu.SemaphoreType.DMA((2 * NX,)),
        ],
    )
    return (keep + swap_cores(send)).astype(bf16)


def solution(mesh):
    fine = Mesh(mesh.devices.reshape(NX, NZ, NY, NC), ("x", "z", "y", "c"))
    token = ("y", "c")
    placed = (
        P(PARTICLE, token, None),
        P(PARTICLE),
        P(None, token, None),
        P(),
        P(),
        P(),
        P(),
        P(),
        P(None, PARTICLE, None),
        P(PARTICLE, None),
    )
    return jax.shard_map(
        body, mesh=fine, in_specs=placed, out_specs=P(PARTICLE, token, None), check_vma=False
    )
```

time: 112 us -> 100 us (0.89)
  starting transfers between devices: 17.4 us -> 40.2 us
  blocking collectives: 21.2 us -> 0 us
  local copies, waits for them, and re-layouts: 22.1 us -> 4.86 us
  between operations: 13.5 us -> 0.18 us
  waiting for transfers between devices: 20.4 us -> 33.6 us
  Pallas kernels: 8.94 us -> 20.4 us
  other arithmetic: 6.72 us -> 0.8 us
  matrix products: 1.17 us -> 0 us
    all_to_all x1 -> x0, blocking collectives: 21.2 us -> none  [body(): spread = lax.all_to_all(spread, PARTICLE, 0, 0)]
    all_to_all x1 -> x2, starting transfers between devices: 8.28 us -> 20.3 us  [the longest x1 12.2 us: body(): lax.all_to_all(pieces.reshape(GROUP, both, width + 128), PARTICLE, 0, 0)]
    pallas_call x2 -> x8, Pallas kernels: 8.94 us -> 20.4 us  [kernel(): pl.pallas_call(f, grid=(1,), out_shape=outs, in_specs=specs, out_specs=tu...]
    ppermute x3 -> x9, waiting for transfers between devices: 7.08 us -> 16.1 us  [others(): lax.ppermute(value, axis, [(i, (i + k) % size) for i in range(size)])]
    unnamed x32 -> x28, local copies, waits for them, and re-layouts: 13 us -> 4.86 us
    ppermute x3 -> x4, starting transfers between devices: 3.83 us -> 9.36 us  [swap_cores(): return lax.ppermute(value, 'c', [(0, 1), (1, 0)])]
    ppermute x3 -> x9, starting transfers between devices: 5.25 us -> 10.5 us  [others(): lax.ppermute(value, axis, [(i, (i + k) % size) for i in range(size)])]
    reshape x3 -> x0, local copies, waits for them, and re-layouts: 3.56 us -> none  [the longest x1 1.77 us: body(): lax.all_to_all(picked, ('c',) + PARTICLE, 0, 0).reshape(rows, width)]
  transfers between devices with their start and end apart: 8 -> 15, of which waited for: 5 -> 8; matrix products, arithmetic and copies ran while one was open for 15% -> 0% of each run, Pallas kernels for 6% -> 15%
where the time goes in v2:
time: 100 us
  starting transfers between devices  40.2 us (40%)
  waiting for transfers between devices  33.6 us (34%)
  Pallas kernels  20.4 us (20%)
  local copies, waits for them, and re-layouts  4.86 us (5%)
    pallas_call x8, Pallas kernels, kernel(): pl.pallas_call(f, grid=(1,), out_shape=outs, in_specs=specs, out_specs=tu...  20.4 us
    ppermute x9, waiting for transfers between devices, others(): lax.ppermute(value, axis, [(i, (i + k) % size) for i in range(size)])  16.1 us
    all_to_all x1, starting transfers between devices, body(): lax.all_to_all(pieces.reshape(GROUP, both, width + 128), PARTICLE, 0, 0)  12.2 us
    all_to_all x1, waiting for transfers between devices, body(): lax.all_to_all(pieces.reshape(GROUP, both, width + 128), PARTICLE, 0, 0)  11.9 us
    ppermute x9, starting transfers between devices, others(): lax.ppermute(value, axis, [(i, (i + k) % size) for i in range(size)])  10.5 us
    ppermute x4, starting transfers between devices, swap_cores(): return lax.ppermute(value, 'c', [(0, 1), (1, 0)])  9.36 us
    all_to_all x1, starting transfers between devices, body(): picked = lax.all_to_all(picked, PARTICLE, 0, 0)  8.02 us
    unnamed x28, local copies, waits for them, and re-layouts  4.86 us
  transfers between devices with their start and end apart: 15, of which 8 were waited for; matrix products, arithmetic and copies ran while one was open for 0% of the time, Pallas kernels for 15%

profile of v2, /device:TPU:1, one launch (start us, length us, event | category | flops | bytes accessed | tf_op | source)
XLA Modules:
  0.0 100.1 jit_solution(7828796442810007344)
XLA Ops:
  0.0 0.1 pad_add_fusion.place
  0.1 0.0 copy-start.7
  0.1 0.9 copy-done.7
  1.0 0.0 copy-start.8
  1.0 0.9 copy-done.8
  1.9 0.0 copy-start.9
  1.9 0.9 copy-done.9
  2.8 0.7 copy-done.13
  3.5 0.8 spread.1
  4.2 0.0 copy-start.1
  4.2 0.8 copy-done.1
  5.0 12.2 %all-to-all-start = ((bf16[32,8,896]{2,1,0:T(8,128)(2,1)}), bf16[32,8,896]{2,1,0:T(8,128)(2,1)}, u32[]{:S(2)}, u32[]{:S(2)}) async-start(bf16[32,8,896]{2,1,0:T(8,128)(2,1)} %bitcast.5), calls=%async_computation | async-start | bytes 917504 | tf_op jit(solution)/shard_map/all_to_all | solution.py:307
  17.2 1.0 %collective-permute-start.4 = (bf16[16,64,512]{2,1,0:T(8,128)(2,1)}, bf16[16,64,512]{2,1,0:T(8,128)(2,1)}, u32[]{:S(2)}, u32[]{:S(2)}) collective-permute-start(bf16[16,64,512]{2,1,0:T(8,128)(2,1)} %bias_own.1), channel_id=1, source_target_pairs={{0,1},{1,0},{2,3},{3,2},{4,5},{5,4},{6,7},{7,6},{8,9},{9,8},{10,11... | collective-permute-start | bytes 3145736 | tf_op jit(solution)/shard_map/ppermute | solution.py:261
  18.3 11.9 %all-to-all-done.pieces = bf16[32,8,896]{2,1,0:T(8,128)(2,1)} async-done(((bf16[32,8,896]{2,1,0:T(8,128)(2,1)}), bf16[32,8,896]{2,1,0:T(8,128)(2,1)}, u32[]{:S(2)}, u32[]{:S(2)}) %all-to-all-start) | async-done | bytes 458784 | tf_op jit(solution)/shard_map/all_to_all | solution.py:307
  30.2 2.2 %pick.1 = (bf16[32,8,384]{2,1,0:T(8,128)(2,1)S(1)}, bf16[288,384]{1,0:T(8,128)(2,1)}) custom-call(s32[3]{0:T(128)S(1)} %pad_add_fusion.place, bf16[32,8,896]{2,1,0:T(8,128)(2,1)} %all-to-all-done.pieces), custom_call_target="tpu_custom_call" | custom-call | tf_op jit(solution)/shard_map/pick/pallas_call | solution.py:276
  32.3 0.7 copy-done.6
  33.0 1.3 %collective-permute-start.6 = (bf16[288,384]{1,0:T(8,128)(2,1)}, bf16[288,384]{1,0:T(8,128)(2,1)}, u32[]{:S(2)}, u32[]{:S(2)}) collective-permute-start(bf16[288,384]{1,0:T(8,128)(2,1)} %get-tuple-element.24.w0), channel_id=1, source_target_pairs={{0,2},{2,4},{4,6},{6,0},{1,3},{3,5},{5,7},{7,1},{8,10},{10,12},{12... | collective-permute-start | bytes 663560 | tf_op jit(solution)/shard_map/ppermute | solution.py:266
  34.3 2.6 %collective-permute-start.7 = (bf16[288,384]{1,0:T(8,128)(2,1)}, bf16[288,384]{1,0:T(8,128)(2,1)}, u32[]{:S(2)}, u32[]{:S(2)}) collective-permute-start(bf16[288,384]{1,0:T(8,128)(2,1)} %get-tuple-element.24.w0), channel_id=1, source_target_pairs={{0,4},{2,6},{4,0},{6,2},{1,5},{3,7},{5,1},{7,3},{8,12},{10,14},{12... | collective-permute-start | bytes 663560 | tf_op jit(solution)/shard_map/ppermute | solution.py:266
  36.9 1.1 %collective-permute-start.8 = (bf16[288,384]{1,0:T(8,128)(2,1)}, bf16[288,384]{1,0:T(8,128)(2,1)}, u32[]{:S(2)}, u32[]{:S(2)}) collective-permute-start(bf16[288,384]{1,0:T(8,128)(2,1)} %get-tuple-element.24.w0), channel_id=1, source_target_pairs={{0,6},{2,0},{4,2},{6,4},{1,7},{3,1},{5,3},{7,5},{8,14},{10,8},{12,... | collective-permute-start | bytes 663560 | tf_op jit(solution)/shard_map/ppermute | solution.py:266
  38.0 8.0 %all-to-all-start.1 = ((bf16[32,8,384]{2,1,0:T(8,128)(2,1)}), bf16[32,8,384]{2,1,0:T(8,128)(2,1)}, u32[]{:S(2)}, u32[]{:S(2)}) async-start(bf16[32,8,384]{2,1,0:T(8,128)(2,1)} %copy-done.6), calls=%async_computation.1 | async-start | bytes 393216 | tf_op jit(solution)/shard_map/all_to_all | solution.py:324
  46.0 0.0 collective-permute-done.6.w1
  46.0 0.0 collective-permute-done.7.w2
  46.1 0.0 collective-permute-done.8.w3
  46.1 2.3 %column.1.w0 = bf16[2,288,768]{2,1,0:T(8,128)(2,1)} custom-call(s32[3]{0:T(128)S(1)} %pad_add_fusion.place, bf16[288,384]{1,0:T(8,128)(2,1)} %get-tuple-element.24.w0, bf16[288,384]{1,0:T(8,128)(2,1)} %collective-permute-done.6.w1, bf16[288,384]{1,0:T(8,128)(2,1)} %collective-permute-done.7.w2, bf16[288,384]{1,0:T(8,128)(2,1)} %collective-permute-done.8.w3), custom_call_target="tpu_custom_call" | custom-call | tf_op jit(solution)/shard_map/column/pallas_call | solution.py:276
  48.3 1.2 %collective-permute-start.9 = (bf16[2,288,768]{2,1,0:T(8,128)(2,1)}, bf16[2,288,768]{2,1,0:T(8,128)(2,1)}, u32[]{:S(2)}, u32[]{:S(2)}) collective-permute-start(bf16[2,288,768]{2,1,0:T(8,128)(2,1)} %column.1.w0), channel_id=1, source_target_pairs={{0,64},{64,128},{128,192},{192,0},{1,65},{65,129},{129,193},{193,1... | collective-permute-start | bytes 2654216 | tf_op jit(solution)/shard_map/ppermute | solution.py:266
  49.5 2.4 %collective-permute-start.10 = (bf16[2,288,768]{2,1,0:T(8,128)(2,1)}, bf16[2,288,768]{2,1,0:T(8,128)(2,1)}, u32[]{:S(2)}, u32[]{:S(2)}) collective-permute-start(bf16[2,288,768]{2,1,0:T(8,128)(2,1)} %column.1.w0), channel_id=1, source_target_pairs={{0,128},{64,192},{128,0},{192,64},{1,129},{65,193},{129,1},{193,65... | collective-permute-start | bytes 2654216 | tf_op jit(solution)/shard_map/ppermute | solution.py:266
  52.0 1.1 %collective-permute-start.11 = (bf16[2,288,768]{2,1,0:T(8,128)(2,1)}, bf16[2,288,768]{2,1,0:T(8,128)(2,1)}, u32[]{:S(2)}, u32[]{:S(2)}) collective-permute-start(bf16[2,288,768]{2,1,0:T(8,128)(2,1)} %column.1.w0), channel_id=1, source_target_pairs={{0,192},{64,0},{128,64},{192,128},{1,193},{65,1},{129,65},{193,129... | collective-permute-start | bytes 2654216 | tf_op jit(solution)/shard_map/ppermute | solution.py:266
  53.1 2.3 %all-to-all-done.1 = bf16[32,8,384]{2,1,0:T(8,128)(2,1)} async-done(((bf16[32,8,384]{2,1,0:T(8,128)(2,1)}), bf16[32,8,384]{2,1,0:T(8,128)(2,1)}, u32[]{:S(2)}, u32[]{:S(2)}) %all-to-all-start.1) | async-done | bytes 196640 | tf_op jit(solution)/shard_map/all_to_all | solution.py:324
  55.4 1.1 %rows.1 = (bf16[64,768]{1,0:T(8,128)(2,1)S(1)}, bf16[64,768]{1,0:T(8,128)(2,1)S(1)}) custom-call(bf16[16,2,8,384]{3,2,1,0:T(8,128)(2,1)} %bitcast.4.pieces), custom_call_target="tpu_custom_call" | custom-call | tf_op jit(solution)/shard_map/rows/pallas_call | solution.py:276
  56.6 3.8 %collective-permute-start = (bf16[64,768]{1,0:T(8,128)(2,1)S(1)}, bf16[64,768]{1,0:T(8,128)(2,1)S(1)}, u32[]{:S(2)}, u32[]{:S(2)}) collective-permute-start(bf16[64,768]{1,0:T(8,128)(2,1)S(1)} %get-tuple-element.18), channel_id=1, source_target_pairs={{0,1},{1,0},{2,3},{3,2},{4,5},{5,4},{6,7},{7,6},{8,9},{9,8},{10,11... | collective-permute-start | bytes 294920 | tf_op jit(solution)/shard_map/ppermute | solution.py:261
  60.4 0.9 collective-permute-done.other.x_other
  61.3 0.0 copy-done.11
  61.3 0.7 norm.1.normed
  62.0 0.0 copy-start.2
  62.0 0.0 copy-start.3
  62.0 0.0 copy-start.5
  62.1 0.0 copy-start.10
  62.1 0.0 copy-start.12
  62.1 0.5 collective-permute-start.1
  62.6 0.0 collective-permute-done.4.bias_other
  62.6 0.3 collective-permute-start.2
  62.9 10.9 %collective-permute-done.1.n1 = bf16[128,768]{1,0:T(8,128)(2,1)S(1)} collective-permute-done((bf16[128,768]{1,0:T(8,128)(2,1)S(1)}, bf16[128,768]{1,0:T(8,128)(2,1)S(1)}, u32[]{:S(2)}, u32[]{:S(2)}) %collective-permute-start.1) | collective-permute-done | bytes 196640 | tf_op jit(solution)/shard_map/ppermute | solution.py:266
  73.8 0.0 collective-permute-start.3
  73.8 0.0 copy-done
  73.8 1.2 %project.1 = (bf16[128,768]{1,0:T(8,128)(2,1)S(1)}, bf16[128,768]{1,0:T(8,128)(2,1)S(1)}, bf16[128,768]{1,0:T(8,128)(2,1)S(1)}) custom-call(s32[3]{0:T(128)S(1)} %pad_add_fusion.place, bf16[128,768]{1,0:T(8,128)(2,1)S(1)} %norm.1.normed, bf16[768,2304]{1,0:T(8,128)(2,1)S(1)} %copy-done), custom_call_target="tpu_custom_call" | custom-call | tf_op jit(solution)/shard_map/project/pallas_call | solution.py:276
  75.0 0.0 collective-permute-done.2.n2
  75.0 4.2 %collective-permute-done.3.n3 = bf16[128,768]{1,0:T(8,128)(2,1)S(1)} collective-permute-done((bf16[128,768]{1,0:T(8,128)(2,1)S(1)}, bf16[128,768]{1,0:T(8,128)(2,1)S(1)}, u32[]{:S(2)}, u32[]{:S(2)}) %collective-permute-start.3) | collective-permute-done | bytes 196640 | tf_op jit(solution)/shard_map/ppermute | solution.py:266
  79.2 0.0 copy-done.2
  79.2 0.0 copy-done.3
  79.2 0.0 copy-done.5
  79.3 0.0 copy-done.10
  79.3 0.0 copy-done.12
  79.3 0.0 copy-start.4
  79.3 7.6 %attention.1 = (f32[128,768]{1,0:T(8,128)S(1)}, bf16[128,768]{1,0:T(8,128)(2,1)S(1)}) custom-call(s32[3]{0:T(128)S(1)} %pad_add_fusion.place, bf16[128,768]{1,0:T(8,128)(2,1)S(1)} %collective-permute-done.1.n1, bf16[128,768]{1,0:T(8,128)(2,1)S(1)} %collective-permute-done.2.n2, bf16[128,768]{1,0:T(8,128)(2,1)S(1)} %collective-permute-done.3.n3, ...), custom_call_target="tpu_custom_call" | custom-call | tf_op jit(solution)/shard_map/attention/pallas_call | solution.py:276
  86.9 2.0 %collective-permute-start.5 = (bf16[128,768]{1,0:T(8,128)(2,1)S(1)}, bf16[128,768]{1,0:T(8,128)(2,1)S(1)}, u32[]{:S(2)}, u32[]{:S(2)}) collective-permute-start(bf16[128,768]{1,0:T(8,128)(2,1)S(1)} %get-tuple-element.22.own), channel_id=1, source_target_pairs={{0,1},{1,0},{2,3},{3,2},{4,5},{5,4},{6,7},{7,6},{8,9},{9,8},{10,11... | collective-permute-start | bytes 589832 | tf_op jit(solution)/shard_map/ppermute | solution.py:261
  88.9 1.1 %collective-permute-done.5.other = bf16[128,768]{1,0:T(8,128)(2,1)S(1)} collective-permute-done((bf16[128,768]{1,0:T(8,128)(2,1)S(1)}, bf16[128,768]{1,0:T(8,128)(2,1)S(1)}, u32[]{:S(2)}, u32[]{:S(2)}) %collective-permute-start.5) | collective-permute-done | bytes 196640 | tf_op jit(solution)/shard_map/ppermute | solution.py:261
  90.0 0.0 collective-permute-done.9.w1
  90.0 0.9 collective-permute-done.10.w2
  90.8 0.0 collective-permute-done.11.w3
  90.9 0.0 copy-done.4
  90.9 4.6 %transition.1 = (f32[2,64,768]{2,1,0:T(8,128)S(1)}, f32[2,64,768]{2,1,0:T(8,128)S(1)}) custom-call(s32[3]{0:T(128)S(1)} %pad_add_fusion.place, bf16[128,768]{1,0:T(8,128)(2,1)S(1)} %get-tuple-element.22.own, bf16[128,768]{1,0:T(8,128)(2,1)S(1)} %collective-permute-done.5.other, f32[128,768]{1,0:T(8,128)S(1)} %get-tuple-element.23.stream, ...), custom_call_target="tpu_custom_call" | custom-call | tf_op jit(solution)/shard_map/transition/pallas_call | solution.py:276
  95.5 2.5 %collective-permute-start.12 = (f32[2,64,768]{2,1,0:T(8,128)S(1)}, f32[2,64,768]{2,1,0:T(8,128)S(1)}, u32[]{:S(2)}, u32[]{:S(2)}) collective-permute-start(f32[2,64,768]{2,1,0:T(8,128)S(1)} %get-tuple-element.26), channel_id=1, source_target_pairs={{0,1},{1,0},{2,3},{3,2},{4,5},{5,4},{6,7},{7,6},{8,9},{9,8},{10,11... | collective-permute-start | bytes 1179656 | tf_op jit(solution)/shard_map/ppermute | solution.py:261
  98.0 1.3 %collective-permute-done.12 = f32[2,64,768]{2,1,0:T(8,128)S(1)} collective-permute-done((f32[2,64,768]{2,1,0:T(8,128)S(1)}, f32[2,64,768]{2,1,0:T(8,128)S(1)}, u32[]{:S(2)}, u32[]{:S(2)}) %collective-permute-start.12) | collective-permute-done | bytes 393248 | tf_op jit(solution)/shard_map/ppermute | solution.py:261
  99.3 0.7 add_convert_fusion
  (4 shorter events, 0.0 us)
Async XLA Ops:
  0.1 0.9 copy-start.7
  1.0 0.9 copy-start.8
  1.9 0.9 copy-start.9
  2.8 0.7 copy-start.13
  4.2 0.8 copy-start.1
  5.0 68.8 %copy-start = (bf16[768,2304]{1,0:T(8,128)(2,1)S(1)}, bf16[768,2304]{1,0:T(8,128)(2,1)}, u32[]{:S(2)}) copy-start(bf16[768,2304]{1,0:T(8,128)(2,1)} %w_qkv.3) | copy-start | bytes 10616836
  5.0 25.2 %all-to-all-start = ((bf16[32,8,896]{2,1,0:T(8,128)(2,1)}), bf16[32,8,896]{2,1,0:T(8,128)(2,1)}, u32[]{:S(2)}, u32[]{:S(2)}) async-start(bf16[32,8,896]{2,1,0:T(8,128)(2,1)} %bitcast.5), calls=%async_computation | async-start | bytes 917504 | tf_op jit(solution)/shard_map/all_to_all | solution.py:307
  17.2 45.3 %collective-permute-start.4 = (bf16[16,64,512]{2,1,0:T(8,128)(2,1)}, bf16[16,64,512]{2,1,0:T(8,128)(2,1)}, u32[]{:S(2)}, u32[]{:S(2)}) collective-permute-start(bf16[16,64,512]{2,1,0:T(8,128)(2,1)} %bias_own.1), channel_id=1, source_target_pairs={{0,1},{1,0},{2,3},{3,2},{4,5},{5,4},{6,7},{7,6},{8,9},{9,8},{10,11... | collective-permute-start | bytes 3145736 | tf_op jit(solution)/shard_map/ppermute | solution.py:261
  32.3 0.7 copy-start.6
  33.0 13.0 %collective-permute-start.6 = (bf16[288,384]{1,0:T(8,128)(2,1)}, bf16[288,384]{1,0:T(8,128)(2,1)}, u32[]{:S(2)}, u32[]{:S(2)}) collective-permute-start(bf16[288,384]{1,0:T(8,128)(2,1)} %get-tuple-element.24.w0), channel_id=1, source_target_pairs={{0,2},{2,4},{4,6},{6,0},{1,3},{3,5},{5,7},{7,1},{8,10},{10,12},{12... | collective-permute-start | bytes 663560 | tf_op jit(solution)/shard_map/ppermute | solution.py:266
  34.3 11.7 %collective-permute-start.7 = (bf16[288,384]{1,0:T(8,128)(2,1)}, bf16[288,384]{1,0:T(8,128)(2,1)}, u32[]{:S(2)}, u32[]{:S(2)}) collective-permute-start(bf16[288,384]{1,0:T(8,128)(2,1)} %get-tuple-element.24.w0), channel_id=1, source_target_pairs={{0,4},{2,6},{4,0},{6,2},{1,5},{3,7},{5,1},{7,3},{8,12},{10,14},{12... | collective-permute-start | bytes 663560 | tf_op jit(solution)/shard_map/ppermute | solution.py:266
  36.9 9.1 %collective-permute-start.8 = (bf16[288,384]{1,0:T(8,128)(2,1)}, bf16[288,384]{1,0:T(8,128)(2,1)}, u32[]{:S(2)}, u32[]{:S(2)}) collective-permute-start(bf16[288,384]{1,0:T(8,128)(2,1)} %get-tuple-element.24.w0), channel_id=1, source_target_pairs={{0,6},{2,0},{4,2},{6,4},{1,7},{3,1},{5,3},{7,5},{8,14},{10,8},{12,... | collective-permute-start | bytes 663560 | tf_op jit(solution)/shard_map/ppermute | solution.py:266
  38.0 23.3 %copy-start.11 = (f32[768]{0:T(1024)S(1)}, f32[768]{0:T(1024)}, u32[]{:S(2)}) copy-start(f32[768]{0:T(1024)} %gain.1) | copy-start | bytes 9220
  38.0 17.4 %all-to-all-start.1 = ((bf16[32,8,384]{2,1,0:T(8,128)(2,1)}), bf16[32,8,384]{2,1,0:T(8,128)(2,1)}, u32[]{:S(2)}, u32[]{:S(2)}) async-start(bf16[32,8,384]{2,1,0:T(8,128)(2,1)} %copy-done.6), calls=%async_computation.1 | async-start | bytes 393216 | tf_op jit(solution)/shard_map/all_to_all | solution.py:324
  48.3 41.6 %collective-permute-start.9 = (bf16[2,288,768]{2,1,0:T(8,128)(2,1)}, bf16[2,288,768]{2,1,0:T(8,128)(2,1)}, u32[]{:S(2)}, u32[]{:S(2)}) collective-permute-start(bf16[2,288,768]{2,1,0:T(8,128)(2,1)} %column.1.w0), channel_id=1, source_target_pairs={{0,64},{64,128},{128,192},{192,0},{1,65},{65,129},{129,193},{193,1... | collective-permute-start | bytes 2654216 | tf_op jit(solution)/shard_map/ppermute | solution.py:266
  49.5 41.3 %collective-permute-start.10 = (bf16[2,288,768]{2,1,0:T(8,128)(2,1)}, bf16[2,288,768]{2,1,0:T(8,128)(2,1)}, u32[]{:S(2)}, u32[]{:S(2)}) collective-permute-start(bf16[2,288,768]{2,1,0:T(8,128)(2,1)} %column.1.w0), channel_id=1, source_target_pairs={{0,128},{64,192},{128,0},{192,64},{1,129},{65,193},{129,1},{193,65... | collective-permute-start | bytes 2654216 | tf_op jit(solution)/shard_map/ppermute | solution.py:266
  52.0 38.9 %collective-permute-start.11 = (bf16[2,288,768]{2,1,0:T(8,128)(2,1)}, bf16[2,288,768]{2,1,0:T(8,128)(2,1)}, u32[]{:S(2)}, u32[]{:S(2)}) collective-permute-start(bf16[2,288,768]{2,1,0:T(8,128)(2,1)} %column.1.w0), channel_id=1, source_target_pairs={{0,192},{64,0},{128,64},{192,128},{1,193},{65,1},{129,65},{193,129... | collective-permute-start | bytes 2654216 | tf_op jit(solution)/shard_map/ppermute | solution.py:266
  56.6 4.8 %collective-permute-start = (bf16[64,768]{1,0:T(8,128)(2,1)S(1)}, bf16[64,768]{1,0:T(8,128)(2,1)S(1)}, u32[]{:S(2)}, u32[]{:S(2)}) collective-permute-start(bf16[64,768]{1,0:T(8,128)(2,1)S(1)} %get-tuple-element.18), channel_id=1, source_target_pairs={{0,1},{1,0},{2,3},{3,2},{4,5},{5,4},{6,7},{7,6},{8,9},{9,8},{10,11... | collective-permute-start | bytes 294920 | tf_op jit(solution)/shard_map/ppermute | solution.py:261
  62.0 17.2 %copy-start.2 = (bf16[768,768]{1,0:T(8,128)(2,1)S(1)}, bf16[768,768]{1,0:T(8,128)(2,1)}, u32[]{:S(2)}) copy-start(bf16[768,768]{1,0:T(8,128)(2,1)} %w_o.1) | copy-start | bytes 3538948
  62.0 17.2 %copy-start.3 = (bf16[768,768]{1,0:T(8,128)(2,1)S(1)}, bf16[768,768]{1,0:T(8,128)(2,1)}, u32[]{:S(2)}) copy-start(bf16[768,768]{1,0:T(8,128)(2,1)} %constant.16.clone.order) | copy-start | bytes 3538948
  62.0 17.2 %copy-start.5 = (bf16[16,64,512]{2,1,0:T(8,128)(2,1)S(1)}, bf16[16,64,512]{2,1,0:T(8,128)(2,1)}, u32[]{:S(2)}) copy-start(bf16[16,64,512]{2,1,0:T(8,128)(2,1)} %bias_own.1) | copy-start | bytes 3145732
  62.1 17.2 %copy-start.10 = (f32[768]{0:T(1024)S(1)}, f32[768]{0:T(1024)}, u32[]{:S(2)}) copy-start(f32[768]{0:T(1024)} %gain_ff.1) | copy-start | bytes 9220
  62.1 17.2 %copy-start.12 = (s32[512]{0:T(512)S(1)}, s32[512]{0:T(512)}, u32[]{:S(2)}) copy-start(s32[512]{0:T(512)} %mask.1) | copy-start | bytes 6148
  62.1 11.7 %collective-permute-start.1 = (bf16[128,768]{1,0:T(8,128)(2,1)S(1)}, bf16[128,768]{1,0:T(8,128)(2,1)S(1)}, u32[]{:S(2)}, u32[]{:S(2)}) collective-permute-start(bf16[128,768]{1,0:T(8,128)(2,1)S(1)} %norm.1.normed), channel_id=1, source_target_pairs={{0,2},{2,4},{4,6},{6,0},{1,3},{3,5},{5,7},{7,1},{8,10},{10,12},{12... | collective-permute-start | bytes 589832 | tf_op jit(solution)/shard_map/ppermute | solution.py:266
  62.6 12.4 %collective-permute-start.2 = (bf16[128,768]{1,0:T(8,128)(2,1)S(1)}, bf16[128,768]{1,0:T(8,128)(2,1)S(1)}, u32[]{:S(2)}, u32[]{:S(2)}) collective-permute-start(bf16[128,768]{1,0:T(8,128)(2,1)S(1)} %norm.1.normed), channel_id=1, source_target_pairs={{0,4},{2,6},{4,0},{6,2},{1,5},{3,7},{5,1},{7,3},{8,12},{10,14},{12... | collective-permute-start | bytes 589832 | tf_op jit(solution)/shard_map/ppermute | solution.py:266
  73.8 5.4 %collective-permute-start.3 = (bf16[128,768]{1,0:T(8,128)(2,1)S(1)}, bf16[128,768]{1,0:T(8,128)(2,1)S(1)}, u32[]{:S(2)}, u32[]{:S(2)}) collective-permute-start(bf16[128,768]{1,0:T(8,128)(2,1)S(1)} %norm.1.normed), channel_id=1, source_target_pairs={{0,6},{2,0},{4,2},{6,4},{1,7},{3,1},{5,3},{7,5},{8,14},{10,8},{12,... | collective-permute-start | bytes 589832 | tf_op jit(solution)/shard_map/ppermute | solution.py:266
  79.3 11.6 %copy-start.4 = (bf16[768,768]{1,0:T(8,128)(2,1)S(1)}, bf16[768,768]{1,0:T(8,128)(2,1)}, u32[]{:S(2)}) copy-start(bf16[768,768]{1,0:T(8,128)(2,1)} %constant.17.clone.order) | copy-start | bytes 3538948
  86.9 3.0 %collective-permute-start.5 = (bf16[128,768]{1,0:T(8,128)(2,1)S(1)}, bf16[128,768]{1,0:T(8,128)(2,1)S(1)}, u32[]{:S(2)}, u32[]{:S(2)}) collective-permute-start(bf16[128,768]{1,0:T(8,128)(2,1)S(1)} %get-tuple-element.22.own), channel_id=1, source_target_pairs={{0,1},{1,0},{2,3},{3,2},{4,5},{5,4},{6,7},{7,6},{8,9},{9,8},{10,11... | collective-permute-start | bytes 589832 | tf_op jit(solution)/shard_map/ppermute | solution.py:261
  95.5 3.9 %collective-permute-start.12 = (f32[2,64,768]{2,1,0:T(8,128)S(1)}, f32[2,64,768]{2,1,0:T(8,128)S(1)}, u32[]{:S(2)}, u32[]{:S(2)}) collective-permute-start(f32[2,64,768]{2,1,0:T(8,128)S(1)} %get-tuple-element.26), channel_id=1, source_target_pairs={{0,1},{1,0},{2,3},{3,2},{4,5},{5,4},{6,7},{7,6},{8,9},{9,8},{10,11... | collective-permute-start | bytes 1179656 | tf_op jit(solution)/shard_map/ppermute | solution.py:261

commit v3 on v2

v3 whole, which is shorter than its diff:
```python
import math

import jax
import jax.numpy as jnp
import numpy as np
from jax import lax
from jax.experimental import pallas as pl
from jax.experimental.pallas import tpu as pltpu
from jax.sharding import Mesh
from jax.sharding import PartitionSpec as P

NX, NZ, NY, NC = 4, 8, 4, 2
GROUP = NX * NZ
PARTICLE = ("x", "z")
HEADS = 16
EPS = 1e-05
PIECE = 4
TILE = 8
TILES = 8
MIB = 2**20
MICROSECOND = 10**9
ANY = pl.BlockSpec(memory_space=pl.ANY)
VMEM = pl.BlockSpec(memory_space=pltpu.VMEM)
SMEM = pl.BlockSpec(memory_space=pltpu.SMEM)


def rms_norm(stream, gain_vec):
    return stream * lax.rsqrt(jnp.mean(stream * stream, axis=-1, keepdims=True) + EPS) * gain_vec


def iotas(shape):
    return lax.broadcasted_iota(jnp.int32, shape, 0), lax.broadcasted_iota(jnp.int32, shape, 1)


def reorder(onehot, values):
    return jnp.dot(onehot.astype(jnp.bfloat16), values, preferred_element_type=jnp.float32)


def weight_orders(width):
    depth = width // GROUP
    tile, source, row = np.meshgrid(np.arange(3), np.arange(GROUP), np.arange(TILE), indexing="ij")
    inputs = (source * depth + tile * TILE + row).reshape(-1)
    outputs = np.concatenate([inputs[: 2 * GROUP * TILE], inputs[2 * GROUP * TILE :].reshape(GROUP, TILE).T.reshape(-1)])
    eye = np.eye(width, dtype=jnp.bfloat16)
    return eye[:, inputs], eye[outputs]


def spread_kernel(ancestors, states, w_in, w_out, out_ref, local):
    y, c = lax.axis_index("y"), lax.axis_index("c")
    part_count, rows, width = states.shape
    half = width // 2
    both = 2 * PIECE
    out_row, in_row = iotas((part_count * rows, part_count * rows))
    group, part, row = out_row // both, out_row // PIECE % 2, out_row % PIECE
    onehot = in_row == part * rows + group * PIECE + row
    moved = reorder(onehot, states[...].reshape(part_count * rows, width))
    for h in range(2):
        out_ref[:, h, :, :half] = (
            moved[:, h * half : (h + 1) * half].reshape(-1, both, half).astype(jnp.bfloat16)
        )
    depth = w_out.shape[0]
    mine = pl.ds(pl.multiple_of(c * width, 128), width)
    local[: 2 * depth] = w_in[:, :, mine].astype(jnp.float32).reshape(2 * depth, width)
    local[2 * depth :] = w_out[:, mine].astype(jnp.float32)
    lanes = pl.ds(pl.multiple_of(lax.rem(y, 2) * half, 128), half)
    tile_row = lax.broadcasted_iota(jnp.int32, (both, 128), 0)
    names = jnp.where(tile_row == 3, ancestors[0], ancestors[1]).astype(jnp.float32)
    groups = GROUP // NX // 2
    for x in range(NX):
        e = 2 * x + y // 2
        tile = local[pl.ds(pl.multiple_of(e * TILE, TILE), TILE), lanes]
        extra = local[pl.ds(TILES * TILE + e, 1), lanes]
        last = names
        for i in range(3):
            last = jnp.where(tile_row == i, extra[:, i * 128 : (i + 1) * 128], last)
        at = slice(x * groups, (x + 1) * groups)
        shape = (groups, 2, both)
        out_ref[at, :, :, half:width] = jnp.broadcast_to(tile.astype(jnp.bfloat16), shape + (half,))
        out_ref[at, :, :, width:] = jnp.broadcast_to(last.astype(jnp.bfloat16), shape + (128,))


def pick_kernel(pieces, picked_ref, weights_ref):
    c = lax.axis_index("c")
    half = picked_ref.shape[2]
    width = 2 * half
    rows = pieces[...].astype(jnp.float32).reshape(-1, width + 128)
    count = rows.shape[0]
    last = rows[:, width:].astype(jnp.bfloat16)
    out_row, in_row = iotas((count, count))
    part = lax.rem(out_row // PIECE + c, 2)
    names = reorder(in_row == out_row // TILE * TILE + 3 + part, last)[:, :1]
    onehot = in_row == names.astype(jnp.int32) * PIECE + out_row % PIECE
    picked = reorder(onehot, rows[:, :half].astype(jnp.bfloat16))
    picked_ref[...] = picked.reshape(picked_ref.shape).astype(jnp.bfloat16)
    weights_ref[:count] = rows[:, half:width].astype(jnp.bfloat16)
    out_row, in_row = iotas((GROUP, count))
    for i in range(3):
        extra = reorder(in_row == out_row * TILE + i, last).astype(jnp.bfloat16)
        weights_ref[count:, i * 128 : (i + 1) * 128] = extra


def column_kernel(w0, w1, w2, w3, out_ref):
    half = w0.shape[1]
    for k, block in enumerate((w0, w1, w2, w3)):
        y = lax.rem(lax.axis_index("y") + (NY - k), NY)
        lanes = pl.ds(pl.multiple_of(lax.rem(y, 2) * half, 128), half)
        out_ref[y // 2, :, lanes] = block[...]


def assemble(pieces, part, width):
    both = 2 * PIECE
    half = width // 2
    count = pieces.shape[0] // 2 * both
    out_row, in_row = iotas((count // 2, count))
    onehot = in_row == out_row // PIECE * both + part * PIECE + out_row % PIECE
    sides = []
    for h in range(2):
        values = pieces[:, :, :].reshape(-1, 2, both, half)[:, h]
        values = values.astype(jnp.float32).reshape(count, half).astype(jnp.bfloat16)
        sides.append(reorder(onehot, values))
    return jnp.concatenate(sides, axis=1)


def chip_rows(mine, theirs, width):
    return jnp.concatenate([assemble(mine, 0, width), assemble(theirs, 1, width)], axis=0)


def store_rows(ref, values):
    c = lax.axis_index("c")
    half = values.shape[0] // 2
    for slot, at in ((c, 0), (1 - c, half)):
        ref[pl.ds(pl.multiple_of(slot * half, half), half), :] = values[at : at + half].astype(ref.dtype)


def own_kernel(
    mine, theirs, gain, w_qkv, _bias, x_ref, normed_ref, queries_ref, keys_ref, values_ref
):
    width = x_ref.shape[1]
    rows = chip_rows(mine, theirs, width)
    x_ref[...] = rows.astype(jnp.bfloat16)
    normed = rms_norm(rows, gain[...][None, :])
    store_rows(normed_ref, normed)
    normed = normed.astype(jnp.bfloat16)
    projected = jnp.dot(normed, w_qkv[...], preferred_element_type=jnp.float32)
    scale = 1.0 / math.sqrt(width // HEADS)
    queries_ref[...] = (projected[:, :width] * scale).astype(jnp.bfloat16)
    store_rows(keys_ref, projected[:, width : 2 * width])
    store_rows(values_ref, projected[:, 2 * width :])


def other_kernel(normed, w_qkv, keys_ref, values_ref):
    width = keys_ref.shape[1]
    projected = jnp.dot(normed[...], w_qkv[:, width:], preferred_element_type=jnp.float32)
    keys_ref[...] = projected[:, :width].astype(jnp.bfloat16)
    values_ref[...] = projected[:, width:].astype(jnp.bfloat16)


def halves_kernel(left, right, _1, _2, _3, left_ref, right_ref, sent):
    copies = [
        pltpu.make_async_copy(left.at[:1], left_ref, sent.at[0]),
        pltpu.make_async_copy(right.at[1:], right_ref, sent.at[1]),
    ]
    for copy in copies:
        copy.start()
    for copy in copies:
        copy.wait()


def attention_kernel(
    k0, k1, k2, k3, v0, v1, v2, v3, queries, x_rows, bias_own, bias_other, mask, w_o, gain_ff, order,
    _left, _right, stream_ref, normed_ff_ref, keys, values, attended, bias, w_o_here, order_here, loaded,
):
    y = lax.axis_index("y")
    row_count, width = queries.shape
    half = row_count // 2
    head_size = width // HEADS
    loads = [
        pltpu.make_async_copy(bias_own, bias.at[:, :half], loaded.at[0]),
        pltpu.make_async_copy(bias_other, bias.at[:, half:], loaded.at[1]),
        pltpu.make_async_copy(w_o, w_o_here, loaded.at[2]),
        pltpu.make_async_copy(order, order_here, loaded.at[3]),
    ]
    for copy in loads:
        copy.start()
    for k, (key_block, value_block) in enumerate(((k0, v0), (k1, v1), (k2, v2), (k3, v3))):
        at = pl.multiple_of(lax.rem(y + (NY - k), NY) * row_count, row_count)
        keys[pl.ds(at, row_count), :] = key_block[...]
        values[pl.ds(at, row_count), :] = value_block[...]
    unusable = jnp.where(mask[...][None, :] > 0, 0.0, -1e30)
    attended[...] = jnp.zeros_like(attended)
    for copy in loads[:2]:
        copy.wait()
    together = 4
    for start in range(0, HEADS, together):
        heads = []
        for h in range(start, start + together):
            first, last = h * head_size, (h + 1) * head_size
            lo, hi = first // 128 * 128, -(-last // 128) * 128
            lanes = lax.broadcasted_iota(jnp.int32, (1, hi - lo), 1) + lo
            heads.append((h, lo, hi, (lanes >= first) & (lanes < last)))
        scores = [
            lax.dot_general(
                jnp.where(inside, queries[:, lo:hi], jnp.zeros((), jnp.bfloat16)),
                keys[:, lo:hi],
                (((1,), (1,)), ((), ())),
                preferred_element_type=jnp.float32,
            )
            for _, lo, hi, inside in heads
        ]
        weights, totals = [], []
        for (h, _, _, _), score in zip(heads, scores):
            score = score + bias[h].astype(jnp.float32) + unusable
            weight = jnp.exp(score - jnp.max(score, axis=1, keepdims=True))
            totals.append(jnp.sum(weight, axis=1, keepdims=True))
            weights.append(weight.astype(jnp.bfloat16))
        for (_, lo, hi, inside), weight, total in zip(heads, weights, totals):
            mixture = jnp.dot(weight, values[:, lo:hi], preferred_element_type=jnp.float32)
            attended[:, lo:hi] += jnp.where(inside, mixture / total, 0.0)
    for copy in loads[2:]:
        copy.wait()
    stream = x_rows[...].astype(jnp.float32) + jnp.dot(
        attended[...].astype(jnp.bfloat16), w_o_here[...], preferred_element_type=jnp.float32
    )
    stream_ref[...] = stream
    normed_ff = rms_norm(stream, gain_ff[...][None, :]).astype(jnp.bfloat16)
    normed_ff_ref[...] = jnp.dot(
        normed_ff, order_here[...], preferred_element_type=jnp.float32
    ).astype(jnp.bfloat16)


def transition_kernel(
    own, other, stream, order, here, left, right, far_0, far_1, keep_ref, send_ref,
    tiles, extras, arrived,
):
    c, x = lax.axis_index("c"), lax.axis_index("x")
    half = own.shape[0] // 2
    width = own.shape[1]
    count = tiles.shape[1]
    far = lax.rem(x + 2, NX) * 2
    parts = [
        (here, pl.ds(x * 2, 2)),
        (left, pl.ds(lax.rem(x + 3, NX) * 2, 2)),
        (right, pl.ds(lax.rem(x + 1, NX) * 2, 2)),
        (far_0, pl.ds(far, 1)),
        (far_1, pl.ds(far + 1, 1)),
    ]
    copies = []
    for k, (block, at) in enumerate(parts):
        copies.append(pltpu.make_async_copy(block.at[:, :count], tiles.at[at], arrived.at[2 * k]))
        copies.append(pltpu.make_async_copy(block.at[:, count:], extras.at[at], arrived.at[2 * k + 1]))
    for copy in copies:
        copy.start()
    rows = jnp.concatenate([own[...], other[...]], axis=0)
    for copy in copies:
        copy.wait()
    gate = jnp.dot(rows, tiles[0:3].reshape(width, width), preferred_element_type=jnp.float32)
    up = jnp.dot(rows, tiles[3:6].reshape(width, width), preferred_element_type=jnp.float32)
    hidden = (gate / (1.0 + jnp.exp(-gate)) * up).astype(jnp.bfloat16)
    across = (((1,), (1,)), ((), ()))
    update = jnp.concatenate(
        [
            lax.dot_general(
                hidden, tiles[6:8].reshape(2 * count, width), across, preferred_element_type=jnp.float32
            ),
            lax.dot_general(
                hidden, extras[...].reshape(-1, width), across, preferred_element_type=jnp.float32
            ),
        ],
        axis=1,
    )
    high = update.astype(jnp.bfloat16)
    low = (update - high.astype(jnp.float32)).astype(jnp.bfloat16)
    update = jnp.dot(high, order[...], preferred_element_type=jnp.float32) + jnp.dot(
        low, order[...], preferred_element_type=jnp.float32
    )
    keep_ref[c] = update[:half] + stream[:half]
    send_ref[c] = update[half : 2 * half] + stream[half:]
    send_ref[1 - c] = update[2 * half : 3 * half]
    keep_ref[1 - c] = update[3 * half :]


def swap_cores(value):
    return lax.ppermute(value, "c", [(0, 1), (1, 0)])


def others(value, axis, size):
    return [
        lax.ppermute(value, axis, [(i, (i + k) % size) for i in range(size)]) for k in range(1, size)
    ]


def kernel(f, name, specs, args, shapes, limit=8, scratch=(), out_spec=None, wait=1):
    def whole(shape):
        return pl.BlockSpec(shape, lambda i: (0,) * len(shape))

    specs = [whole(a.shape) if s is None else s for s, a in zip(specs, args, strict=True)]
    outs = tuple(jax.ShapeDtypeStruct(shape, dtype) for shape, dtype in shapes)
    return pl.pallas_call(
        f,
        grid=(1,),
        out_shape=outs,
        in_specs=specs,
        out_specs=tuple(out_spec or whole(o.shape) for o in outs),
        scratch_shapes=scratch,
        compiler_params=pltpu.CompilerParams(vmem_limit_bytes=limit * MIB),
        cost_estimate=pl.CostEstimate(
            flops=int(wait * MICROSECOND), bytes_accessed=0, transcendentals=0
        ),
        name=name,
    )(*args)


def body(states, ancestors, pair_bias, key_mask, gain_attn, w_qkv, w_o, gain_ff, w_in, w_out):
    part_count, block_rows, width = states.shape
    rows = block_rows * NC
    half = width // 2
    both = 2 * PIECE
    depth = w_out.shape[0]
    bf16, f32 = jnp.bfloat16, jnp.float32
    order_in, order_out = weight_orders(width)

    bias_other = swap_cores(pair_bias)
    (pieces,) = kernel(
        spread_kernel,
        "spread",
        [SMEM, None, None, None],
        (ancestors, states, w_in, w_out),
        [((GROUP // 2, 2, both, width + 128), bf16)],
        limit=56,
        scratch=[pltpu.VMEM((3 * depth, width), f32)],
    )
    pieces = lax.all_to_all(pieces.reshape(GROUP, both, width + 128), PARTICLE, 0, 0)
    picked, piece = kernel(
        pick_kernel,
        "pick",
        [None],
        (pieces,),
        [((GROUP, both, half), bf16), ((GROUP * (TILE + 1), half), bf16)],
        limit=56,
    )
    ring = [piece] + others(piece, "y", NY)
    (column,) = kernel(
        column_kernel,
        "column",
        [None] * NY,
        ring,
        [((2, GROUP * (TILE + 1), width), bf16)],
    )
    forward, back = ([(i, (i + k) % NX) for i in range(NX)] for k in (1, -1))
    left, right = lax.ppermute(column, "x", forward), lax.ppermute(column, "x", back)

    mine = lax.all_to_all(picked, PARTICLE, 0, 0)
    x_rows, normed, queries, *own = kernel(
        own_kernel,
        "own",
        [None, None, None, VMEM, ANY],
        (mine, swap_cores(mine), gain_attn, w_qkv, bias_other),
        [((rows, width), bf16)] * 5,
    )
    made = [own] + [
        kernel(other_kernel, "other", [None, VMEM], (block, w_qkv), [((rows, width), bf16)] * 2)
        for block in others(normed, "y", NY)
    ]
    left_half, right_half = kernel(
        halves_kernel,
        "halves",
        [ANY] * (2 + NY - 1),
        (left, right, *(k for k, _ in made[1:])),
        [((1,) + column.shape[1:], bf16)] * 2,
        out_spec=ANY,
        scratch=[pltpu.SemaphoreType.DMA((2,))],
    )
    far = [lax.ppermute(left_half, "x", forward), lax.ppermute(right_half, "x", back)]
    stream, normed_ff = kernel(
        attention_kernel,
        "attention",
        [None] * 10 + [ANY, ANY, None, ANY, None] + [ANY] * 3,
        (
            *[k for k, _ in made], *[v for _, v in made], queries, x_rows, pair_bias, bias_other,
            key_mask, w_o, gain_ff, order_in, left_half, right_half,
        ),
        [((rows, width), f32), ((rows, width), bf16)],
        limit=16,
        wait=4,
        scratch=[
            pltpu.VMEM((rows * NY, width), bf16),
            pltpu.VMEM((rows * NY, width), bf16),
            pltpu.VMEM((rows, width), f32),
            pltpu.VMEM((HEADS, rows, rows * NY), bf16),
            pltpu.VMEM((width, width), bf16),
            pltpu.VMEM((width, width), bf16),
            pltpu.SemaphoreType.DMA((4,)),
        ],
    )
    keep, send = kernel(
        transition_kernel,
        "transition",
        [None] * 4 + [ANY] * 5,
        (normed_ff, swap_cores(normed_ff), stream, order_out, column, left, right, *far),
        [((part_count, block_rows, width), f32)] * 2,
        limit=16,
        scratch=[
            pltpu.VMEM((TILES, GROUP * TILE, width), bf16),
            pltpu.VMEM((TILES, GROUP, width), bf16),
            pltpu.SemaphoreType.DMA((10,)),
        ],
    )
    return (keep + swap_cores(send)).astype(bf16)


def solution(mesh):
    fine = Mesh(mesh.devices.reshape(NX, NZ, NY, NC), ("x", "z", "y", "c"))
    token = ("y", "c")
    placed = (
        P(PARTICLE, token, None),
        P(PARTICLE),
        P(None, token, None),
        P(),
        P(),
        P(),
        P(),
        P(),
        P(None, PARTICLE, None),
        P(PARTICLE, None),
    )
    return jax.shard_map(
        body, mesh=fine, in_specs=placed, out_specs=P(PARTICLE, token, None), check_vma=False
    )
```

time: 100 us -> 94.6 us (0.946)
  local copies, waits for them, and re-layouts: 4.86 us -> 1.78 us
  starting transfers between devices: 40.2 us -> 38.6 us
    ppermute x0 -> x4, starting transfers between devices: none -> 4.22 us  [the longest x1 2.33 us: body(): lax.ppermute(right_half, 'x', back)]
    ppermute x9 -> x6, starting transfers between devices: 10.5 us -> 7.25 us  [others(): lax.ppermute(value, axis, [(i, (i + k) % size) for i in range(size)])]
    unnamed x28 -> x18, local copies, waits for them, and re-layouts: 4.86 us -> 1.78 us
    ppermute x9 -> x6, waiting for transfers between devices: 16.1 us -> 13.1 us  [others(): lax.ppermute(value, axis, [(i, (i + k) % size) for i in range(size)])]
    ppermute x0 -> x4, waiting for transfers between devices: none -> 2.77 us  [the longest x1 2.76 us: body(): lax.ppermute(left_half, 'x', forward)]
    ppermute x4, starting transfers between devices: 9.36 us -> 7.37 us  [swap_cores(): return lax.ppermute(value, 'c', [(0, 1), (1, 0)])]
    pallas_call x8 -> x10, Pallas kernels: 20.4 us -> 19.6 us  [kernel(): pl.pallas_call(f, grid=(1,), out_shape=outs, in_specs=specs, out_specs=tu...]
  transfers between devices with their start and end apart: 15 -> 16, of which waited for: 8 -> 10; matrix products, arithmetic and copies ran while one was open for 0% -> 0% of each run, Pallas kernels for 15% -> 13%
where the time goes in v3:
time: 94.6 us; the launch traced here: 94.2 us
  starting transfers between devices  38.6 us (41%)
  waiting for transfers between devices  33.3 us (35%)
  Pallas kernels  19.6 us (21%)
  local copies, waits for them, and re-layouts  1.78 us (2%)
    pallas_call x10, Pallas kernels, kernel(): pl.pallas_call(f, grid=(1,), out_shape=outs, in_specs=specs, out_specs=tu...  19.6 us
    ppermute x6, waiting for transfers between devices, others(): lax.ppermute(value, axis, [(i, (i + k) % size) for i in range(size)])  13.1 us
    all_to_all x1, waiting for transfers between devices, body(): lax.all_to_all(pieces.reshape(GROUP, both, width + 128), PARTICLE, 0, 0)  11.9 us
    all_to_all x1, starting transfers between devices, body(): lax.all_to_all(pieces.reshape(GROUP, both, width + 128), PARTICLE, 0, 0)  11.9 us
    all_to_all x1, starting transfers between devices, body(): mine = lax.all_to_all(picked, PARTICLE, 0, 0)  7.9 us
    ppermute x4, starting transfers between devices, swap_cores(): return lax.ppermute(value, 'c', [(0, 1), (1, 0)])  7.37 us
    ppermute x6, starting transfers between devices, others(): lax.ppermute(value, axis, [(i, (i + k) % size) for i in range(size)])  7.25 us
    ppermute x4, waiting for transfers between devices, swap_cores(): return lax.ppermute(value, 'c', [(0, 1), (1, 0)])  3.7 us
  transfers between devices with their start and end apart: 16, of which 10 were waited for; matrix products, arithmetic and copies ran while one was open for 0% of the time, Pallas kernels for 13%

profile of v3, /device:TPU:1, one launch (start us, length us, event | category | flops | bytes accessed | tf_op | source)
XLA Modules:
  0.0 94.2 jit_solution(13293839250601003460)
XLA Ops:
  0.0 2.1 %spread.1 = bf16[16,2,8,896]{3,2,1,0:T(8,128)(2,1)} custom-call(s32[2]{0:T(128)} %ancestors.1, bf16[2,64,768]{2,1,0:T(8,128)(2,1)} %states.1, bf16[2,24,1536]{2,1,0:T(8,128)(2,1)} %w_in.1, bf16[24,1536]{1,0:T(8,128)(2,1)} %w_out.1), custom_call_target="tpu_custom_call" | custom-call | flops 1000000000 | tf_op jit(solution)/shard_map/spread/pallas_call | solution.py:298
  2.1 11.9 %all-to-all-start = ((bf16[32,8,896]{2,1,0:T(8,128)(2,1)}), bf16[32,8,896]{2,1,0:T(8,128)(2,1)S(1)}, u32[]{:S(2)}, u32[]{:S(2)}) async-start(bf16[32,8,896]{2,1,0:T(8,128)(2,1)} %bitcast.1), calls=%async_computation | async-start | bytes 917504 | tf_op jit(solution)/shard_map/all_to_all | solution.py:332
  14.0 1.0 %collective-permute-start.1 = (bf16[16,64,512]{2,1,0:T(8,128)(2,1)}, bf16[16,64,512]{2,1,0:T(8,128)(2,1)}, u32[]{:S(2)}, u32[]{:S(2)}) collective-permute-start(bf16[16,64,512]{2,1,0:T(8,128)(2,1)} %bias_own.1), channel_id=1, source_target_pairs={{0,1},{1,0},{2,3},{3,2},{4,5},{5,4},{6,7},{7,6},{8,9},{9,8},{10,11... | collective-permute-start | bytes 3145736 | tf_op jit(solution)/shard_map/ppermute | solution.py:283
  15.0 11.9 %all-to-all-done.pieces = bf16[32,8,896]{2,1,0:T(8,128)(2,1)S(1)} async-done(((bf16[32,8,896]{2,1,0:T(8,128)(2,1)}), bf16[32,8,896]{2,1,0:T(8,128)(2,1)S(1)}, u32[]{:S(2)}, u32[]{:S(2)}) %all-to-all-start) | async-done | bytes 458784 | tf_op jit(solution)/shard_map/all_to_all | solution.py:332
  26.9 0.0 copy-start.8
  26.9 0.8 copy-done.8
  27.7 2.2 %pick.1 = (bf16[32,8,384]{2,1,0:T(8,128)(2,1)}, bf16[288,384]{1,0:T(8,128)(2,1)}) custom-call(bf16[32,8,896]{2,1,0:T(8,128)(2,1)} %copy-done.8), custom_call_target="tpu_custom_call" | custom-call | flops 1000000000 | tf_op jit(solution)/shard_map/pick/pallas_call | solution.py:298
  29.9 2.7 %collective-permute-start.7 = (bf16[288,384]{1,0:T(8,128)(2,1)}, bf16[288,384]{1,0:T(8,128)(2,1)}, u32[]{:S(2)}, u32[]{:S(2)}) collective-permute-start(bf16[288,384]{1,0:T(8,128)(2,1)} %get-tuple-element.36.w0), channel_id=1, source_target_pairs={{0,6},{2,0},{4,2},{6,4},{1,7},{3,1},{5,3},{7,5},{8,14},{10,8},{12,... | collective-permute-start | bytes 663560 | tf_op jit(solution)/shard_map/ppermute | solution.py:288
  32.6 0.4 collective-permute-start.6
  33.0 0.7 collective-permute-start.5
  33.7 7.9 %all-to-all-start.1 = ((bf16[32,8,384]{2,1,0:T(8,128)(2,1)}), bf16[32,8,384]{2,1,0:T(8,128)(2,1)}, u32[]{:S(2)}, u32[]{:S(2)}) async-start(bf16[32,8,384]{2,1,0:T(8,128)(2,1)} %get-tuple-element.24), calls=%async_computation.1 | async-start | bytes 393216 | tf_op jit(solution)/shard_map/all_to_all | solution.py:352
  41.6 0.0 copy-start
  41.6 0.0 copy-start.2
  41.6 0.0 collective-permute-done.7.w3
  41.6 0.0 collective-permute-done.6.w2
  41.6 2.9 %collective-permute-done.5.w1 = bf16[288,384]{1,0:T(8,128)(2,1)} collective-permute-done((bf16[288,384]{1,0:T(8,128)(2,1)}, bf16[288,384]{1,0:T(8,128)(2,1)}, u32[]{:S(2)}, u32[]{:S(2)}) %collective-permute-start.5) | collective-permute-done | bytes 221216 | tf_op jit(solution)/shard_map/ppermute | solution.py:288
  44.5 0.0 copy-start.4
  44.5 0.9 copy-done.4
  45.5 2.2 %column.1.here = bf16[2,288,768]{2,1,0:T(8,128)(2,1)} custom-call(bf16[288,384]{1,0:T(8,128)(2,1)S(1)} %copy-done.4, bf16[288,384]{1,0:T(8,128)(2,1)} %collective-permute-done.5.w1, bf16[288,384]{1,0:T(8,128)(2,1)} %collective-permute-done.6.w2, bf16[288,384]{1,0:T(8,128)(2,1)} %collective-permute-done.7.w3), custom_call_target="tpu_custom_call" | custom-call | flops 1000000000 | tf_op jit(solution)/shard_map/column/pallas_call | solution.py:298
  47.6 1.4 %collective-permute-start.9 = (bf16[2,288,768]{2,1,0:T(8,128)(2,1)}, bf16[2,288,768]{2,1,0:T(8,128)(2,1)}, u32[]{:S(2)}, u32[]{:S(2)}) collective-permute-start(bf16[2,288,768]{2,1,0:T(8,128)(2,1)} %column.1.here), channel_id=1, source_target_pairs={{0,192},{64,0},{128,64},{192,128},{1,193},{65,1},{129,65},{193,129... | collective-permute-start | bytes 2654216 | tf_op jit(solution)/shard_map/ppermute | solution.py:350
  49.0 0.1 collective-permute-start.8
  49.1 1.9 %all-to-all-done.1.mine = bf16[32,8,384]{2,1,0:T(8,128)(2,1)} async-done(((bf16[32,8,384]{2,1,0:T(8,128)(2,1)}), bf16[32,8,384]{2,1,0:T(8,128)(2,1)}, u32[]{:S(2)}, u32[]{:S(2)}) %all-to-all-start.1) | async-done | bytes 196640 | tf_op jit(solution)/shard_map/all_to_all | solution.py:352
  50.9 3.8 %collective-permute-start = (bf16[32,8,384]{2,1,0:T(8,128)(2,1)}, bf16[32,8,384]{2,1,0:T(8,128)(2,1)S(1)}, u32[]{:S(2)}, u32[]{:S(2)}) collective-permute-start(bf16[32,8,384]{2,1,0:T(8,128)(2,1)} %all-to-all-done.1.mine), channel_id=1, source_target_pairs={{0,1},{1,0},{2,3},{3,2},{4,5},{5,4},{6,7},{7,6},{8,9},{9,8},{10,11... | collective-permute-start | bytes 589832 | tf_op jit(solution)/shard_map/ppermute | solution.py:283
  54.7 0.0 collective-permute-done.1._bias.bias_other
  54.7 1.3 %collective-permute-done.theirs = bf16[32,8,384]{2,1,0:T(8,128)(2,1)S(1)} collective-permute-done((bf16[32,8,384]{2,1,0:T(8,128)(2,1)}, bf16[32,8,384]{2,1,0:T(8,128)(2,1)S(1)}, u32[]{:S(2)}, u32[]{:S(2)}) %collective-permute-start) | collective-permute-done | bytes 196640 | tf_op jit(solution)/shard_map/ppermute | solution.py:283
  56.0 0.0 copy-done
  56.0 0.0 copy-done.2
  56.0 1.8 %own.1 = (bf16[128,768]{1,0:T(8,128)(2,1)S(1)}, bf16[128,768]{1,0:T(8,128)(2,1)S(1)}, bf16[128,768]{1,0:T(8,128)(2,1)S(1)}, bf16[128,768]{1,0:T(8,128)(2,1)S(1)}, bf16[128,768]{1,0:T(8,128)(2,1)S(1)}) custom-call(bf16[32,8,384]{2,1,0:T(8,128)(2,1)} %all-to-all-done.1.mine, bf16[32,8,384]{2,1,0:T(8,128)(2,1)S(1)} %collective-permute-done.theirs, ...), custom_call_target="tpu_custom_call" | custom-call | flops 1000000000 | tf_op jit(solution)/shard_map/own/pallas_call | solution.py:298
  57.8 2.1 %collective-permute-start.4 = (bf16[128,768]{1,0:T(8,128)(2,1)S(1)}, bf16[128,768]{1,0:T(8,128)(2,1)S(1)}, u32[]{:S(2)}, u32[]{:S(2)}) collective-permute-start(bf16[128,768]{1,0:T(8,128)(2,1)S(1)} %get-tuple-element.26), channel_id=1, source_target_pairs={{0,6},{2,0},{4,2},{6,4},{1,7},{3,1},{5,3},{7,5},{8,14},{10,8},{12,... | collective-permute-start | bytes 589832 | tf_op jit(solution)/shard_map/ppermute | solution.py:288
  59.9 1.4 %collective-permute-start.3 = (bf16[128,768]{1,0:T(8,128)(2,1)S(1)}, bf16[128,768]{1,0:T(8,128)(2,1)S(1)}, u32[]{:S(2)}, u32[]{:S(2)}) collective-permute-start(bf16[128,768]{1,0:T(8,128)(2,1)S(1)} %get-tuple-element.26), channel_id=1, source_target_pairs={{0,4},{2,6},{4,0},{6,2},{1,5},{3,7},{5,1},{7,3},{8,12},{10,14},{12... | collective-permute-start | bytes 589832 | tf_op jit(solution)/shard_map/ppermute | solution.py:288
  61.3 0.0 collective-permute-start.2
  61.3 3.1 %collective-permute-done.4.normed = bf16[128,768]{1,0:T(8,128)(2,1)S(1)} collective-permute-done((bf16[128,768]{1,0:T(8,128)(2,1)S(1)}, bf16[128,768]{1,0:T(8,128)(2,1)S(1)}, u32[]{:S(2)}, u32[]{:S(2)}) %collective-permute-start.4) | collective-permute-done | bytes 196640 | tf_op jit(solution)/shard_map/ppermute | solution.py:288
  64.4 0.5 other.5
  64.9 2.3 %collective-permute-done.3.normed = bf16[128,768]{1,0:T(8,128)(2,1)S(1)} collective-permute-done((bf16[128,768]{1,0:T(8,128)(2,1)S(1)}, bf16[128,768]{1,0:T(8,128)(2,1)S(1)}, u32[]{:S(2)}, u32[]{:S(2)}) %collective-permute-start.3) | collective-permute-done | bytes 196640 | tf_op jit(solution)/shard_map/ppermute | solution.py:288
  67.2 0.5 other.4
  67.7 4.7 %collective-permute-done.2.normed = bf16[128,768]{1,0:T(8,128)(2,1)S(1)} collective-permute-done((bf16[128,768]{1,0:T(8,128)(2,1)S(1)}, bf16[128,768]{1,0:T(8,128)(2,1)S(1)}, u32[]{:S(2)}, u32[]{:S(2)}) %collective-permute-start.2) | collective-permute-done | bytes 196640 | tf_op jit(solution)/shard_map/ppermute | solution.py:288
  72.4 0.5 other.3
  72.9 0.0 collective-permute-done.9.right
  72.9 0.0 collective-permute-done.8.left
  73.0 0.0 copy-start.3
  73.0 0.0 copy-start.5
  73.0 0.0 copy-start.6
  73.0 0.0 copy-start.7
  73.0 1.3 %halves.1 = (bf16[1,288,768]{2,1,0:T(8,128)(2,1)S(1)}, bf16[1,288,768]{2,1,0:T(8,128)(2,1)S(1)}) custom-call(bf16[2,288,768]{2,1,0:T(8,128)(2,1)} %collective-permute-done.8.left, bf16[2,288,768]{2,1,0:T(8,128)(2,1)} %collective-permute-done.9.right, bf16[128,768]{1,0:T(8,128)(2,1)S(1)} %get-tuple-element.27._1.k1, ...), custom_call_target="tpu_custom_call" | custom-call | flops 1000000000 | tf_op jit(solution)/shard_map/halves/pallas_call | solution.py:298
  74.3 0.4 collective-permute-start.11
  74.7 2.3 %collective-permute-start.12 = (bf16[1,288,768]{2,1,0:T(8,128)(2,1)S(1)}, bf16[1,288,768]{2,1,0:T(8,128)(2,1)S(1)}, u32[]{:S(2)}, u32[]{:S(2)}) collective-permute-start(bf16[1,288,768]{2,1,0:T(8,128)(2,1)S(1)} %get-tuple-element.38._right), channel_id=1, source_target_pairs={{0,192},{64,0},{128,64},{192,128},{1,193},{65,1},{129,65},{193,129... | collective-permute-start | bytes 1327112 | tf_op jit(solution)/shard_map/ppermute | solution.py:373
  77.1 0.0 copy-done.3
  77.1 0.0 copy-done.5
  77.1 0.0 copy-done.6
  77.1 0.0 copy-done.7
  77.1 0.0 copy-start.1
  77.1 4.8 %attention.1 = (f32[128,768]{1,0:T(8,128)S(1)}, bf16[128,768]{1,0:T(8,128)(2,1)S(1)}) custom-call(bf16[128,768]{1,0:T(8,128)(2,1)S(1)} %get-tuple-element.25.k0, bf16[128,768]{1,0:T(8,128)(2,1)S(1)} %get-tuple-element.27._1.k1, bf16[128,768]{1,0:T(8,128)(2,1)S(1)} %get-tuple-element.28._2.k2, bf16[128,768]{1,0:T(8,128)(2,1)S(1)} %get-tuple-element.29._3.k3, ...), custom_call_target="tpu_custom_call" | custom-call | flops 4000000000 | tf_op jit(solution)/shard_map/attention/pallas_call | solution.py:298
  81.9 1.1 %collective-permute-start.10 = (bf16[128,768]{1,0:T(8,128)(2,1)S(1)}, bf16[128,768]{1,0:T(8,128)(2,1)S(1)}, u32[]{:S(2)}, u32[]{:S(2)}) collective-permute-start(bf16[128,768]{1,0:T(8,128)(2,1)S(1)} %get-tuple-element.39.own), channel_id=1, source_target_pairs={{0,1},{1,0},{2,3},{3,2},{4,5},{5,4},{6,7},{7,6},{8,9},{9,8},{10,11... | collective-permute-start | bytes 589832 | tf_op jit(solution)/shard_map/ppermute | solution.py:283
  83.0 1.1 %collective-permute-done.10.other = bf16[128,768]{1,0:T(8,128)(2,1)S(1)} collective-permute-done((bf16[128,768]{1,0:T(8,128)(2,1)S(1)}, bf16[128,768]{1,0:T(8,128)(2,1)S(1)}, u32[]{:S(2)}, u32[]{:S(2)}) %collective-permute-start.10) | collective-permute-done | bytes 196640 | tf_op jit(solution)/shard_map/ppermute | solution.py:283
  84.1 2.8 %collective-permute-done.11.far_0 = bf16[1,288,768]{2,1,0:T(8,128)(2,1)S(1)} collective-permute-done((bf16[1,288,768]{2,1,0:T(8,128)(2,1)S(1)}, bf16[1,288,768]{2,1,0:T(8,128)(2,1)S(1)}, u32[]{:S(2)}, u32[]{:S(2)}) %collective-permute-start.11) | collective-permute-done | bytes 442400 | tf_op jit(solution)/shard_map/ppermute | solution.py:373
  86.9 0.0 collective-permute-done.12.far_1
  86.9 0.0 copy-done.1
  86.9 3.8 %transition.1 = (f32[2,64,768]{2,1,0:T(8,128)S(1)}, f32[2,64,768]{2,1,0:T(8,128)S(1)}) custom-call(bf16[128,768]{1,0:T(8,128)(2,1)S(1)} %get-tuple-element.39.own, bf16[128,768]{1,0:T(8,128)(2,1)S(1)} %collective-permute-done.10.other, f32[128,768]{1,0:T(8,128)S(1)} %get-tuple-element.40.stream, bf16[768,768]{1,0:T(8,128)(2,1)S(1)} %copy-done.1, ...), custom_call_target="tpu_custom_call" | custom-call | flops 1000000000 | tf_op jit(solution)/shard_map/transition/pallas_call | solution.py:298
  90.7 1.4 %collective-permute-start.13 = (f32[2,64,768]{2,1,0:T(8,128)S(1)}, f32[2,64,768]{2,1,0:T(8,128)S(1)}, u32[]{:S(2)}, u32[]{:S(2)}) collective-permute-start(f32[2,64,768]{2,1,0:T(8,128)S(1)} %get-tuple-element.42), channel_id=1, source_target_pairs={{0,1},{1,0},{2,3},{3,2},{4,5},{5,4},{6,7},{7,6},{8,9},{9,8},{10,11... | collective-permute-start | bytes 1179656 | tf_op jit(solution)/shard_map/ppermute | solution.py:283
  92.1 1.3 %collective-permute-done.13 = f32[2,64,768]{2,1,0:T(8,128)S(1)} collective-permute-done((f32[2,64,768]{2,1,0:T(8,128)S(1)}, f32[2,64,768]{2,1,0:T(8,128)S(1)}, u32[]{:S(2)}, u32[]{:S(2)}) %collective-permute-start.13) | collective-permute-done | bytes 393248 | tf_op jit(solution)/shard_map/ppermute | solution.py:283
  93.5 0.7 add_convert_fusion
Async XLA Ops:
  2.1 24.8 %all-to-all-start = ((bf16[32,8,896]{2,1,0:T(8,128)(2,1)}), bf16[32,8,896]{2,1,0:T(8,128)(2,1)S(1)}, u32[]{:S(2)}, u32[]{:S(2)}) async-start(bf16[32,8,896]{2,1,0:T(8,128)(2,1)} %bitcast.1), calls=%async_computation | async-start | bytes 917504 | tf_op jit(solution)/shard_map/all_to_all | solution.py:332
  14.0 40.7 %collective-permute-start.1 = (bf16[16,64,512]{2,1,0:T(8,128)(2,1)}, bf16[16,64,512]{2,1,0:T(8,128)(2,1)}, u32[]{:S(2)}, u32[]{:S(2)}) collective-permute-start(bf16[16,64,512]{2,1,0:T(8,128)(2,1)} %bias_own.1), channel_id=1, source_target_pairs={{0,1},{1,0},{2,3},{3,2},{4,5},{5,4},{6,7},{7,6},{8,9},{9,8},{10,11... | collective-permute-start | bytes 3145736 | tf_op jit(solution)/shard_map/ppermute | solution.py:283
  26.9 0.8 copy-start.8
  29.9 11.7 %collective-permute-start.7 = (bf16[288,384]{1,0:T(8,128)(2,1)}, bf16[288,384]{1,0:T(8,128)(2,1)}, u32[]{:S(2)}, u32[]{:S(2)}) collective-permute-start(bf16[288,384]{1,0:T(8,128)(2,1)} %get-tuple-element.36.w0), channel_id=1, source_target_pairs={{0,6},{2,0},{4,2},{6,4},{1,7},{3,1},{5,3},{7,5},{8,14},{10,8},{12,... | collective-permute-start | bytes 663560 | tf_op jit(solution)/shard_map/ppermute | solution.py:288
  32.6 9.0 %collective-permute-start.6 = (bf16[288,384]{1,0:T(8,128)(2,1)}, bf16[288,384]{1,0:T(8,128)(2,1)}, u32[]{:S(2)}, u32[]{:S(2)}) collective-permute-start(bf16[288,384]{1,0:T(8,128)(2,1)} %get-tuple-element.36.w0), channel_id=1, source_target_pairs={{0,4},{2,6},{4,0},{6,2},{1,5},{3,7},{5,1},{7,3},{8,12},{10,14},{12... | collective-permute-start | bytes 663560 | tf_op jit(solution)/shard_map/ppermute | solution.py:288
  33.0 11.6 %collective-permute-start.5 = (bf16[288,384]{1,0:T(8,128)(2,1)}, bf16[288,384]{1,0:T(8,128)(2,1)}, u32[]{:S(2)}, u32[]{:S(2)}) collective-permute-start(bf16[288,384]{1,0:T(8,128)(2,1)} %get-tuple-element.36.w0), channel_id=1, source_target_pairs={{0,2},{2,4},{4,6},{6,0},{1,3},{3,5},{5,7},{7,1},{8,10},{10,12},{12... | collective-permute-start | bytes 663560 | tf_op jit(solution)/shard_map/ppermute | solution.py:288
  33.7 17.3 %all-to-all-start.1 = ((bf16[32,8,384]{2,1,0:T(8,128)(2,1)}), bf16[32,8,384]{2,1,0:T(8,128)(2,1)}, u32[]{:S(2)}, u32[]{:S(2)}) async-start(bf16[32,8,384]{2,1,0:T(8,128)(2,1)} %get-tuple-element.24), calls=%async_computation.1 | async-start | bytes 393216 | tf_op jit(solution)/shard_map/all_to_all | solution.py:352
  41.6 14.4 %copy-start = (bf16[768,2304]{1,0:T(8,128)(2,1)S(1)}, bf16[768,2304]{1,0:T(8,128)(2,1)}, u32[]{:S(2)}) copy-start(bf16[768,2304]{1,0:T(8,128)(2,1)} %w_qkv.7) | copy-start | bytes 10616836
  41.6 14.4 %copy-start.2 = (f32[768]{0:T(1024)S(1)}, f32[768]{0:T(1024)}, u32[]{:S(2)}) copy-start(f32[768]{0:T(1024)} %gain.1) | copy-start | bytes 9220
  44.5 0.9 copy-start.4
  47.6 25.3 %collective-permute-start.9 = (bf16[2,288,768]{2,1,0:T(8,128)(2,1)}, bf16[2,288,768]{2,1,0:T(8,128)(2,1)}, u32[]{:S(2)}, u32[]{:S(2)}) collective-permute-start(bf16[2,288,768]{2,1,0:T(8,128)(2,1)} %column.1.here), channel_id=1, source_target_pairs={{0,192},{64,0},{128,64},{192,128},{1,193},{65,1},{129,65},{193,129... | collective-permute-start | bytes 2654216 | tf_op jit(solution)/shard_map/ppermute | solution.py:350
  49.0 23.9 %collective-permute-start.8 = (bf16[2,288,768]{2,1,0:T(8,128)(2,1)}, bf16[2,288,768]{2,1,0:T(8,128)(2,1)}, u32[]{:S(2)}, u32[]{:S(2)}) collective-permute-start(bf16[2,288,768]{2,1,0:T(8,128)(2,1)} %column.1.here), channel_id=1, source_target_pairs={{0,64},{64,128},{128,192},{192,0},{1,65},{65,129},{129,193},{193,1... | collective-permute-start | bytes 2654216 | tf_op jit(solution)/shard_map/ppermute | solution.py:350
  50.9 5.0 %collective-permute-start = (bf16[32,8,384]{2,1,0:T(8,128)(2,1)}, bf16[32,8,384]{2,1,0:T(8,128)(2,1)S(1)}, u32[]{:S(2)}, u32[]{:S(2)}) collective-permute-start(bf16[32,8,384]{2,1,0:T(8,128)(2,1)} %all-to-all-done.1.mine), channel_id=1, source_target_pairs={{0,1},{1,0},{2,3},{3,2},{4,5},{5,4},{6,7},{7,6},{8,9},{9,8},{10,11... | collective-permute-start | bytes 589832 | tf_op jit(solution)/shard_map/ppermute | solution.py:283
  57.8 6.6 %collective-permute-start.4 = (bf16[128,768]{1,0:T(8,128)(2,1)S(1)}, bf16[128,768]{1,0:T(8,128)(2,1)S(1)}, u32[]{:S(2)}, u32[]{:S(2)}) collective-permute-start(bf16[128,768]{1,0:T(8,128)(2,1)S(1)} %get-tuple-element.26), channel_id=1, source_target_pairs={{0,6},{2,0},{4,2},{6,4},{1,7},{3,1},{5,3},{7,5},{8,14},{10,8},{12,... | collective-permute-start | bytes 589832 | tf_op jit(solution)/shard_map/ppermute | solution.py:288
  59.9 7.3 %collective-permute-start.3 = (bf16[128,768]{1,0:T(8,128)(2,1)S(1)}, bf16[128,768]{1,0:T(8,128)(2,1)S(1)}, u32[]{:S(2)}, u32[]{:S(2)}) collective-permute-start(bf16[128,768]{1,0:T(8,128)(2,1)S(1)} %get-tuple-element.26), channel_id=1, source_target_pairs={{0,4},{2,6},{4,0},{6,2},{1,5},{3,7},{5,1},{7,3},{8,12},{10,14},{12... | collective-permute-start | bytes 589832 | tf_op jit(solution)/shard_map/ppermute | solution.py:288
  61.3 11.1 %collective-permute-start.2 = (bf16[128,768]{1,0:T(8,128)(2,1)S(1)}, bf16[128,768]{1,0:T(8,128)(2,1)S(1)}, u32[]{:S(2)}, u32[]{:S(2)}) collective-permute-start(bf16[128,768]{1,0:T(8,128)(2,1)S(1)} %get-tuple-element.26), channel_id=1, source_target_pairs={{0,2},{2,4},{4,6},{6,0},{1,3},{3,5},{5,7},{7,1},{8,10},{10,12},{12... | collective-permute-start | bytes 589832 | tf_op jit(solution)/shard_map/ppermute | solution.py:288
  73.0 4.1 %copy-start.3 = (bf16[768,768]{1,0:T(8,128)(2,1)S(1)}, bf16[768,768]{1,0:T(8,128)(2,1)}, u32[]{:S(2)}) copy-start(bf16[768,768]{1,0:T(8,128)(2,1)} %w_o.1) | copy-start | bytes 3538948
  73.0 4.1 %copy-start.5 = (f32[768]{0:T(1024)S(1)}, f32[768]{0:T(1024)}, u32[]{:S(2)}) copy-start(f32[768]{0:T(1024)} %gain_ff.1) | copy-start | bytes 9220
  73.0 4.1 %copy-start.6 = (s32[512]{0:T(512)S(1)}, s32[512]{0:T(512)}, u32[]{:S(2)}) copy-start(s32[512]{0:T(512)} %mask.1) | copy-start | bytes 6148
  73.0 4.1 %copy-start.7 = (bf16[768,768]{1,0:T(8,128)(2,1)S(1)}, bf16[768,768]{1,0:T(8,128)(2,1)}, u32[]{:S(2)}) copy-start(bf16[768,768]{1,0:T(8,128)(2,1)} %constant.4.clone.order) | copy-start | bytes 3538948
  74.3 12.5 %collective-permute-start.11 = (bf16[1,288,768]{2,1,0:T(8,128)(2,1)S(1)}, bf16[1,288,768]{2,1,0:T(8,128)(2,1)S(1)}, u32[]{:S(2)}, u32[]{:S(2)}) collective-permute-start(bf16[1,288,768]{2,1,0:T(8,128)(2,1)S(1)} %get-tuple-element.37._left), channel_id=1, source_target_pairs={{0,64},{64,128},{128,192},{192,0},{1,65},{65,129},{129,193},{193,1... | collective-permute-start | bytes 1327112 | tf_op jit(solution)/shard_map/ppermute | solution.py:373
  74.7 12.1 %collective-permute-start.12 = (bf16[1,288,768]{2,1,0:T(8,128)(2,1)S(1)}, bf16[1,288,768]{2,1,0:T(8,128)(2,1)S(1)}, u32[]{:S(2)}, u32[]{:S(2)}) collective-permute-start(bf16[1,288,768]{2,1,0:T(8,128)(2,1)S(1)} %get-tuple-element.38._right), channel_id=1, source_target_pairs={{0,192},{64,0},{128,64},{192,128},{1,193},{65,1},{129,65},{193,129... | collective-permute-start | bytes 1327112 | tf_op jit(solution)/shard_map/ppermute | solution.py:373
  77.1 9.8 %copy-start.1 = (bf16[768,768]{1,0:T(8,128)(2,1)S(1)}, bf16[768,768]{1,0:T(8,128)(2,1)}, u32[]{:S(2)}) copy-start(bf16[768,768]{1,0:T(8,128)(2,1)} %constant.5.clone.order) | copy-start | bytes 3538948
  81.9 2.2 %collective-permute-start.10 = (bf16[128,768]{1,0:T(8,128)(2,1)S(1)}, bf16[128,768]{1,0:T(8,128)(2,1)S(1)}, u32[]{:S(2)}, u32[]{:S(2)}) collective-permute-start(bf16[128,768]{1,0:T(8,128)(2,1)S(1)} %get-tuple-element.39.own), channel_id=1, source_target_pairs={{0,1},{1,0},{2,3},{3,2},{4,5},{5,4},{6,7},{7,6},{8,9},{9,8},{10,11... | collective-permute-start | bytes 589832 | tf_op jit(solution)/shard_map/ppermute | solution.py:283
  90.7 2.8 %collective-permute-start.13 = (f32[2,64,768]{2,1,0:T(8,128)S(1)}, f32[2,64,768]{2,1,0:T(8,128)S(1)}, u32[]{:S(2)}, u32[]{:S(2)}) collective-permute-start(f32[2,64,768]{2,1,0:T(8,128)S(1)} %get-tuple-element.42), channel_id=1, source_target_pairs={{0,1},{1,0},{2,3},{3,2},{4,5},{5,4},{6,7},{7,6},{8,9},{9,8},{10,11... | collective-permute-start | bytes 1179656 | tf_op jit(solution)/shard_map/ppermute | solution.py:283

commit v4 on v3

--- a/solution.py
+++ b/solution.py
@@ -132,30 +132,30 @@
         ref[pl.ds(pl.multiple_of(slot * half, half), half), :] = values[at : at + half].astype(ref.dtype)
 
 
-def own_kernel(
-    mine, theirs, gain, w_qkv, _bias, x_ref, normed_ref, queries_ref, keys_ref, values_ref
-):
-    width = x_ref.shape[1]
-    rows = chip_rows(mine, theirs, width)
+def own_kernel(mine, theirs, gain, _bias, x_ref, normed_ref):
+    rows = chip_rows(mine, theirs, x_ref.shape[1])
     x_ref[...] = rows.astype(jnp.bfloat16)
-    normed = rms_norm(rows, gain[...][None, :])
-    store_rows(normed_ref, normed)
-    normed = normed.astype(jnp.bfloat16)
-    projected = jnp.dot(normed, w_qkv[...], preferred_element_type=jnp.float32)
+    store_rows(normed_ref, rms_norm(rows, gain[...][None, :]))
+
+
+def project_kernel(normed, w_qkv, queries_ref, keys_ref, values_ref):
+    width = keys_ref.shape[1]
+    projected = jnp.dot(normed[...], w_qkv[...], preferred_element_type=jnp.float32)
     scale = 1.0 / math.sqrt(width // HEADS)
-    queries_ref[...] = (projected[:, :width] * scale).astype(jnp.bfloat16)
-    store_rows(keys_ref, projected[:, width : 2 * width])
-    store_rows(values_ref, projected[:, 2 * width :])
-
-
-def other_kernel(normed, w_qkv, keys_ref, values_ref):
+    store_rows(queries_ref, projected[:, :width] * scale)
+    keys_ref[...] = projected[:, width : 2 * width].astype(jnp.bfloat16)
+    values_ref[...] = projected[:, 2 * width :].astype(jnp.bfloat16)
+
+
+def other_kernel(normed, w_qkv, *refs):
+    keys_ref, values_ref = refs[-2:]
     width = keys_ref.shape[1]
     projected = jnp.dot(normed[...], w_qkv[:, width:], preferred_element_type=jnp.float32)
     keys_ref[...] = projected[:, :width].astype(jnp.bfloat16)
     values_ref[...] = projected[:, width:].astype(jnp.bfloat16)
 
 
-def halves_kernel(left, right, _1, _2, _3, left_ref, right_ref, sent):
+def halves_kernel(left, right, _after, left_ref, right_ref, sent):
     copies = [
         pltpu.make_async_copy(left.at[:1], left_ref, sent.at[0]),
         pltpu.make_async_copy(right.at[1:], right_ref, sent.at[1]),
@@ -174,13 +174,20 @@
     row_count, width = queries.shape
     half = row_count // 2
     head_size = width // HEADS
-    loads = [
-        pltpu.make_async_copy(bias_own, bias.at[:, :half], loaded.at[0]),
-        pltpu.make_async_copy(bias_other, bias.at[:, half:], loaded.at[1]),
-        pltpu.make_async_copy(w_o, w_o_here, loaded.at[2]),
-        pltpu.make_async_copy(order, order_here, loaded.at[3]),
+    together = 4
+    loads = []
+    for i in range(HEADS // together):
+        part = pl.ds(i * together, together)
+        for j, source in enumerate((bias_own, bias_other)):
+            at = pl.ds(j * half, half)
+            loads.append(
+                pltpu.make_async_copy(source.at[part], bias.at[part, at], loaded.at[2 * i + j])
+            )
+    later = [
+        pltpu.make_async_copy(w_o, w_o_here, loaded.at[len(loads)]),
+        pltpu.make_async_copy(order, order_here, loaded.at[len(loads) + 1]),
     ]
-    for copy in loads:
+    for copy in loads + later:
         copy.start()
     for k, (key_block, value_block) in enumerate(((k0, v0), (k1, v1), (k2, v2), (k3, v3))):
         at = pl.multiple_of(lax.rem(y + (NY - k), NY) * row_count, row_count)
@@ -188,9 +195,6 @@
         values[pl.ds(at, row_count), :] = value_block[...]
     unusable = jnp.where(mask[...][None, :] > 0, 0.0, -1e30)
     attended[...] = jnp.zeros_like(attended)
-    for copy in loads[:2]:
-        copy.wait()
-    together = 4
     for start in range(0, HEADS, together):
         heads = []
         for h in range(start, start + together):
@@ -207,6 +211,8 @@
             )
             for _, lo, hi, inside in heads
         ]
+        for j in range(2):
+            loads[2 * (start // together) + j].wait()
         weights, totals = [], []
         for (h, _, _, _), score in zip(heads, scores):
             score = score + bias[h].astype(jnp.float32) + unusable
@@ -216,7 +222,7 @@
         for (_, lo, hi, inside), weight, total in zip(heads, weights, totals):
             mixture = jnp.dot(weight, values[:, lo:hi], preferred_element_type=jnp.float32)
             attended[:, lo:hi] += jnp.where(inside, mixture / total, 0.0)
-    for copy in loads[2:]:
+    for copy in later:
         copy.wait()
     stream = x_rows[...].astype(jnp.float32) + jnp.dot(
         attended[...].astype(jnp.bfloat16), w_o_here[...], preferred_element_type=jnp.float32
@@ -336,7 +342,7 @@
         [None],
         (pieces,),
         [((GROUP, both, half), bf16), ((GROUP * (TILE + 1), half), bf16)],
-        limit=56,
+        limit=40,
     )
     ring = [piece] + others(piece, "y", NY)
     (column,) = kernel(
@@ -350,26 +356,38 @@
     left, right = lax.ppermute(column, "x", forward), lax.ppermute(column, "x", back)
 
     mine = lax.all_to_all(picked, PARTICLE, 0, 0)
-    x_rows, normed, queries, *own = kernel(
+    x_rows, normed = kernel(
         own_kernel,
         "own",
-        [None, None, None, VMEM, ANY],
-        (mine, swap_cores(mine), gain_attn, w_qkv, bias_other),
-        [((rows, width), bf16)] * 5,
-    )
-    made = [own] + [
+        [None, None, None, ANY],
+        (mine, swap_cores(mine), gain_attn, bias_other),
+        [((rows, width), bf16)] * 2,
+    )
+    queries, *own = kernel(
+        project_kernel, "project", [None, VMEM], (normed, w_qkv), [((rows, width), bf16)] * 3
+    )
+    blocks = others(normed, "y", NY)
+    made = [
         kernel(other_kernel, "other", [None, VMEM], (block, w_qkv), [((rows, width), bf16)] * 2)
-        for block in others(normed, "y", NY)
+        for block in blocks[1:]
     ]
     left_half, right_half = kernel(
         halves_kernel,
         "halves",
-        [ANY] * (2 + NY - 1),
-        (left, right, *(k for k, _ in made[1:])),
+        [ANY] * 3,
+        (left, right, made[0][0]),
         [((1,) + column.shape[1:], bf16)] * 2,
         out_spec=ANY,
         scratch=[pltpu.SemaphoreType.DMA((2,))],
     )
+    first = kernel(
+        other_kernel,
+        "other",
+        [None, VMEM, ANY, ANY],
+        (blocks[0], w_qkv, left_half, right_half),
+        [((rows, width), bf16)] * 2,
+    )
+    made = [own, first] + made
     far = [lax.ppermute(left_half, "x", forward), lax.ppermute(right_half, "x", back)]
     stream, normed_ff = kernel(
         attention_kernel,
@@ -389,7 +407,7 @@
             pltpu.VMEM((HEADS, rows, rows * NY), bf16),
             pltpu.VMEM((width, width), bf16),
             pltpu.VMEM((width, width), bf16),
-            pltpu.SemaphoreType.DMA((4,)),
+            pltpu.SemaphoreType.DMA((10,)),
         ],
     )
     keep, send = kernel(

time: 94.6 us -> 88.8 us (0.939)
  the two profiles are of different devices: /device:TPU:1 before, /device:TPU:71 now
where the time goes in v4:
time: 88.8 us; the launch traced here: 88.5 us
  starting transfers between devices  40.2 us (45%)
  waiting for transfers between devices  29.2 us (33%)
  Pallas kernels  17.3 us (19%)
  local copies, waits for them, and re-layouts  0.9 us (1%)
    pallas_call x11, Pallas kernels, kernel(): pl.pallas_call(f, grid=(1,), out_shape=outs, in_specs=specs, out_specs=tu...  17.3 us
    all_to_all x1, waiting for transfers between devices, body(): lax.all_to_all(pieces.reshape(GROUP, both, width + 128), PARTICLE, 0, 0)  11.7 us
    all_to_all x1, starting transfers between devices, body(): lax.all_to_all(pieces.reshape(GROUP, both, width + 128), PARTICLE, 0, 0)  10.1 us
    ppermute x4, starting transfers between devices, swap_cores(): return lax.ppermute(value, 'c', [(0, 1), (1, 0)])  9.99 us
    ppermute x6, waiting for transfers between devices, others(): lax.ppermute(value, axis, [(i, (i + k) % size) for i in range(size)])  9.07 us
    all_to_all x1, starting transfers between devices, body(): mine = lax.all_to_all(picked, PARTICLE, 0, 0)  7.71 us
    ppermute x6, starting transfers between devices, others(): lax.ppermute(value, axis, [(i, (i + k) % size) for i in range(size)])  7.24 us
    ppermute x1, waiting for transfers between devices, body(): lax.ppermute(column, 'x', back)  4.17 us
  transfers between devices with their start and end apart: 16, of which 10 were waited for; matrix products, arithmetic and copies ran while one was open for 0% of the time, Pallas kernels for 13%

profile of v4, /device:TPU:71, one launch (start us, length us, event | category | flops | bytes accessed | tf_op | source)
XLA Modules:
  0.0 88.5 jit_solution(4696614385809612617)
XLA Ops:
  0.0 2.1 %spread.1 = bf16[16,2,8,896]{3,2,1,0:T(8,128)(2,1)} custom-call(s32[2]{0:T(128)} %ancestors.1, bf16[2,64,768]{2,1,0:T(8,128)(2,1)} %states.1, bf16[2,24,1536]{2,1,0:T(8,128)(2,1)} %w_in.1, bf16[24,1536]{1,0:T(8,128)(2,1)} %w_out.1), custom_call_target="tpu_custom_call" | custom-call | flops 1000000000 | tf_op jit(solution)/shard_map/spread/pallas_call | solution.py:304
  2.1 10.1 %all-to-all-start = ((bf16[32,8,896]{2,1,0:T(8,128)(2,1)}), bf16[32,8,896]{2,1,0:T(8,128)(2,1)S(1)}, u32[]{:S(2)}, u32[]{:S(2)}) async-start(bf16[32,8,896]{2,1,0:T(8,128)(2,1)} %bitcast.1), calls=%async_computation | async-start | bytes 917504 | tf_op jit(solution)/shard_map/all_to_all | solution.py:338
  12.2 1.3 %collective-permute-start.1 = (bf16[16,64,512]{2,1,0:T(8,128)(2,1)}, bf16[16,64,512]{2,1,0:T(8,128)(2,1)}, u32[]{:S(2)}, u32[]{:S(2)}) collective-permute-start(bf16[16,64,512]{2,1,0:T(8,128)(2,1)} %bias_own.1), channel_id=1, source_target_pairs={{0,1},{1,0},{2,3},{3,2},{4,5},{5,4},{6,7},{7,6},{8,9},{9,8},{10,11... | collective-permute-start | bytes 3145736 | tf_op jit(solution)/shard_map/ppermute | solution.py:289
  13.6 11.7 %all-to-all-done.pieces = bf16[32,8,896]{2,1,0:T(8,128)(2,1)S(1)} async-done(((bf16[32,8,896]{2,1,0:T(8,128)(2,1)}), bf16[32,8,896]{2,1,0:T(8,128)(2,1)S(1)}, u32[]{:S(2)}, u32[]{:S(2)}) %all-to-all-start) | async-done | bytes 458784 | tf_op jit(solution)/shard_map/all_to_all | solution.py:338
  25.3 1.1 %pick.1 = (bf16[32,8,384]{2,1,0:T(8,128)(2,1)}, bf16[288,384]{1,0:T(8,128)(2,1)S(1)}) custom-call(bf16[32,8,896]{2,1,0:T(8,128)(2,1)S(1)} %all-to-all-done.pieces), custom_call_target="tpu_custom_call" | custom-call | flops 1000000000 | tf_op jit(solution)/shard_map/pick/pallas_call | solution.py:304
  26.4 2.7 %collective-permute-start.5 = (bf16[288,384]{1,0:T(8,128)(2,1)S(1)}, bf16[288,384]{1,0:T(8,128)(2,1)S(1)}, u32[]{:S(2)}, u32[]{:S(2)}) collective-permute-start(bf16[288,384]{1,0:T(8,128)(2,1)S(1)} %get-tuple-element.27.w0), channel_id=1, source_target_pairs={{0,6},{2,0},{4,2},{6,4},{1,7},{3,1},{5,3},{7,5},{8,14},{10,8},{12,... | collective-permute-start | bytes 663560 | tf_op jit(solution)/shard_map/ppermute | solution.py:294
  29.1 0.4 collective-permute-start.4
  29.5 0.7 collective-permute-start.3
  30.1 7.7 %all-to-all-start.1 = ((bf16[32,8,384]{2,1,0:T(8,128)(2,1)}), bf16[32,8,384]{2,1,0:T(8,128)(2,1)}, u32[]{:S(2)}, u32[]{:S(2)}) async-start(bf16[32,8,384]{2,1,0:T(8,128)(2,1)} %get-tuple-element.24), calls=%async_computation.1 | async-start | bytes 393216 | tf_op jit(solution)/shard_map/all_to_all | solution.py:358
  37.9 0.0 copy-start.3
  37.9 0.0 collective-permute-done.5.w3
  37.9 0.0 collective-permute-done.4.w2
  37.9 4.2 %collective-permute-done.3.w1 = bf16[288,384]{1,0:T(8,128)(2,1)S(1)} collective-permute-done((bf16[288,384]{1,0:T(8,128)(2,1)S(1)}, bf16[288,384]{1,0:T(8,128)(2,1)S(1)}, u32[]{:S(2)}, u32[]{:S(2)}) %collective-permute-start.3) | collective-permute-done | bytes 221216 | tf_op jit(solution)/shard_map/ppermute | solution.py:294
  42.1 1.0 %column.1.here = bf16[2,288,768]{2,1,0:T(8,128)(2,1)} custom-call(bf16[288,384]{1,0:T(8,128)(2,1)S(1)} %get-tuple-element.27.w0, bf16[288,384]{1,0:T(8,128)(2,1)S(1)} %collective-permute-done.3.w1, bf16[288,384]{1,0:T(8,128)(2,1)S(1)} %collective-permute-done.4.w2, bf16[288,384]{1,0:T(8,128)(2,1)S(1)} %collective-permute-done.5.w3), custom_call_target="tpu_custom_call" | custom-call | flops 1000000000 | tf_op jit(solution)/shard_map/column/pallas_call | solution.py:304
  43.2 0.0 copy-start
  43.2 1.5 %collective-permute-start.7 = (bf16[2,288,768]{2,1,0:T(8,128)(2,1)}, bf16[2,288,768]{2,1,0:T(8,128)(2,1)}, u32[]{:S(2)}, u32[]{:S(2)}) collective-permute-start(bf16[2,288,768]{2,1,0:T(8,128)(2,1)} %column.1.here), channel_id=1, source_target_pairs={{0,192},{64,0},{128,64},{192,128},{1,193},{65,1},{129,65},{193,129... | collective-permute-start | bytes 2654216 | tf_op jit(solution)/shard_map/ppermute | solution.py:356
  44.6 1.2 %collective-permute-start.6 = (bf16[2,288,768]{2,1,0:T(8,128)(2,1)}, bf16[2,288,768]{2,1,0:T(8,128)(2,1)}, u32[]{:S(2)}, u32[]{:S(2)}) collective-permute-start(bf16[2,288,768]{2,1,0:T(8,128)(2,1)} %column.1.here), channel_id=1, source_target_pairs={{0,64},{64,128},{128,192},{192,0},{1,65},{65,129},{129,193},{193,1... | collective-permute-start | bytes 2654216 | tf_op jit(solution)/shard_map/ppermute | solution.py:356
  45.8 0.0 all-to-all-done.1.mine
  45.8 2.5 %collective-permute-start = (bf16[32,8,384]{2,1,0:T(8,128)(2,1)}, bf16[32,8,384]{2,1,0:T(8,128)(2,1)S(1)}, u32[]{:S(2)}, u32[]{:S(2)}) collective-permute-start(bf16[32,8,384]{2,1,0:T(8,128)(2,1)} %all-to-all-done.1.mine), channel_id=1, source_target_pairs={{0,1},{1,0},{2,3},{3,2},{4,5},{5,4},{6,7},{7,6},{8,9},{9,8},{10,11... | collective-permute-start | bytes 589832 | tf_op jit(solution)/shard_map/ppermute | solution.py:289
  48.3 0.0 collective-permute-done.1._bias.bias_other
  48.3 1.3 %collective-permute-done.theirs = bf16[32,8,384]{2,1,0:T(8,128)(2,1)S(1)} collective-permute-done((bf16[32,8,384]{2,1,0:T(8,128)(2,1)}, bf16[32,8,384]{2,1,0:T(8,128)(2,1)S(1)}, u32[]{:S(2)}, u32[]{:S(2)}) %collective-permute-start) | collective-permute-done | bytes 196640 | tf_op jit(solution)/shard_map/ppermute | solution.py:289
  49.6 0.0 copy-done.3
  49.6 1.2 %own.1 = (bf16[128,768]{1,0:T(8,128)(2,1)S(1)}, bf16[128,768]{1,0:T(8,128)(2,1)S(1)}) custom-call(bf16[32,8,384]{2,1,0:T(8,128)(2,1)} %all-to-all-done.1.mine, bf16[32,8,384]{2,1,0:T(8,128)(2,1)S(1)} %collective-permute-done.theirs, f32[768]{0:T(1024)S(1)} %copy-done.3, bf16[16,64,512]{2,1,0:T(8,128)(2,1)} %collective-permute-done.1._bias.bias_other), custom_call_target="tpu_custom_call" | custom-call | flops 1000000000 | tf_op jit(solution)/shard_map/own/pallas_call | solution.py:304
  50.8 2.1 %collective-permute-start.9 = (bf16[128,768]{1,0:T(8,128)(2,1)S(1)}, bf16[128,768]{1,0:T(8,128)(2,1)S(1)}, u32[]{:S(2)}, u32[]{:S(2)}) collective-permute-start(bf16[128,768]{1,0:T(8,128)(2,1)S(1)} %get-tuple-element.25.normed), channel_id=1, source_target_pairs={{0,6},{2,0},{4,2},{6,4},{1,7},{3,1},{5,3},{7,5},{8,14},{10,8},{12,... | collective-permute-start | bytes 589832 | tf_op jit(solution)/shard_map/ppermute | solution.py:294
  52.9 1.4 %collective-permute-start.8 = (bf16[128,768]{1,0:T(8,128)(2,1)S(1)}, bf16[128,768]{1,0:T(8,128)(2,1)S(1)}, u32[]{:S(2)}, u32[]{:S(2)}) collective-permute-start(bf16[128,768]{1,0:T(8,128)(2,1)S(1)} %get-tuple-element.25.normed), channel_id=1, source_target_pairs={{0,4},{2,6},{4,0},{6,2},{1,5},{3,7},{5,1},{7,3},{8,12},{10,14},{12... | collective-permute-start | bytes 589832 | tf_op jit(solution)/shard_map/ppermute | solution.py:294
  54.3 0.0 collective-permute-start.2
  54.3 0.0 copy-done
  54.3 0.6 project.1
  54.9 2.5 %collective-permute-done.9.normed = bf16[128,768]{1,0:T(8,128)(2,1)S(1)} collective-permute-done((bf16[128,768]{1,0:T(8,128)(2,1)S(1)}, bf16[128,768]{1,0:T(8,128)(2,1)S(1)}, u32[]{:S(2)}, u32[]{:S(2)}) %collective-permute-start.9) | collective-permute-done | bytes 196640 | tf_op jit(solution)/shard_map/ppermute | solution.py:294
  57.4 0.5 other.5
  57.9 2.3 %collective-permute-done.8.normed = bf16[128,768]{1,0:T(8,128)(2,1)S(1)} collective-permute-done((bf16[128,768]{1,0:T(8,128)(2,1)S(1)}, bf16[128,768]{1,0:T(8,128)(2,1)S(1)}, u32[]{:S(2)}, u32[]{:S(2)}) %collective-permute-start.8) | collective-permute-done | bytes 196640 | tf_op jit(solution)/shard_map/ppermute | solution.py:294
  60.2 0.5 other.3
  60.7 4.2 %collective-permute-done.7.right = bf16[2,288,768]{2,1,0:T(8,128)(2,1)} collective-permute-done((bf16[2,288,768]{2,1,0:T(8,128)(2,1)}, bf16[2,288,768]{2,1,0:T(8,128)(2,1)}, u32[]{:S(2)}, u32[]{:S(2)}) %collective-permute-start.7) | collective-permute-done | bytes 884768 | tf_op jit(solution)/shard_map/ppermute | solution.py:356
  64.9 0.2 collective-permute-done.6.left
  65.1 1.2 %halves.1 = (bf16[1,288,768]{2,1,0:T(8,128)(2,1)S(1)}, bf16[1,288,768]{2,1,0:T(8,128)(2,1)S(1)}) custom-call(bf16[2,288,768]{2,1,0:T(8,128)(2,1)} %collective-permute-done.6.left, bf16[2,288,768]{2,1,0:T(8,128)(2,1)} %collective-permute-done.7.right, bf16[128,768]{1,0:T(8,128)(2,1)S(1)} %get-tuple-element.28._after.k2), custom_call_target="tpu_custom_call" | custom-call | flops 1000000000 | tf_op jit(solution)/shard_map/halves/pallas_call | solution.py:304
  66.2 2.2 %collective-permute-start.11 = (bf16[1,288,768]{2,1,0:T(8,128)(2,1)S(1)}, bf16[1,288,768]{2,1,0:T(8,128)(2,1)S(1)}, u32[]{:S(2)}, u32[]{:S(2)}) collective-permute-start(bf16[1,288,768]{2,1,0:T(8,128)(2,1)S(1)} %get-tuple-element.29.refs_0_._left), channel_id=1, source_target_pairs={{0,64},{64,128},{128,192},{192,0},{1,65},{65,129},{129,193},{193,1... | collective-permute-start | bytes 1327112 | tf_op jit(solution)/shard_map/ppermute | solution.py:391
  68.4 0.0 copy-start.2
  68.4 0.0 copy-start.4
  68.4 0.0 copy-start.5
  68.4 0.0 copy-start.6
  68.4 0.3 collective-permute-start.12
  68.7 0.0 collective-permute-done.2.normed
  68.7 0.5 other.4
  69.2 0.5 copy-done.2
  69.7 0.0 copy-done.4
  69.7 0.0 copy-done.5
  69.7 0.4 copy-done.6
  70.1 0.0 copy-start.1
  70.1 4.8 %attention.1 = (f32[128,768]{1,0:T(8,128)S(1)}, bf16[128,768]{1,0:T(8,128)(2,1)S(1)}) custom-call(bf16[128,768]{1,0:T(8,128)(2,1)S(1)} %get-tuple-element.26.k0, bf16[128,768]{1,0:T(8,128)(2,1)S(1)} %get-tuple-element.31.k1, bf16[128,768]{1,0:T(8,128)(2,1)S(1)} %get-tuple-element.28._after.k2, bf16[128,768]{1,0:T(8,128)(2,1)S(1)} %get-tuple-element.32.k3, ...), custom_call_target="tpu_custom_call" | custom-call | flops 4000000000 | tf_op jit(solution)/shard_map/attention/pallas_call | solution.py:304
  74.9 2.6 %collective-permute-start.10 = (bf16[128,768]{1,0:T(8,128)(2,1)S(1)}, bf16[128,768]{1,0:T(8,128)(2,1)S(1)}, u32[]{:S(2)}, u32[]{:S(2)}) collective-permute-start(bf16[128,768]{1,0:T(8,128)(2,1)S(1)} %get-tuple-element.39.own), channel_id=1, source_target_pairs={{0,1},{1,0},{2,3},{3,2},{4,5},{5,4},{6,7},{7,6},{8,9},{9,8},{10,11... | collective-permute-start | bytes 589832 | tf_op jit(solution)/shard_map/ppermute | solution.py:289
  77.5 1.1 %collective-permute-done.10.other = bf16[128,768]{1,0:T(8,128)(2,1)S(1)} collective-permute-done((bf16[128,768]{1,0:T(8,128)(2,1)S(1)}, bf16[128,768]{1,0:T(8,128)(2,1)S(1)}, u32[]{:S(2)}, u32[]{:S(2)}) %collective-permute-start.10) | collective-permute-done | bytes 196640 | tf_op jit(solution)/shard_map/ppermute | solution.py:289
  78.6 0.0 collective-permute-done.11.far_0
  78.6 0.4 collective-permute-done.12.far_1
  79.0 0.0 copy-done.1
  79.0 3.8 %transition.1 = (f32[2,64,768]{2,1,0:T(8,128)S(1)}, f32[2,64,768]{2,1,0:T(8,128)S(1)}) custom-call(bf16[128,768]{1,0:T(8,128)(2,1)S(1)} %get-tuple-element.39.own, bf16[128,768]{1,0:T(8,128)(2,1)S(1)} %collective-permute-done.10.other, f32[128,768]{1,0:T(8,128)S(1)} %get-tuple-element.40.stream, bf16[768,768]{1,0:T(8,128)(2,1)S(1)} %copy-done.1, ...), custom_call_target="tpu_custom_call" | custom-call | flops 1000000000 | tf_op jit(solution)/shard_map/transition/pallas_call | solution.py:304
  82.8 3.5 %collective-permute-start.13 = (f32[2,64,768]{2,1,0:T(8,128)S(1)}, f32[2,64,768]{2,1,0:T(8,128)S(1)}, u32[]{:S(2)}, u32[]{:S(2)}) collective-permute-start(f32[2,64,768]{2,1,0:T(8,128)S(1)} %get-tuple-element.42), channel_id=1, source_target_pairs={{0,1},{1,0},{2,3},{3,2},{4,5},{5,4},{6,7},{7,6},{8,9},{9,8},{10,11... | collective-permute-start | bytes 1179656 | tf_op jit(solution)/shard_map/ppermute | solution.py:289
  86.4 1.3 %collective-permute-done.13 = f32[2,64,768]{2,1,0:T(8,128)S(1)} collective-permute-done((f32[2,64,768]{2,1,0:T(8,128)S(1)}, f32[2,64,768]{2,1,0:T(8,128)S(1)}, u32[]{:S(2)}, u32[]{:S(2)}) %collective-permute-start.13) | collective-permute-done | bytes 393248 | tf_op jit(solution)/shard_map/ppermute | solution.py:289
  87.7 0.7 add_convert_fusion
Async XLA Ops:
  2.1 23.2 %all-to-all-start = ((bf16[32,8,896]{2,1,0:T(8,128)(2,1)}), bf16[32,8,896]{2,1,0:T(8,128)(2,1)S(1)}, u32[]{:S(2)}, u32[]{:S(2)}) async-start(bf16[32,8,896]{2,1,0:T(8,128)(2,1)} %bitcast.1), calls=%async_computation | async-start | bytes 917504 | tf_op jit(solution)/shard_map/all_to_all | solution.py:338
  12.2 36.1 %collective-permute-start.1 = (bf16[16,64,512]{2,1,0:T(8,128)(2,1)}, bf16[16,64,512]{2,1,0:T(8,128)(2,1)}, u32[]{:S(2)}, u32[]{:S(2)}) collective-permute-start(bf16[16,64,512]{2,1,0:T(8,128)(2,1)} %bias_own.1), channel_id=1, source_target_pairs={{0,1},{1,0},{2,3},{3,2},{4,5},{5,4},{6,7},{7,6},{8,9},{9,8},{10,11... | collective-permute-start | bytes 3145736 | tf_op jit(solution)/shard_map/ppermute | solution.py:289
  26.4 11.5 %collective-permute-start.5 = (bf16[288,384]{1,0:T(8,128)(2,1)S(1)}, bf16[288,384]{1,0:T(8,128)(2,1)S(1)}, u32[]{:S(2)}, u32[]{:S(2)}) collective-permute-start(bf16[288,384]{1,0:T(8,128)(2,1)S(1)} %get-tuple-element.27.w0), channel_id=1, source_target_pairs={{0,6},{2,0},{4,2},{6,4},{1,7},{3,1},{5,3},{7,5},{8,14},{10,8},{12,... | collective-permute-start | bytes 663560 | tf_op jit(solution)/shard_map/ppermute | solution.py:294
  29.1 8.8 %collective-permute-start.4 = (bf16[288,384]{1,0:T(8,128)(2,1)S(1)}, bf16[288,384]{1,0:T(8,128)(2,1)S(1)}, u32[]{:S(2)}, u32[]{:S(2)}) collective-permute-start(bf16[288,384]{1,0:T(8,128)(2,1)S(1)} %get-tuple-element.27.w0), channel_id=1, source_target_pairs={{0,4},{2,6},{4,0},{6,2},{1,5},{3,7},{5,1},{7,3},{8,12},{10,14},{12... | collective-permute-start | bytes 663560 | tf_op jit(solution)/shard_map/ppermute | solution.py:294
  29.5 12.7 %collective-permute-start.3 = (bf16[288,384]{1,0:T(8,128)(2,1)S(1)}, bf16[288,384]{1,0:T(8,128)(2,1)S(1)}, u32[]{:S(2)}, u32[]{:S(2)}) collective-permute-start(bf16[288,384]{1,0:T(8,128)(2,1)S(1)} %get-tuple-element.27.w0), channel_id=1, source_target_pairs={{0,2},{2,4},{4,6},{6,0},{1,3},{3,5},{5,7},{7,1},{8,10},{10,12},{12... | collective-permute-start | bytes 663560 | tf_op jit(solution)/shard_map/ppermute | solution.py:294
  30.1 15.7 %all-to-all-start.1 = ((bf16[32,8,384]{2,1,0:T(8,128)(2,1)}), bf16[32,8,384]{2,1,0:T(8,128)(2,1)}, u32[]{:S(2)}, u32[]{:S(2)}) async-start(bf16[32,8,384]{2,1,0:T(8,128)(2,1)} %get-tuple-element.24), calls=%async_computation.1 | async-start | bytes 393216 | tf_op jit(solution)/shard_map/all_to_all | solution.py:358
  37.9 11.7 %copy-start.3 = (f32[768]{0:T(1024)S(1)}, f32[768]{0:T(1024)}, u32[]{:S(2)}) copy-start(f32[768]{0:T(1024)} %gain.1) | copy-start | bytes 9220
  43.2 11.2 %copy-start = (bf16[768,2304]{1,0:T(8,128)(2,1)S(1)}, bf16[768,2304]{1,0:T(8,128)(2,1)}, u32[]{:S(2)}) copy-start(bf16[768,2304]{1,0:T(8,128)(2,1)} %w_qkv.7) | copy-start | bytes 10616836
  43.2 21.7 %collective-permute-start.7 = (bf16[2,288,768]{2,1,0:T(8,128)(2,1)}, bf16[2,288,768]{2,1,0:T(8,128)(2,1)}, u32[]{:S(2)}, u32[]{:S(2)}) collective-permute-start(bf16[2,288,768]{2,1,0:T(8,128)(2,1)} %column.1.here), channel_id=1, source_target_pairs={{0,192},{64,0},{128,64},{192,128},{1,193},{65,1},{129,65},{193,129... | collective-permute-start | bytes 2654216 | tf_op jit(solution)/shard_map/ppermute | solution.py:356
  44.6 20.4 %collective-permute-start.6 = (bf16[2,288,768]{2,1,0:T(8,128)(2,1)}, bf16[2,288,768]{2,1,0:T(8,128)(2,1)}, u32[]{:S(2)}, u32[]{:S(2)}) collective-permute-start(bf16[2,288,768]{2,1,0:T(8,128)(2,1)} %column.1.here), channel_id=1, source_target_pairs={{0,64},{64,128},{128,192},{192,0},{1,65},{65,129},{129,193},{193,1... | collective-permute-start | bytes 2654216 | tf_op jit(solution)/shard_map/ppermute | solution.py:356
  45.8 3.8 %collective-permute-start = (bf16[32,8,384]{2,1,0:T(8,128)(2,1)}, bf16[32,8,384]{2,1,0:T(8,128)(2,1)S(1)}, u32[]{:S(2)}, u32[]{:S(2)}) collective-permute-start(bf16[32,8,384]{2,1,0:T(8,128)(2,1)} %all-to-all-done.1.mine), channel_id=1, source_target_pairs={{0,1},{1,0},{2,3},{3,2},{4,5},{5,4},{6,7},{7,6},{8,9},{9,8},{10,11... | collective-permute-start | bytes 589832 | tf_op jit(solution)/shard_map/ppermute | solution.py:289
  50.8 6.6 %collective-permute-start.9 = (bf16[128,768]{1,0:T(8,128)(2,1)S(1)}, bf16[128,768]{1,0:T(8,128)(2,1)S(1)}, u32[]{:S(2)}, u32[]{:S(2)}) collective-permute-start(bf16[128,768]{1,0:T(8,128)(2,1)S(1)} %get-tuple-element.25.normed), channel_id=1, source_target_pairs={{0,6},{2,0},{4,2},{6,4},{1,7},{3,1},{5,3},{7,5},{8,14},{10,8},{12,... | collective-permute-start | bytes 589832 | tf_op jit(solution)/shard_map/ppermute | solution.py:294
  52.9 7.3 %collective-permute-start.8 = (bf16[128,768]{1,0:T(8,128)(2,1)S(1)}, bf16[128,768]{1,0:T(8,128)(2,1)S(1)}, u32[]{:S(2)}, u32[]{:S(2)}) collective-permute-start(bf16[128,768]{1,0:T(8,128)(2,1)S(1)} %get-tuple-element.25.normed), channel_id=1, source_target_pairs={{0,4},{2,6},{4,0},{6,2},{1,5},{3,7},{5,1},{7,3},{8,12},{10,14},{12... | collective-permute-start | bytes 589832 | tf_op jit(solution)/shard_map/ppermute | solution.py:294
  54.3 14.4 %collective-permute-start.2 = (bf16[128,768]{1,0:T(8,128)(2,1)S(1)}, bf16[128,768]{1,0:T(8,128)(2,1)S(1)}, u32[]{:S(2)}, u32[]{:S(2)}) collective-permute-start(bf16[128,768]{1,0:T(8,128)(2,1)S(1)} %get-tuple-element.25.normed), channel_id=1, source_target_pairs={{0,2},{2,4},{4,6},{6,0},{1,3},{3,5},{5,7},{7,1},{8,10},{10,12},{12... | collective-permute-start | bytes 589832 | tf_op jit(solution)/shard_map/ppermute | solution.py:294
  66.2 12.4 %collective-permute-start.11 = (bf16[1,288,768]{2,1,0:T(8,128)(2,1)S(1)}, bf16[1,288,768]{2,1,0:T(8,128)(2,1)S(1)}, u32[]{:S(2)}, u32[]{:S(2)}) collective-permute-start(bf16[1,288,768]{2,1,0:T(8,128)(2,1)S(1)} %get-tuple-element.29.refs_0_._left), channel_id=1, source_target_pairs={{0,64},{64,128},{128,192},{192,0},{1,65},{65,129},{129,193},{193,1... | collective-permute-start | bytes 1327112 | tf_op jit(solution)/shard_map/ppermute | solution.py:391
  68.4 1.3 %copy-start.2 = (bf16[768,768]{1,0:T(8,128)(2,1)S(1)}, bf16[768,768]{1,0:T(8,128)(2,1)}, u32[]{:S(2)}) copy-start(bf16[768,768]{1,0:T(8,128)(2,1)} %w_o.1) | copy-start | bytes 3538948
  68.4 1.3 %copy-start.4 = (f32[768]{0:T(1024)S(1)}, f32[768]{0:T(1024)}, u32[]{:S(2)}) copy-start(f32[768]{0:T(1024)} %gain_ff.1) | copy-start | bytes 9220
  68.4 1.3 %copy-start.5 = (s32[512]{0:T(512)S(1)}, s32[512]{0:T(512)}, u32[]{:S(2)}) copy-start(s32[512]{0:T(512)} %mask.1) | copy-start | bytes 6148
  68.4 1.7 %copy-start.6 = (bf16[768,768]{1,0:T(8,128)(2,1)S(1)}, bf16[768,768]{1,0:T(8,128)(2,1)}, u32[]{:S(2)}) copy-start(bf16[768,768]{1,0:T(8,128)(2,1)} %constant.4.clone.order) | copy-start | bytes 3538948
  68.4 10.6 %collective-permute-start.12 = (bf16[1,288,768]{2,1,0:T(8,128)(2,1)S(1)}, bf16[1,288,768]{2,1,0:T(8,128)(2,1)S(1)}, u32[]{:S(2)}, u32[]{:S(2)}) collective-permute-start(bf16[1,288,768]{2,1,0:T(8,128)(2,1)S(1)} %get-tuple-element.30.refs_1_._right), channel_id=1, source_target_pairs={{0,192},{64,0},{128,64},{192,128},{1,193},{65,1},{129,65},{193,129... | collective-permute-start | bytes 1327112 | tf_op jit(solution)/shard_map/ppermute | solution.py:391
  70.1 8.9 %copy-start.1 = (bf16[768,768]{1,0:T(8,128)(2,1)S(1)}, bf16[768,768]{1,0:T(8,128)(2,1)}, u32[]{:S(2)}) copy-start(bf16[768,768]{1,0:T(8,128)(2,1)} %constant.5.clone.order) | copy-start | bytes 3538948
  74.9 3.7 %collective-permute-start.10 = (bf16[128,768]{1,0:T(8,128)(2,1)S(1)}, bf16[128,768]{1,0:T(8,128)(2,1)S(1)}, u32[]{:S(2)}, u32[]{:S(2)}) collective-permute-start(bf16[128,768]{1,0:T(8,128)(2,1)S(1)} %get-tuple-element.39.own), channel_id=1, source_target_pairs={{0,1},{1,0},{2,3},{3,2},{4,5},{5,4},{6,7},{7,6},{8,9},{9,8},{10,11... | collective-permute-start | bytes 589832 | tf_op jit(solution)/shard_map/ppermute | solution.py:289
  82.8 4.9 %collective-permute-start.13 = (f32[2,64,768]{2,1,0:T(8,128)S(1)}, f32[2,64,768]{2,1,0:T(8,128)S(1)}, u32[]{:S(2)}, u32[]{:S(2)}) collective-permute-start(f32[2,64,768]{2,1,0:T(8,128)S(1)} %get-tuple-element.42), channel_id=1, source_target_pairs={{0,1},{1,0},{2,3},{3,2},{4,5},{5,4},{6,7},{7,6},{8,9},{9,8},{10,11... | collective-permute-start | bytes 1179656 | tf_op jit(solution)/shard_map/ppermute | solution.py:289

commit v5 on v4

--- a/solution.py
+++ b/solution.py
@@ -36,13 +36,10 @@
     return jnp.dot(onehot.astype(jnp.bfloat16), values, preferred_element_type=jnp.float32)
 
 
-def weight_orders(width):
+def input_order(width):
     depth = width // GROUP
     tile, source, row = np.meshgrid(np.arange(3), np.arange(GROUP), np.arange(TILE), indexing="ij")
-    inputs = (source * depth + tile * TILE + row).reshape(-1)
-    outputs = np.concatenate([inputs[: 2 * GROUP * TILE], inputs[2 * GROUP * TILE :].reshape(GROUP, TILE).T.reshape(-1)])
-    eye = np.eye(width, dtype=jnp.bfloat16)
-    return eye[:, inputs], eye[outputs]
+    return np.eye(width, dtype=jnp.bfloat16)[:, (source * depth + tile * TILE + row).reshape(-1)]
 
 
 def spread_kernel(ancestors, states, w_in, w_out, out_ref, local):
@@ -174,7 +171,7 @@
     row_count, width = queries.shape
     half = row_count // 2
     head_size = width // HEADS
-    together = 4
+    together = 8
     loads = []
     for i in range(HEADS // together):
         part = pl.ds(i * together, together)
@@ -235,53 +232,41 @@
 
 
 def transition_kernel(
-    own, other, stream, order, here, left, right, far_0, far_1, keep_ref, send_ref,
-    tiles, extras, arrived,
+    own, other, stream, here, left, right, far_0, far_1, keep_ref, send_ref, weights, extras, arrived
 ):
     c, x = lax.axis_index("c"), lax.axis_index("x")
     half = own.shape[0] // 2
     width = own.shape[1]
-    count = tiles.shape[1]
-    far = lax.rem(x + 2, NX) * 2
-    parts = [
-        (here, pl.ds(x * 2, 2)),
-        (left, pl.ds(lax.rem(x + 3, NX) * 2, 2)),
-        (right, pl.ds(lax.rem(x + 1, NX) * 2, 2)),
-        (far_0, pl.ds(far, 1)),
-        (far_1, pl.ds(far + 1, 1)),
-    ]
+    parts = [(block.at[i], across, i) for block, across in ((here, 0), (left, 3), (right, 1)) for i in range(2)]
+    parts += [(far_0.at[0], 2, 0), (far_1.at[0], 2, 1)]
     copies = []
-    for k, (block, at) in enumerate(parts):
-        copies.append(pltpu.make_async_copy(block.at[:, :count], tiles.at[at], arrived.at[2 * k]))
-        copies.append(pltpu.make_async_copy(block.at[:, count:], extras.at[at], arrived.at[2 * k + 1]))
+    for k, (part, across, i) in enumerate(parts):
+        e = lax.rem(x + across, NX) * 2 + i
+        copies.append(pltpu.make_async_copy(part.at[:GROUP], weights.at[e], arrived.at[2 * k]))
+        copies.append(pltpu.make_async_copy(part.at[GROUP:], extras.at[e], arrived.at[2 * k + 1]))
     for copy in copies:
         copy.start()
     rows = jnp.concatenate([own[...], other[...]], axis=0)
     for copy in copies:
         copy.wait()
-    gate = jnp.dot(rows, tiles[0:3].reshape(width, width), preferred_element_type=jnp.float32)
-    up = jnp.dot(rows, tiles[3:6].reshape(width, width), preferred_element_type=jnp.float32)
+
+    def plain(tiles):
+        return tiles.astype(jnp.float32).reshape(-1, width).astype(jnp.bfloat16)
+
+    gate = jnp.dot(rows, weights[0:3].reshape(width, width), preferred_element_type=jnp.float32)
+    up = jnp.dot(rows, weights[3:6].reshape(width, width), preferred_element_type=jnp.float32)
+    out_row, in_row = iotas((GROUP * TILE, GROUP * TILE))
+    onehot = in_row == out_row % TILE * GROUP + out_row // TILE
+    last = reorder(onehot, plain(extras[...])).reshape(GROUP, 1, TILE, width)
+    first = [weights[e].astype(jnp.float32).reshape(GROUP, 1, TILE, width) for e in (6, 7)]
+    down = jnp.concatenate([*first, last], axis=1).reshape(width, width).astype(jnp.bfloat16)
     hidden = (gate / (1.0 + jnp.exp(-gate)) * up).astype(jnp.bfloat16)
-    across = (((1,), (1,)), ((), ()))
-    update = jnp.concatenate(
-        [
-            lax.dot_general(
-                hidden, tiles[6:8].reshape(2 * count, width), across, preferred_element_type=jnp.float32
-            ),
-            lax.dot_general(
-                hidden, extras[...].reshape(-1, width), across, preferred_element_type=jnp.float32
-            ),
-        ],
-        axis=1,
-    )
-    high = update.astype(jnp.bfloat16)
-    low = (update - high.astype(jnp.float32)).astype(jnp.bfloat16)
-    update = jnp.dot(high, order[...], preferred_element_type=jnp.float32) + jnp.dot(
-        low, order[...], preferred_element_type=jnp.float32
+    update = lax.dot_general(
+        hidden, down, (((1,), (1,)), ((), ())), preferred_element_type=jnp.float32
     )
     keep_ref[c] = update[:half] + stream[:half]
-    send_ref[c] = update[half : 2 * half] + stream[half:]
-    send_ref[1 - c] = update[2 * half : 3 * half]
+    send_ref[c] = (update[half : 2 * half] + stream[half:]).astype(jnp.bfloat16)
+    send_ref[1 - c] = update[2 * half : 3 * half].astype(jnp.bfloat16)
     keep_ref[1 - c] = update[3 * half :]
 
 
@@ -323,7 +308,7 @@
     both = 2 * PIECE
     depth = w_out.shape[0]
     bf16, f32 = jnp.bfloat16, jnp.float32
-    order_in, order_out = weight_orders(width)
+    order_in = input_order(width)
 
     bias_other = swap_cores(pair_bias)
     (pieces,) = kernel(
@@ -407,20 +392,23 @@
             pltpu.VMEM((HEADS, rows, rows * NY), bf16),
             pltpu.VMEM((width, width), bf16),
             pltpu.VMEM((width, width), bf16),
-            pltpu.SemaphoreType.DMA((10,)),
+            pltpu.SemaphoreType.DMA((6,)),
         ],
     )
     keep, send = kernel(
         transition_kernel,
         "transition",
-        [None] * 4 + [ANY] * 5,
-        (normed_ff, swap_cores(normed_ff), stream, order_out, column, left, right, *far),
-        [((part_count, block_rows, width), f32)] * 2,
+        [None] * 3 + [ANY] * 5,
+        (
+            normed_ff, swap_cores(normed_ff), stream,
+            *(w.reshape(w.shape[0], -1, TILE, width) for w in (column, left, right, *far)),
+        ),
+        [((part_count, block_rows, width), t) for t in (f32, bf16)],
         limit=16,
         scratch=[
-            pltpu.VMEM((TILES, GROUP * TILE, width), bf16),
-            pltpu.VMEM((TILES, GROUP, width), bf16),
-            pltpu.SemaphoreType.DMA((10,)),
+            pltpu.VMEM((TILES, GROUP, TILE, width), bf16),
+            pltpu.VMEM((TILES, GROUP // TILE, TILE, width), bf16),
+            pltpu.SemaphoreType.DMA((16,)),
         ],
     )
     return (keep + swap_cores(send)).astype(bf16)

time: 88.8 us -> 88 us (level)
  Pallas kernels: 17.3 us -> 16.3 us
    pallas_call x11, Pallas kernels: 17.3 us -> 16.3 us  [kernel(): pl.pallas_call(f, grid=(1,), out_shape=outs, in_specs=specs, out_specs=tu...]
where the time goes in v5:
time: 88 us; the launch traced here: 87.6 us
  starting transfers between devices  40.2 us (46%)
  waiting for transfers between devices  29.4 us (33%)
  Pallas kernels  16.3 us (19%)
  local copies, waits for them, and re-layouts  0.89 us (1%)
    pallas_call x11, Pallas kernels, kernel(): pl.pallas_call(f, grid=(1,), out_shape=outs, in_specs=specs, out_specs=tu...  16.3 us
    all_to_all x1, waiting for transfers between devices, body(): lax.all_to_all(pieces.reshape(GROUP, both, width + 128), PARTICLE, 0, 0)  11.7 us
    all_to_all x1, starting transfers between devices, body(): lax.all_to_all(pieces.reshape(GROUP, both, width + 128), PARTICLE, 0, 0)  10.1 us
    ppermute x4, starting transfers between devices, swap_cores(): return lax.ppermute(value, 'c', [(0, 1), (1, 0)])  9.96 us
    ppermute x6, waiting for transfers between devices, others(): lax.ppermute(value, axis, [(i, (i + k) % size) for i in range(size)])  9.05 us
    all_to_all x1, starting transfers between devices, body(): mine = lax.all_to_all(picked, PARTICLE, 0, 0)  7.71 us
    ppermute x6, starting transfers between devices, others(): lax.ppermute(value, axis, [(i, (i + k) % size) for i in range(size)])  7.25 us
    ppermute x1, waiting for transfers between devices, body(): lax.ppermute(column, 'x', back)  4.18 us
  transfers between devices with their start and end apart: 16, of which 10 were waited for; matrix products, arithmetic and copies ran while one was open for 0% of the time, Pallas kernels for 13%

profile of v5, /device:TPU:71, one launch (start us, length us, event | category | flops | bytes accessed | tf_op | source)
XLA Modules:
  0.0 87.6 jit_solution(8060246700706867416)
XLA Ops:
  0.0 2.1 %spread.1 = bf16[16,2,8,896]{3,2,1,0:T(8,128)(2,1)} custom-call(s32[2]{0:T(128)} %ancestors.1, bf16[2,64,768]{2,1,0:T(8,128)(2,1)} %states.1, bf16[2,24,1536]{2,1,0:T(8,128)(2,1)} %w_in.1, bf16[24,1536]{1,0:T(8,128)(2,1)} %w_out.1), custom_call_target="tpu_custom_call" | custom-call | flops 1000000000 | tf_op jit(solution)/shard_map/spread/pallas_call | solution.py:289
  2.1 10.1 %all-to-all-start = ((bf16[32,8,896]{2,1,0:T(8,128)(2,1)}), bf16[32,8,896]{2,1,0:T(8,128)(2,1)S(1)}, u32[]{:S(2)}, u32[]{:S(2)}) async-start(bf16[32,8,896]{2,1,0:T(8,128)(2,1)} %bitcast.8), calls=%async_computation | async-start | bytes 917504 | tf_op jit(solution)/shard_map/all_to_all | solution.py:323
  12.2 1.3 %collective-permute-start.1 = (bf16[16,64,512]{2,1,0:T(8,128)(2,1)}, bf16[16,64,512]{2,1,0:T(8,128)(2,1)}, u32[]{:S(2)}, u32[]{:S(2)}) collective-permute-start(bf16[16,64,512]{2,1,0:T(8,128)(2,1)} %bias_own.1), channel_id=1, source_target_pairs={{0,1},{1,0},{2,3},{3,2},{4,5},{5,4},{6,7},{7,6},{8,9},{9,8},{10,11... | collective-permute-start | bytes 3145736 | tf_op jit(solution)/shard_map/ppermute | solution.py:274
  13.5 11.7 %all-to-all-done.pieces = bf16[32,8,896]{2,1,0:T(8,128)(2,1)S(1)} async-done(((bf16[32,8,896]{2,1,0:T(8,128)(2,1)}), bf16[32,8,896]{2,1,0:T(8,128)(2,1)S(1)}, u32[]{:S(2)}, u32[]{:S(2)}) %all-to-all-start) | async-done | bytes 458784 | tf_op jit(solution)/shard_map/all_to_all | solution.py:323
  25.3 1.1 %pick.1 = (bf16[32,8,384]{2,1,0:T(8,128)(2,1)}, bf16[288,384]{1,0:T(8,128)(2,1)S(1)}) custom-call(bf16[32,8,896]{2,1,0:T(8,128)(2,1)S(1)} %all-to-all-done.pieces), custom_call_target="tpu_custom_call" | custom-call | flops 1000000000 | tf_op jit(solution)/shard_map/pick/pallas_call | solution.py:289
  26.4 2.7 %collective-permute-start.5 = (bf16[288,384]{1,0:T(8,128)(2,1)S(1)}, bf16[288,384]{1,0:T(8,128)(2,1)S(1)}, u32[]{:S(2)}, u32[]{:S(2)}) collective-permute-start(bf16[288,384]{1,0:T(8,128)(2,1)S(1)} %get-tuple-element.27.w0), channel_id=1, source_target_pairs={{0,6},{2,0},{4,2},{6,4},{1,7},{3,1},{5,3},{7,5},{8,14},{10,8},{12,... | collective-permute-start | bytes 663560 | tf_op jit(solution)/shard_map/ppermute | solution.py:279
  29.1 0.4 collective-permute-start.4
  29.4 0.7 collective-permute-start.3
  30.1 7.7 %all-to-all-start.1 = ((bf16[32,8,384]{2,1,0:T(8,128)(2,1)}), bf16[32,8,384]{2,1,0:T(8,128)(2,1)}, u32[]{:S(2)}, u32[]{:S(2)}) async-start(bf16[32,8,384]{2,1,0:T(8,128)(2,1)} %get-tuple-element.24), calls=%async_computation.1 | async-start | bytes 393216 | tf_op jit(solution)/shard_map/all_to_all | solution.py:343
  37.8 0.0 copy-start.2
  37.9 0.0 collective-permute-done.5.w3
  37.9 0.0 collective-permute-done.4.w2
  37.9 4.2 %collective-permute-done.3.w1 = bf16[288,384]{1,0:T(8,128)(2,1)S(1)} collective-permute-done((bf16[288,384]{1,0:T(8,128)(2,1)S(1)}, bf16[288,384]{1,0:T(8,128)(2,1)S(1)}, u32[]{:S(2)}, u32[]{:S(2)}) %collective-permute-start.3) | collective-permute-done | bytes 221216 | tf_op jit(solution)/shard_map/ppermute | solution.py:279
  42.1 1.0 %column.1 = bf16[2,288,768]{2,1,0:T(8,128)(2,1)} custom-call(bf16[288,384]{1,0:T(8,128)(2,1)S(1)} %get-tuple-element.27.w0, bf16[288,384]{1,0:T(8,128)(2,1)S(1)} %collective-permute-done.3.w1, bf16[288,384]{1,0:T(8,128)(2,1)S(1)} %collective-permute-done.4.w2, bf16[288,384]{1,0:T(8,128)(2,1)S(1)} %collective-permute-done.5.w3), custom_call_target="tpu_custom_call" | custom-call | flops 1000000000 | tf_op jit(solution)/shard_map/column/pallas_call | solution.py:289
  43.1 0.0 copy-start
  43.1 1.5 %collective-permute-start.7 = (bf16[2,288,768]{2,1,0:T(8,128)(2,1)}, bf16[2,288,768]{2,1,0:T(8,128)(2,1)}, u32[]{:S(2)}, u32[]{:S(2)}) collective-permute-start(bf16[2,288,768]{2,1,0:T(8,128)(2,1)} %column.1), channel_id=1, source_target_pairs={{0,192},{64,0},{128,64},{192,128},{1,193},{65,1},{129,65},{193,129... | collective-permute-start | bytes 2654216 | tf_op jit(solution)/shard_map/ppermute | solution.py:341
  44.6 1.2 %collective-permute-start.6 = (bf16[2,288,768]{2,1,0:T(8,128)(2,1)}, bf16[2,288,768]{2,1,0:T(8,128)(2,1)}, u32[]{:S(2)}, u32[]{:S(2)}) collective-permute-start(bf16[2,288,768]{2,1,0:T(8,128)(2,1)} %column.1), channel_id=1, source_target_pairs={{0,64},{64,128},{128,192},{192,0},{1,65},{65,129},{129,193},{193,1... | collective-permute-start | bytes 2654216 | tf_op jit(solution)/shard_map/ppermute | solution.py:341
  45.8 0.0 all-to-all-done.1.mine
  45.8 2.5 %collective-permute-start = (bf16[32,8,384]{2,1,0:T(8,128)(2,1)}, bf16[32,8,384]{2,1,0:T(8,128)(2,1)S(1)}, u32[]{:S(2)}, u32[]{:S(2)}) collective-permute-start(bf16[32,8,384]{2,1,0:T(8,128)(2,1)} %all-to-all-done.1.mine), channel_id=1, source_target_pairs={{0,1},{1,0},{2,3},{3,2},{4,5},{5,4},{6,7},{7,6},{8,9},{9,8},{10,11... | collective-permute-start | bytes 589832 | tf_op jit(solution)/shard_map/ppermute | solution.py:274
  48.3 0.0 collective-permute-done.1._bias.bias_other
  48.3 1.3 %collective-permute-done.theirs = bf16[32,8,384]{2,1,0:T(8,128)(2,1)S(1)} collective-permute-done((bf16[32,8,384]{2,1,0:T(8,128)(2,1)}, bf16[32,8,384]{2,1,0:T(8,128)(2,1)S(1)}, u32[]{:S(2)}, u32[]{:S(2)}) %collective-permute-start) | collective-permute-done | bytes 196640 | tf_op jit(solution)/shard_map/ppermute | solution.py:274
  49.6 0.0 copy-done.2
  49.6 1.2 %own.1 = (bf16[128,768]{1,0:T(8,128)(2,1)S(1)}, bf16[128,768]{1,0:T(8,128)(2,1)S(1)}) custom-call(bf16[32,8,384]{2,1,0:T(8,128)(2,1)} %all-to-all-done.1.mine, bf16[32,8,384]{2,1,0:T(8,128)(2,1)S(1)} %collective-permute-done.theirs, f32[768]{0:T(1024)S(1)} %copy-done.2, bf16[16,64,512]{2,1,0:T(8,128)(2,1)} %collective-permute-done.1._bias.bias_other), custom_call_target="tpu_custom_call" | custom-call | flops 1000000000 | tf_op jit(solution)/shard_map/own/pallas_call | solution.py:289
  50.8 2.1 %collective-permute-start.9 = (bf16[128,768]{1,0:T(8,128)(2,1)S(1)}, bf16[128,768]{1,0:T(8,128)(2,1)S(1)}, u32[]{:S(2)}, u32[]{:S(2)}) collective-permute-start(bf16[128,768]{1,0:T(8,128)(2,1)S(1)} %get-tuple-element.25.normed), channel_id=1, source_target_pairs={{0,6},{2,0},{4,2},{6,4},{1,7},{3,1},{5,3},{7,5},{8,14},{10,8},{12,... | collective-permute-start | bytes 589832 | tf_op jit(solution)/shard_map/ppermute | solution.py:279
  52.9 1.4 %collective-permute-start.8 = (bf16[128,768]{1,0:T(8,128)(2,1)S(1)}, bf16[128,768]{1,0:T(8,128)(2,1)S(1)}, u32[]{:S(2)}, u32[]{:S(2)}) collective-permute-start(bf16[128,768]{1,0:T(8,128)(2,1)S(1)} %get-tuple-element.25.normed), channel_id=1, source_target_pairs={{0,4},{2,6},{4,0},{6,2},{1,5},{3,7},{5,1},{7,3},{8,12},{10,14},{12... | collective-permute-start | bytes 589832 | tf_op jit(solution)/shard_map/ppermute | solution.py:279
  54.3 0.0 collective-permute-start.2
  54.3 0.0 copy-done
  54.3 0.6 project.1
  54.9 2.5 %collective-permute-done.9.normed = bf16[128,768]{1,0:T(8,128)(2,1)S(1)} collective-permute-done((bf16[128,768]{1,0:T(8,128)(2,1)S(1)}, bf16[128,768]{1,0:T(8,128)(2,1)S(1)}, u32[]{:S(2)}, u32[]{:S(2)}) %collective-permute-start.9) | collective-permute-done | bytes 196640 | tf_op jit(solution)/shard_map/ppermute | solution.py:279
  57.5 0.5 other.5
  57.9 2.3 %collective-permute-done.8.normed = bf16[128,768]{1,0:T(8,128)(2,1)S(1)} collective-permute-done((bf16[128,768]{1,0:T(8,128)(2,1)S(1)}, bf16[128,768]{1,0:T(8,128)(2,1)S(1)}, u32[]{:S(2)}, u32[]{:S(2)}) %collective-permute-start.8) | collective-permute-done | bytes 196640 | tf_op jit(solution)/shard_map/ppermute | solution.py:279
  60.2 0.5 other.3
  60.7 4.2 %collective-permute-done.7.right = bf16[2,288,768]{2,1,0:T(8,128)(2,1)} collective-permute-done((bf16[2,288,768]{2,1,0:T(8,128)(2,1)}, bf16[2,288,768]{2,1,0:T(8,128)(2,1)}, u32[]{:S(2)}, u32[]{:S(2)}) %collective-permute-start.7) | collective-permute-done | bytes 884768 | tf_op jit(solution)/shard_map/ppermute | solution.py:341
  64.9 0.2 collective-permute-done.6.left
  65.0 1.2 %halves.1 = (bf16[1,288,768]{2,1,0:T(8,128)(2,1)S(1)}, bf16[1,288,768]{2,1,0:T(8,128)(2,1)S(1)}) custom-call(bf16[2,288,768]{2,1,0:T(8,128)(2,1)} %collective-permute-done.6.left, bf16[2,288,768]{2,1,0:T(8,128)(2,1)} %collective-permute-done.7.right, bf16[128,768]{1,0:T(8,128)(2,1)S(1)} %get-tuple-element.28._after.k2), custom_call_target="tpu_custom_call" | custom-call | flops 1000000000 | tf_op jit(solution)/shard_map/halves/pallas_call | solution.py:289
  66.2 2.2 %collective-permute-start.11 = (bf16[1,288,768]{2,1,0:T(8,128)(2,1)S(1)}, bf16[1,288,768]{2,1,0:T(8,128)(2,1)S(1)}, u32[]{:S(2)}, u32[]{:S(2)}) collective-permute-start(bf16[1,288,768]{2,1,0:T(8,128)(2,1)S(1)} %get-tuple-element.29.refs_0_._left), channel_id=1, source_target_pairs={{0,64},{64,128},{128,192},{192,0},{1,65},{65,129},{129,193},{193,1... | collective-permute-start | bytes 1327112 | tf_op jit(solution)/shard_map/ppermute | solution.py:376
  68.4 0.0 copy-start.1
  68.4 0.0 copy-start.3
  68.4 0.0 copy-start.4
  68.4 0.0 copy-start.5
  68.4 0.3 collective-permute-start.12
  68.7 0.0 collective-permute-done.2.normed
  68.7 0.5 other.4
  69.2 0.5 copy-done.1
  69.7 0.0 copy-done.3
  69.7 0.0 copy-done.4
  69.7 0.4 copy-done.5
  70.1 4.4 %attention.1 = (f32[128,768]{1,0:T(8,128)S(1)}, bf16[128,768]{1,0:T(8,128)(2,1)S(1)}) custom-call(bf16[128,768]{1,0:T(8,128)(2,1)S(1)} %get-tuple-element.26.k0, bf16[128,768]{1,0:T(8,128)(2,1)S(1)} %get-tuple-element.31.k1, bf16[128,768]{1,0:T(8,128)(2,1)S(1)} %get-tuple-element.28._after.k2, bf16[128,768]{1,0:T(8,128)(2,1)S(1)} %get-tuple-element.32.k3, ...), custom_call_target="tpu_custom_call" | custom-call | flops 4000000000 | tf_op jit(solution)/shard_map/attention/pallas_call | solution.py:289
  74.5 2.6 %collective-permute-start.10 = (bf16[128,768]{1,0:T(8,128)(2,1)S(1)}, bf16[128,768]{1,0:T(8,128)(2,1)S(1)}, u32[]{:S(2)}, u32[]{:S(2)}) collective-permute-start(bf16[128,768]{1,0:T(8,128)(2,1)S(1)} %get-tuple-element.39.own), channel_id=1, source_target_pairs={{0,1},{1,0},{2,3},{3,2},{4,5},{5,4},{6,7},{7,6},{8,9},{9,8},{10,11... | collective-permute-start | bytes 589832 | tf_op jit(solution)/shard_map/ppermute | solution.py:274
  77.1 1.1 %collective-permute-done.10.other = bf16[128,768]{1,0:T(8,128)(2,1)S(1)} collective-permute-done((bf16[128,768]{1,0:T(8,128)(2,1)S(1)}, bf16[128,768]{1,0:T(8,128)(2,1)S(1)}, u32[]{:S(2)}, u32[]{:S(2)}) %collective-permute-start.10) | collective-permute-done | bytes 196640 | tf_op jit(solution)/shard_map/ppermute | solution.py:274
  78.1 0.0 collective-permute-done.11
  78.1 0.9 collective-permute-done.12
  79.0 3.3 %transition.1 = (f32[2,64,768]{2,1,0:T(8,128)S(1)}, bf16[2,64,768]{2,1,0:T(8,128)(2,1)S(1)}) custom-call(bf16[128,768]{1,0:T(8,128)(2,1)S(1)} %get-tuple-element.39.own, bf16[128,768]{1,0:T(8,128)(2,1)S(1)} %collective-permute-done.10.other, f32[128,768]{1,0:T(8,128)S(1)} %get-tuple-element.40.stream, bf16[2,36,8,768]{3,2,1,0:T(8,128)(2,1)} %bitcast.1.here, ...), custom_call_target="tpu_custom_call" | custom-call | flops 1000000000 | tf_op jit(solution)/shard_map/transition/pallas_call | solution.py:289
  82.3 3.5 %collective-permute-start.13 = (bf16[2,64,768]{2,1,0:T(8,128)(2,1)S(1)}, bf16[2,64,768]{2,1,0:T(8,128)(2,1)S(1)}, u32[]{:S(2)}, u32[]{:S(2)}) collective-permute-start(bf16[2,64,768]{2,1,0:T(8,128)(2,1)S(1)} %get-tuple-element.42), channel_id=1, source_target_pairs={{0,1},{1,0},{2,3},{3,2},{4,5},{5,4},{6,7},{7,6},{8,9},{9,8},{10,11... | collective-permute-start | bytes 589832 | tf_op jit(solution)/shard_map/ppermute | solution.py:274
  85.8 1.1 %collective-permute-done.13 = bf16[2,64,768]{2,1,0:T(8,128)(2,1)S(1)} collective-permute-done((bf16[2,64,768]{2,1,0:T(8,128)(2,1)S(1)}, bf16[2,64,768]{2,1,0:T(8,128)(2,1)S(1)}, u32[]{:S(2)}, u32[]{:S(2)}) %collective-permute-start.13) | collective-permute-done | bytes 196640 | tf_op jit(solution)/shard_map/ppermute | solution.py:274
  86.9 0.7 add_convert_fusion
Async XLA Ops:
  2.1 23.2 %all-to-all-start = ((bf16[32,8,896]{2,1,0:T(8,128)(2,1)}), bf16[32,8,896]{2,1,0:T(8,128)(2,1)S(1)}, u32[]{:S(2)}, u32[]{:S(2)}) async-start(bf16[32,8,896]{2,1,0:T(8,128)(2,1)} %bitcast.8), calls=%async_computation | async-start | bytes 917504 | tf_op jit(solution)/shard_map/all_to_all | solution.py:323
  12.2 36.1 %collective-permute-start.1 = (bf16[16,64,512]{2,1,0:T(8,128)(2,1)}, bf16[16,64,512]{2,1,0:T(8,128)(2,1)}, u32[]{:S(2)}, u32[]{:S(2)}) collective-permute-start(bf16[16,64,512]{2,1,0:T(8,128)(2,1)} %bias_own.1), channel_id=1, source_target_pairs={{0,1},{1,0},{2,3},{3,2},{4,5},{5,4},{6,7},{7,6},{8,9},{9,8},{10,11... | collective-permute-start | bytes 3145736 | tf_op jit(solution)/shard_map/ppermute | solution.py:274
  26.4 11.5 %collective-permute-start.5 = (bf16[288,384]{1,0:T(8,128)(2,1)S(1)}, bf16[288,384]{1,0:T(8,128)(2,1)S(1)}, u32[]{:S(2)}, u32[]{:S(2)}) collective-permute-start(bf16[288,384]{1,0:T(8,128)(2,1)S(1)} %get-tuple-element.27.w0), channel_id=1, source_target_pairs={{0,6},{2,0},{4,2},{6,4},{1,7},{3,1},{5,3},{7,5},{8,14},{10,8},{12,... | collective-permute-start | bytes 663560 | tf_op jit(solution)/shard_map/ppermute | solution.py:279
  29.1 8.8 %collective-permute-start.4 = (bf16[288,384]{1,0:T(8,128)(2,1)S(1)}, bf16[288,384]{1,0:T(8,128)(2,1)S(1)}, u32[]{:S(2)}, u32[]{:S(2)}) collective-permute-start(bf16[288,384]{1,0:T(8,128)(2,1)S(1)} %get-tuple-element.27.w0), channel_id=1, source_target_pairs={{0,4},{2,6},{4,0},{6,2},{1,5},{3,7},{5,1},{7,3},{8,12},{10,14},{12... | collective-permute-start | bytes 663560 | tf_op jit(solution)/shard_map/ppermute | solution.py:279
  29.4 12.7 %collective-permute-start.3 = (bf16[288,384]{1,0:T(8,128)(2,1)S(1)}, bf16[288,384]{1,0:T(8,128)(2,1)S(1)}, u32[]{:S(2)}, u32[]{:S(2)}) collective-permute-start(bf16[288,384]{1,0:T(8,128)(2,1)S(1)} %get-tuple-element.27.w0), channel_id=1, source_target_pairs={{0,2},{2,4},{4,6},{6,0},{1,3},{3,5},{5,7},{7,1},{8,10},{10,12},{12... | collective-permute-start | bytes 663560 | tf_op jit(solution)/shard_map/ppermute | solution.py:279
  30.1 15.7 %all-to-all-start.1 = ((bf16[32,8,384]{2,1,0:T(8,128)(2,1)}), bf16[32,8,384]{2,1,0:T(8,128)(2,1)}, u32[]{:S(2)}, u32[]{:S(2)}) async-start(bf16[32,8,384]{2,1,0:T(8,128)(2,1)} %get-tuple-element.24), calls=%async_computation.1 | async-start | bytes 393216 | tf_op jit(solution)/shard_map/all_to_all | solution.py:343
  37.8 11.7 %copy-start.2 = (f32[768]{0:T(1024)S(1)}, f32[768]{0:T(1024)}, u32[]{:S(2)}) copy-start(f32[768]{0:T(1024)} %gain.1) | copy-start | bytes 9220
  43.1 11.2 %copy-start = (bf16[768,2304]{1,0:T(8,128)(2,1)S(1)}, bf16[768,2304]{1,0:T(8,128)(2,1)}, u32[]{:S(2)}) copy-start(bf16[768,2304]{1,0:T(8,128)(2,1)} %w_qkv.7) | copy-start | bytes 10616836
  43.1 21.7 %collective-permute-start.7 = (bf16[2,288,768]{2,1,0:T(8,128)(2,1)}, bf16[2,288,768]{2,1,0:T(8,128)(2,1)}, u32[]{:S(2)}, u32[]{:S(2)}) collective-permute-start(bf16[2,288,768]{2,1,0:T(8,128)(2,1)} %column.1), channel_id=1, source_target_pairs={{0,192},{64,0},{128,64},{192,128},{1,193},{65,1},{129,65},{193,129... | collective-permute-start | bytes 2654216 | tf_op jit(solution)/shard_map/ppermute | solution.py:341
  44.6 20.4 %collective-permute-start.6 = (bf16[2,288,768]{2,1,0:T(8,128)(2,1)}, bf16[2,288,768]{2,1,0:T(8,128)(2,1)}, u32[]{:S(2)}, u32[]{:S(2)}) collective-permute-start(bf16[2,288,768]{2,1,0:T(8,128)(2,1)} %column.1), channel_id=1, source_target_pairs={{0,64},{64,128},{128,192},{192,0},{1,65},{65,129},{129,193},{193,1... | collective-permute-start | bytes 2654216 | tf_op jit(solution)/shard_map/ppermute | solution.py:341
  45.8 3.7 %collective-permute-start = (bf16[32,8,384]{2,1,0:T(8,128)(2,1)}, bf16[32,8,384]{2,1,0:T(8,128)(2,1)S(1)}, u32[]{:S(2)}, u32[]{:S(2)}) collective-permute-start(bf16[32,8,384]{2,1,0:T(8,128)(2,1)} %all-to-all-done.1.mine), channel_id=1, source_target_pairs={{0,1},{1,0},{2,3},{3,2},{4,5},{5,4},{6,7},{7,6},{8,9},{9,8},{10,11... | collective-permute-start | bytes 589832 | tf_op jit(solution)/shard_map/ppermute | solution.py:274
  50.8 6.6 %collective-permute-start.9 = (bf16[128,768]{1,0:T(8,128)(2,1)S(1)}, bf16[128,768]{1,0:T(8,128)(2,1)S(1)}, u32[]{:S(2)}, u32[]{:S(2)}) collective-permute-start(bf16[128,768]{1,0:T(8,128)(2,1)S(1)} %get-tuple-element.25.normed), channel_id=1, source_target_pairs={{0,6},{2,0},{4,2},{6,4},{1,7},{3,1},{5,3},{7,5},{8,14},{10,8},{12,... | collective-permute-start | bytes 589832 | tf_op jit(solution)/shard_map/ppermute | solution.py:279
  52.9 7.3 %collective-permute-start.8 = (bf16[128,768]{1,0:T(8,128)(2,1)S(1)}, bf16[128,768]{1,0:T(8,128)(2,1)S(1)}, u32[]{:S(2)}, u32[]{:S(2)}) collective-permute-start(bf16[128,768]{1,0:T(8,128)(2,1)S(1)} %get-tuple-element.25.normed), channel_id=1, source_target_pairs={{0,4},{2,6},{4,0},{6,2},{1,5},{3,7},{5,1},{7,3},{8,12},{10,14},{12... | collective-permute-start | bytes 589832 | tf_op jit(solution)/shard_map/ppermute | solution.py:279
  54.3 14.4 %collective-permute-start.2 = (bf16[128,768]{1,0:T(8,128)(2,1)S(1)}, bf16[128,768]{1,0:T(8,128)(2,1)S(1)}, u32[]{:S(2)}, u32[]{:S(2)}) collective-permute-start(bf16[128,768]{1,0:T(8,128)(2,1)S(1)} %get-tuple-element.25.normed), channel_id=1, source_target_pairs={{0,2},{2,4},{4,6},{6,0},{1,3},{3,5},{5,7},{7,1},{8,10},{10,12},{12... | collective-permute-start | bytes 589832 | tf_op jit(solution)/shard_map/ppermute | solution.py:279
  66.2 11.9 %collective-permute-start.11 = (bf16[1,288,768]{2,1,0:T(8,128)(2,1)S(1)}, bf16[1,288,768]{2,1,0:T(8,128)(2,1)S(1)}, u32[]{:S(2)}, u32[]{:S(2)}) collective-permute-start(bf16[1,288,768]{2,1,0:T(8,128)(2,1)S(1)} %get-tuple-element.29.refs_0_._left), channel_id=1, source_target_pairs={{0,64},{64,128},{128,192},{192,0},{1,65},{65,129},{129,193},{193,1... | collective-permute-start | bytes 1327112 | tf_op jit(solution)/shard_map/ppermute | solution.py:376
  68.4 1.3 %copy-start.1 = (bf16[768,768]{1,0:T(8,128)(2,1)S(1)}, bf16[768,768]{1,0:T(8,128)(2,1)}, u32[]{:S(2)}) copy-start(bf16[768,768]{1,0:T(8,128)(2,1)} %w_o.1) | copy-start | bytes 3538948
  68.4 1.3 %copy-start.3 = (f32[768]{0:T(1024)S(1)}, f32[768]{0:T(1024)}, u32[]{:S(2)}) copy-start(f32[768]{0:T(1024)} %gain_ff.1) | copy-start | bytes 9220
  68.4 1.3 %copy-start.4 = (s32[512]{0:T(512)S(1)}, s32[512]{0:T(512)}, u32[]{:S(2)}) copy-start(s32[512]{0:T(512)} %mask.1) | copy-start | bytes 6148
  68.4 1.7 %copy-start.5 = (bf16[768,768]{1,0:T(8,128)(2,1)S(1)}, bf16[768,768]{1,0:T(8,128)(2,1)}, u32[]{:S(2)}) copy-start(bf16[768,768]{1,0:T(8,128)(2,1)} %constant.2.clone.order) | copy-start | bytes 3538948
  68.4 10.6 %collective-permute-start.12 = (bf16[1,288,768]{2,1,0:T(8,128)(2,1)S(1)}, bf16[1,288,768]{2,1,0:T(8,128)(2,1)S(1)}, u32[]{:S(2)}, u32[]{:S(2)}) collective-permute-start(bf16[1,288,768]{2,1,0:T(8,128)(2,1)S(1)} %get-tuple-element.30.refs_1_._right), channel_id=1, source_target_pairs={{0,192},{64,0},{128,64},{192,128},{1,193},{65,1},{129,65},{193,129... | collective-permute-start | bytes 1327112 | tf_op jit(solution)/shard_map/ppermute | solution.py:376
  74.5 3.7 %collective-permute-start.10 = (bf16[128,768]{1,0:T(8,128)(2,1)S(1)}, bf16[128,768]{1,0:T(8,128)(2,1)S(1)}, u32[]{:S(2)}, u32[]{:S(2)}) collective-permute-start(bf16[128,768]{1,0:T(8,128)(2,1)S(1)} %get-tuple-element.39.own), channel_id=1, source_target_pairs={{0,1},{1,0},{2,3},{3,2},{4,5},{5,4},{6,7},{7,6},{8,9},{9,8},{10,11... | collective-permute-start | bytes 589832 | tf_op jit(solution)/shard_map/ppermute | solution.py:274
  82.3 4.6 %collective-permute-start.13 = (bf16[2,64,768]{2,1,0:T(8,128)(2,1)S(1)}, bf16[2,64,768]{2,1,0:T(8,128)(2,1)S(1)}, u32[]{:S(2)}, u32[]{:S(2)}) collective-permute-start(bf16[2,64,768]{2,1,0:T(8,128)(2,1)S(1)} %get-tuple-element.42), channel_id=1, source_target_pairs={{0,1},{1,0},{2,3},{3,2},{4,5},{5,4},{6,7},{7,6},{8,9},{9,8},{10,11... | collective-permute-start | bytes 589832 | tf_op jit(solution)/shard_map/ppermute | solution.py:274

commit v6 on v5

--- a/solution.py
+++ b/solution.py
@@ -76,24 +76,28 @@
         out_ref[at, :, :, width:] = jnp.broadcast_to(last.astype(jnp.bfloat16), shape + (128,))
 
 
-def pick_kernel(pieces, picked_ref, weights_ref):
-    c = lax.axis_index("c")
-    half = picked_ref.shape[2]
+def unpack_kernel(pieces, states_ref, weights_ref, onehot_ref):
+    half = states_ref.shape[1]
     width = 2 * half
     rows = pieces[...].astype(jnp.float32).reshape(-1, width + 128)
     count = rows.shape[0]
+    states_ref[...] = rows[:, :half].astype(jnp.bfloat16)
     last = rows[:, width:].astype(jnp.bfloat16)
-    out_row, in_row = iotas((count, count))
-    part = lax.rem(out_row // PIECE + c, 2)
-    names = reorder(in_row == out_row // TILE * TILE + 3 + part, last)[:, :1]
-    onehot = in_row == names.astype(jnp.int32) * PIECE + out_row % PIECE
-    picked = reorder(onehot, rows[:, :half].astype(jnp.bfloat16))
-    picked_ref[...] = picked.reshape(picked_ref.shape).astype(jnp.bfloat16)
     weights_ref[:count] = rows[:, half:width].astype(jnp.bfloat16)
     out_row, in_row = iotas((GROUP, count))
     for i in range(3):
         extra = reorder(in_row == out_row * TILE + i, last).astype(jnp.bfloat16)
         weights_ref[count:, i * 128 : (i + 1) * 128] = extra
+    out_row, in_row = iotas((count, count))
+    part = lax.rem(out_row // PIECE + lax.axis_index("c"), 2)
+    names = reorder(in_row == out_row // TILE * TILE + 3 + part, last)[:, :1]
+    onehot = in_row == names.astype(jnp.int32) * PIECE + out_row % PIECE
+    onehot_ref[...] = onehot.astype(jnp.bfloat16)
+
+
+def pick_kernel(onehot, states, picked_ref):
+    picked = reorder(onehot[...], states[...])
+    picked_ref[...] = picked.reshape(picked_ref.shape).astype(jnp.bfloat16)
 
 
 def column_kernel(w0, w1, w2, w3, out_ref):
@@ -321,13 +325,25 @@
         scratch=[pltpu.VMEM((3 * depth, width), f32)],
     )
     pieces = lax.all_to_all(pieces.reshape(GROUP, both, width + 128), PARTICLE, 0, 0)
-    picked, piece = kernel(
+    come, piece, onehot = kernel(
+        unpack_kernel,
+        "unpack",
+        [None],
+        (pieces,),
+        [
+            ((GROUP * both, half), bf16),
+            ((GROUP * (TILE + 1), half), bf16),
+            ((GROUP * both, GROUP * both), bf16),
+        ],
+    )
+    (picked,) = kernel(
         pick_kernel,
         "pick",
-        [None],
-        (pieces,),
-        [((GROUP, both, half), bf16), ((GROUP * (TILE + 1), half), bf16)],
+        [None, None],
+        (onehot, come),
+        [((GROUP, both, half), bf16)],
         limit=40,
+        wait=1,
     )
     ring = [piece] + others(piece, "y", NY)
     (column,) = kernel(

time: 88 us -> 87.3 us (level)
  the two profiles are of different devices: /device:TPU:71 before, /device:TPU:1 now
where the time goes in v6:
time: 87.3 us; the launch traced here: 85.9 us
  starting transfers between devices  41.1 us (47%)
  waiting for transfers between devices  27.5 us (32%)
  Pallas kernels  16.4 us (19%)
    pallas_call x12, Pallas kernels, kernel(): pl.pallas_call(f, grid=(1,), out_shape=outs, in_specs=specs, out_specs=tu...  16.4 us
    all_to_all x1, waiting for transfers between devices, body(): lax.all_to_all(pieces.reshape(GROUP, both, width + 128), PARTICLE, 0, 0)  11.9 us
    all_to_all x1, starting transfers between devices, body(): lax.all_to_all(pieces.reshape(GROUP, both, width + 128), PARTICLE, 0, 0)  11.9 us
    ppermute x4, starting transfers between devices, swap_cores(): return lax.ppermute(value, 'c', [(0, 1), (1, 0)])  9.59 us
    all_to_all x1, starting transfers between devices, body(): mine = lax.all_to_all(picked, PARTICLE, 0, 0)  7.9 us
    ppermute x6, starting transfers between devices, others(): lax.ppermute(value, axis, [(i, (i + k) % size) for i in range(size)])  7.33 us
    ppermute x6, waiting for transfers between devices, others(): lax.ppermute(value, axis, [(i, (i + k) % size) for i in range(size)])  6.68 us
    all_to_all x1, waiting for transfers between devices, body(): mine = lax.all_to_all(picked, PARTICLE, 0, 0)  5.14 us
  transfers between devices with their start and end apart: 16, of which 10 were waited for; matrix products, arithmetic and copies ran while one was open for 0% of the time, Pallas kernels for 13%

profile of v6, /device:TPU:1, one launch (start us, length us, event | category | flops | bytes accessed | tf_op | source)
XLA Modules:
  0.0 85.9 jit_solution(1128031267183181169)
XLA Ops:
  0.0 2.1 %spread.1 = bf16[16,2,8,896]{3,2,1,0:T(8,128)(2,1)} custom-call(s32[2]{0:T(128)} %ancestors.1, bf16[2,64,768]{2,1,0:T(8,128)(2,1)} %states.1, bf16[2,24,1536]{2,1,0:T(8,128)(2,1)} %w_in.1, bf16[24,1536]{1,0:T(8,128)(2,1)} %w_out.1), custom_call_target="tpu_custom_call" | custom-call | flops 1000000000 | tf_op jit(solution)/shard_map/spread/pallas_call | solution.py:293
  2.1 11.9 %all-to-all-start = ((bf16[32,8,896]{2,1,0:T(8,128)(2,1)}), bf16[32,8,896]{2,1,0:T(8,128)(2,1)S(1)}, u32[]{:S(2)}, u32[]{:S(2)}) async-start(bf16[32,8,896]{2,1,0:T(8,128)(2,1)} %bitcast.8), calls=%async_computation | async-start | bytes 917504 | tf_op jit(solution)/shard_map/all_to_all | solution.py:327
  13.9 1.0 %collective-permute-start.1 = (bf16[16,64,512]{2,1,0:T(8,128)(2,1)}, bf16[16,64,512]{2,1,0:T(8,128)(2,1)}, u32[]{:S(2)}, u32[]{:S(2)}) collective-permute-start(bf16[16,64,512]{2,1,0:T(8,128)(2,1)} %bias_own.1), channel_id=1, source_target_pairs={{0,1},{1,0},{2,3},{3,2},{4,5},{5,4},{6,7},{7,6},{8,9},{9,8},{10,11... | collective-permute-start | bytes 3145736 | tf_op jit(solution)/shard_map/ppermute | solution.py:278
  15.0 11.9 %all-to-all-done.pieces = bf16[32,8,896]{2,1,0:T(8,128)(2,1)S(1)} async-done(((bf16[32,8,896]{2,1,0:T(8,128)(2,1)}), bf16[32,8,896]{2,1,0:T(8,128)(2,1)S(1)}, u32[]{:S(2)}, u32[]{:S(2)}) %all-to-all-start) | async-done | bytes 458784 | tf_op jit(solution)/shard_map/all_to_all | solution.py:327
  26.8 0.3 unpack.1
  27.1 2.8 %collective-permute-start.5 = (bf16[288,384]{1,0:T(8,128)(2,1)S(1)}, bf16[288,384]{1,0:T(8,128)(2,1)S(1)}, u32[]{:S(2)}, u32[]{:S(2)}) collective-permute-start(bf16[288,384]{1,0:T(8,128)(2,1)S(1)} %get-tuple-element.29.w0), channel_id=1, source_target_pairs={{0,6},{2,0},{4,2},{6,4},{1,7},{3,1},{5,3},{7,5},{8,14},{10,8},{12,... | collective-permute-start | bytes 663560 | tf_op jit(solution)/shard_map/ppermute | solution.py:283
  30.0 0.4 collective-permute-start.4
  30.3 0.7 collective-permute-start.3
  31.0 0.9 %pick.1 = bf16[32,8,384]{2,1,0:T(8,128)(2,1)} custom-call(bf16[256,256]{1,0:T(8,128)(2,1)S(1)} %get-tuple-element.25.onehot, bf16[256,384]{1,0:T(8,128)(2,1)S(1)} %get-tuple-element.26.states), custom_call_target="tpu_custom_call" | custom-call | flops 1000000000 | tf_op jit(solution)/shard_map/pick/pallas_call | solution.py:293
  31.9 7.9 %all-to-all-start.1 = ((bf16[32,8,384]{2,1,0:T(8,128)(2,1)}), bf16[32,8,384]{2,1,0:T(8,128)(2,1)}, u32[]{:S(2)}, u32[]{:S(2)}) async-start(bf16[32,8,384]{2,1,0:T(8,128)(2,1)} %pick.1), calls=%async_computation.1 | async-start | bytes 393216 | tf_op jit(solution)/shard_map/all_to_all | solution.py:359
  39.8 0.0 copy-start.2
  39.8 0.0 collective-permute-done.5.w3
  39.8 0.0 collective-permute-done.4.w2
  39.8 1.7 %collective-permute-done.3.w1 = bf16[288,384]{1,0:T(8,128)(2,1)S(1)} collective-permute-done((bf16[288,384]{1,0:T(8,128)(2,1)S(1)}, bf16[288,384]{1,0:T(8,128)(2,1)S(1)}, u32[]{:S(2)}, u32[]{:S(2)}) %collective-permute-start.3) | collective-permute-done | bytes 221216 | tf_op jit(solution)/shard_map/ppermute | solution.py:283
  41.6 1.0 %column.1 = bf16[2,288,768]{2,1,0:T(8,128)(2,1)} custom-call(bf16[288,384]{1,0:T(8,128)(2,1)S(1)} %get-tuple-element.29.w0, bf16[288,384]{1,0:T(8,128)(2,1)S(1)} %collective-permute-done.3.w1, bf16[288,384]{1,0:T(8,128)(2,1)S(1)} %collective-permute-done.4.w2, bf16[288,384]{1,0:T(8,128)(2,1)S(1)} %collective-permute-done.5.w3), custom_call_target="tpu_custom_call" | custom-call | flops 1000000000 | tf_op jit(solution)/shard_map/column/pallas_call | solution.py:293
  42.6 0.0 copy-start
  42.6 1.4 %collective-permute-start.7 = (bf16[2,288,768]{2,1,0:T(8,128)(2,1)}, bf16[2,288,768]{2,1,0:T(8,128)(2,1)}, u32[]{:S(2)}, u32[]{:S(2)}) collective-permute-start(bf16[2,288,768]{2,1,0:T(8,128)(2,1)} %column.1), channel_id=1, source_target_pairs={{0,192},{64,0},{128,64},{192,128},{1,193},{65,1},{129,65},{193,129... | collective-permute-start | bytes 2654216 | tf_op jit(solution)/shard_map/ppermute | solution.py:357
  44.0 0.1 collective-permute-start.6
  44.1 5.1 %all-to-all-done.1.mine = bf16[32,8,384]{2,1,0:T(8,128)(2,1)} async-done(((bf16[32,8,384]{2,1,0:T(8,128)(2,1)}), bf16[32,8,384]{2,1,0:T(8,128)(2,1)}, u32[]{:S(2)}, u32[]{:S(2)}) %all-to-all-start.1) | async-done | bytes 196640 | tf_op jit(solution)/shard_map/all_to_all | solution.py:359
  49.2 3.8 %collective-permute-start = (bf16[32,8,384]{2,1,0:T(8,128)(2,1)}, bf16[32,8,384]{2,1,0:T(8,128)(2,1)S(1)}, u32[]{:S(2)}, u32[]{:S(2)}) collective-permute-start(bf16[32,8,384]{2,1,0:T(8,128)(2,1)} %all-to-all-done.1.mine), channel_id=1, source_target_pairs={{0,1},{1,0},{2,3},{3,2},{4,5},{5,4},{6,7},{7,6},{8,9},{9,8},{10,11... | collective-permute-start | bytes 589832 | tf_op jit(solution)/shard_map/ppermute | solution.py:278
  52.9 0.0 collective-permute-done.1._bias.bias_other
  52.9 1.3 %collective-permute-done.theirs = bf16[32,8,384]{2,1,0:T(8,128)(2,1)S(1)} collective-permute-done((bf16[32,8,384]{2,1,0:T(8,128)(2,1)}, bf16[32,8,384]{2,1,0:T(8,128)(2,1)S(1)}, u32[]{:S(2)}, u32[]{:S(2)}) %collective-permute-start) | collective-permute-done | bytes 196640 | tf_op jit(solution)/shard_map/ppermute | solution.py:278
  54.2 0.0 copy-done.2
  54.2 1.2 %own.1 = (bf16[128,768]{1,0:T(8,128)(2,1)S(1)}, bf16[128,768]{1,0:T(8,128)(2,1)S(1)}) custom-call(bf16[32,8,384]{2,1,0:T(8,128)(2,1)} %all-to-all-done.1.mine, bf16[32,8,384]{2,1,0:T(8,128)(2,1)S(1)} %collective-permute-done.theirs, f32[768]{0:T(1024)S(1)} %copy-done.2, bf16[16,64,512]{2,1,0:T(8,128)(2,1)} %collective-permute-done.1._bias.bias_other), custom_call_target="tpu_custom_call" | custom-call | flops 1000000000 | tf_op jit(solution)/shard_map/own/pallas_call | solution.py:293
  55.5 2.1 %collective-permute-start.9 = (bf16[128,768]{1,0:T(8,128)(2,1)S(1)}, bf16[128,768]{1,0:T(8,128)(2,1)S(1)}, u32[]{:S(2)}, u32[]{:S(2)}) collective-permute-start(bf16[128,768]{1,0:T(8,128)(2,1)S(1)} %get-tuple-element.27.normed), channel_id=1, source_target_pairs={{0,6},{2,0},{4,2},{6,4},{1,7},{3,1},{5,3},{7,5},{8,14},{10,8},{12,... | collective-permute-start | bytes 589832 | tf_op jit(solution)/shard_map/ppermute | solution.py:283
  57.5 1.4 %collective-permute-start.8 = (bf16[128,768]{1,0:T(8,128)(2,1)S(1)}, bf16[128,768]{1,0:T(8,128)(2,1)S(1)}, u32[]{:S(2)}, u32[]{:S(2)}) collective-permute-start(bf16[128,768]{1,0:T(8,128)(2,1)S(1)} %get-tuple-element.27.normed), channel_id=1, source_target_pairs={{0,4},{2,6},{4,0},{6,2},{1,5},{3,7},{5,1},{7,3},{8,12},{10,14},{12... | collective-permute-start | bytes 589832 | tf_op jit(solution)/shard_map/ppermute | solution.py:283
  58.9 0.0 collective-permute-start.2
  58.9 0.0 copy-done
  58.9 0.6 project.1
  59.6 2.5 %collective-permute-done.9.normed = bf16[128,768]{1,0:T(8,128)(2,1)S(1)} collective-permute-done((bf16[128,768]{1,0:T(8,128)(2,1)S(1)}, bf16[128,768]{1,0:T(8,128)(2,1)S(1)}, u32[]{:S(2)}, u32[]{:S(2)}) %collective-permute-start.9) | collective-permute-done | bytes 196640 | tf_op jit(solution)/shard_map/ppermute | solution.py:283
  62.1 0.5 other.5
  62.6 2.3 %collective-permute-done.8.normed = bf16[128,768]{1,0:T(8,128)(2,1)S(1)} collective-permute-done((bf16[128,768]{1,0:T(8,128)(2,1)S(1)}, bf16[128,768]{1,0:T(8,128)(2,1)S(1)}, u32[]{:S(2)}, u32[]{:S(2)}) %collective-permute-start.8) | collective-permute-done | bytes 196640 | tf_op jit(solution)/shard_map/ppermute | solution.py:283
  64.9 0.5 other.3
  65.4 0.0 collective-permute-done.7.right
  65.4 0.4 collective-permute-done.6.left
  65.7 1.2 %halves.1 = (bf16[1,288,768]{2,1,0:T(8,128)(2,1)S(1)}, bf16[1,288,768]{2,1,0:T(8,128)(2,1)S(1)}) custom-call(bf16[2,288,768]{2,1,0:T(8,128)(2,1)} %collective-permute-done.6.left, bf16[2,288,768]{2,1,0:T(8,128)(2,1)} %collective-permute-done.7.right, bf16[128,768]{1,0:T(8,128)(2,1)S(1)} %get-tuple-element.30._after.k2), custom_call_target="tpu_custom_call" | custom-call | flops 1000000000 | tf_op jit(solution)/shard_map/halves/pallas_call | solution.py:293
  66.9 0.1 collective-permute-start.11
  67.0 0.0 copy-start.1
  67.0 0.0 copy-start.3
  67.0 0.0 copy-start.4
  67.0 0.0 copy-start.5
  67.0 2.9 %collective-permute-start.12 = (bf16[1,288,768]{2,1,0:T(8,128)(2,1)S(1)}, bf16[1,288,768]{2,1,0:T(8,128)(2,1)S(1)}, u32[]{:S(2)}, u32[]{:S(2)}) collective-permute-start(bf16[1,288,768]{2,1,0:T(8,128)(2,1)S(1)} %get-tuple-element.32.refs_1_._right), channel_id=1, source_target_pairs={{0,192},{64,0},{128,64},{192,128},{1,193},{65,1},{129,65},{193,129... | collective-permute-start | bytes 1327112 | tf_op jit(solution)/shard_map/ppermute | solution.py:392
  69.9 0.1 collective-permute-done.2.normed
  70.1 0.5 other.4
  70.6 0.0 copy-done.1
  70.6 0.0 copy-done.3
  70.6 0.0 copy-done.4
  70.6 0.0 copy-done.5
  70.6 4.4 %attention.1 = (f32[128,768]{1,0:T(8,128)S(1)}, bf16[128,768]{1,0:T(8,128)(2,1)S(1)}) custom-call(bf16[128,768]{1,0:T(8,128)(2,1)S(1)} %get-tuple-element.28.k0, bf16[128,768]{1,0:T(8,128)(2,1)S(1)} %get-tuple-element.33.k1, bf16[128,768]{1,0:T(8,128)(2,1)S(1)} %get-tuple-element.30._after.k2, bf16[128,768]{1,0:T(8,128)(2,1)S(1)} %get-tuple-element.34.k3, ...), custom_call_target="tpu_custom_call" | custom-call | flops 4000000000 | tf_op jit(solution)/shard_map/attention/pallas_call | solution.py:293
  75.0 3.3 %collective-permute-start.10 = (bf16[128,768]{1,0:T(8,128)(2,1)S(1)}, bf16[128,768]{1,0:T(8,128)(2,1)S(1)}, u32[]{:S(2)}, u32[]{:S(2)}) collective-permute-start(bf16[128,768]{1,0:T(8,128)(2,1)S(1)} %get-tuple-element.41.own), channel_id=1, source_target_pairs={{0,1},{1,0},{2,3},{3,2},{4,5},{5,4},{6,7},{7,6},{8,9},{9,8},{10,11... | collective-permute-start | bytes 589832 | tf_op jit(solution)/shard_map/ppermute | solution.py:278
  78.3 1.1 %collective-permute-done.10.other = bf16[128,768]{1,0:T(8,128)(2,1)S(1)} collective-permute-done((bf16[128,768]{1,0:T(8,128)(2,1)S(1)}, bf16[128,768]{1,0:T(8,128)(2,1)S(1)}, u32[]{:S(2)}, u32[]{:S(2)}) %collective-permute-start.10) | collective-permute-done | bytes 196640 | tf_op jit(solution)/shard_map/ppermute | solution.py:278
  79.4 0.0 collective-permute-done.11
  79.4 0.0 collective-permute-done.12
  79.4 3.3 %transition.1 = (f32[2,64,768]{2,1,0:T(8,128)S(1)}, bf16[2,64,768]{2,1,0:T(8,128)(2,1)S(1)}) custom-call(bf16[128,768]{1,0:T(8,128)(2,1)S(1)} %get-tuple-element.41.own, bf16[128,768]{1,0:T(8,128)(2,1)S(1)} %collective-permute-done.10.other, f32[128,768]{1,0:T(8,128)S(1)} %get-tuple-element.42.stream, bf16[2,36,8,768]{3,2,1,0:T(8,128)(2,1)} %bitcast.1.here, ...), custom_call_target="tpu_custom_call" | custom-call | flops 1000000000 | tf_op jit(solution)/shard_map/transition/pallas_call | solution.py:293
  82.7 1.5 %collective-permute-start.13 = (bf16[2,64,768]{2,1,0:T(8,128)(2,1)S(1)}, bf16[2,64,768]{2,1,0:T(8,128)(2,1)S(1)}, u32[]{:S(2)}, u32[]{:S(2)}) collective-permute-start(bf16[2,64,768]{2,1,0:T(8,128)(2,1)S(1)} %get-tuple-element.44), channel_id=1, source_target_pairs={{0,1},{1,0},{2,3},{3,2},{4,5},{5,4},{6,7},{7,6},{8,9},{9,8},{10,11... | collective-permute-start | bytes 589832 | tf_op jit(solution)/shard_map/ppermute | solution.py:278
  84.2 1.1 %collective-permute-done.13 = bf16[2,64,768]{2,1,0:T(8,128)(2,1)S(1)} collective-permute-done((bf16[2,64,768]{2,1,0:T(8,128)(2,1)S(1)}, bf16[2,64,768]{2,1,0:T(8,128)(2,1)S(1)}, u32[]{:S(2)}, u32[]{:S(2)}) %collective-permute-start.13) | collective-permute-done | bytes 196640 | tf_op jit(solution)/shard_map/ppermute | solution.py:278
  85.2 0.7 add_convert_fusion
Async XLA Ops:
  2.1 24.8 %all-to-all-start = ((bf16[32,8,896]{2,1,0:T(8,128)(2,1)}), bf16[32,8,896]{2,1,0:T(8,128)(2,1)S(1)}, u32[]{:S(2)}, u32[]{:S(2)}) async-start(bf16[32,8,896]{2,1,0:T(8,128)(2,1)} %bitcast.8), calls=%async_computation | async-start | bytes 917504 | tf_op jit(solution)/shard_map/all_to_all | solution.py:327
  13.9 39.0 %collective-permute-start.1 = (bf16[16,64,512]{2,1,0:T(8,128)(2,1)}, bf16[16,64,512]{2,1,0:T(8,128)(2,1)}, u32[]{:S(2)}, u32[]{:S(2)}) collective-permute-start(bf16[16,64,512]{2,1,0:T(8,128)(2,1)} %bias_own.1), channel_id=1, source_target_pairs={{0,1},{1,0},{2,3},{3,2},{4,5},{5,4},{6,7},{7,6},{8,9},{9,8},{10,11... | collective-permute-start | bytes 3145736 | tf_op jit(solution)/shard_map/ppermute | solution.py:278
  27.1 12.7 %collective-permute-start.5 = (bf16[288,384]{1,0:T(8,128)(2,1)S(1)}, bf16[288,384]{1,0:T(8,128)(2,1)S(1)}, u32[]{:S(2)}, u32[]{:S(2)}) collective-permute-start(bf16[288,384]{1,0:T(8,128)(2,1)S(1)} %get-tuple-element.29.w0), channel_id=1, source_target_pairs={{0,6},{2,0},{4,2},{6,4},{1,7},{3,1},{5,3},{7,5},{8,14},{10,8},{12,... | collective-permute-start | bytes 663560 | tf_op jit(solution)/shard_map/ppermute | solution.py:283
  30.0 9.9 %collective-permute-start.4 = (bf16[288,384]{1,0:T(8,128)(2,1)S(1)}, bf16[288,384]{1,0:T(8,128)(2,1)S(1)}, u32[]{:S(2)}, u32[]{:S(2)}) collective-permute-start(bf16[288,384]{1,0:T(8,128)(2,1)S(1)} %get-tuple-element.29.w0), channel_id=1, source_target_pairs={{0,4},{2,6},{4,0},{6,2},{1,5},{3,7},{5,1},{7,3},{8,12},{10,14},{12... | collective-permute-start | bytes 663560 | tf_op jit(solution)/shard_map/ppermute | solution.py:283
  30.3 11.2 %collective-permute-start.3 = (bf16[288,384]{1,0:T(8,128)(2,1)S(1)}, bf16[288,384]{1,0:T(8,128)(2,1)S(1)}, u32[]{:S(2)}, u32[]{:S(2)}) collective-permute-start(bf16[288,384]{1,0:T(8,128)(2,1)S(1)} %get-tuple-element.29.w0), channel_id=1, source_target_pairs={{0,2},{2,4},{4,6},{6,0},{1,3},{3,5},{5,7},{7,1},{8,10},{10,12},{12... | collective-permute-start | bytes 663560 | tf_op jit(solution)/shard_map/ppermute | solution.py:283
  31.9 17.3 %all-to-all-start.1 = ((bf16[32,8,384]{2,1,0:T(8,128)(2,1)}), bf16[32,8,384]{2,1,0:T(8,128)(2,1)}, u32[]{:S(2)}, u32[]{:S(2)}) async-start(bf16[32,8,384]{2,1,0:T(8,128)(2,1)} %pick.1), calls=%async_computation.1 | async-start | bytes 393216 | tf_op jit(solution)/shard_map/all_to_all | solution.py:359
  39.8 14.4 %copy-start.2 = (f32[768]{0:T(1024)S(1)}, f32[768]{0:T(1024)}, u32[]{:S(2)}) copy-start(f32[768]{0:T(1024)} %gain.1) | copy-start | bytes 9220
  42.6 16.4 %copy-start = (bf16[768,2304]{1,0:T(8,128)(2,1)S(1)}, bf16[768,2304]{1,0:T(8,128)(2,1)}, u32[]{:S(2)}) copy-start(bf16[768,2304]{1,0:T(8,128)(2,1)} %w_qkv.7) | copy-start | bytes 10616836
  42.6 22.8 %collective-permute-start.7 = (bf16[2,288,768]{2,1,0:T(8,128)(2,1)}, bf16[2,288,768]{2,1,0:T(8,128)(2,1)}, u32[]{:S(2)}, u32[]{:S(2)}) collective-permute-start(bf16[2,288,768]{2,1,0:T(8,128)(2,1)} %column.1), channel_id=1, source_target_pairs={{0,192},{64,0},{128,64},{192,128},{1,193},{65,1},{129,65},{193,129... | collective-permute-start | bytes 2654216 | tf_op jit(solution)/shard_map/ppermute | solution.py:357
  44.0 21.8 %collective-permute-start.6 = (bf16[2,288,768]{2,1,0:T(8,128)(2,1)}, bf16[2,288,768]{2,1,0:T(8,128)(2,1)}, u32[]{:S(2)}, u32[]{:S(2)}) collective-permute-start(bf16[2,288,768]{2,1,0:T(8,128)(2,1)} %column.1), channel_id=1, source_target_pairs={{0,64},{64,128},{128,192},{192,0},{1,65},{65,129},{129,193},{193,1... | collective-permute-start | bytes 2654216 | tf_op jit(solution)/shard_map/ppermute | solution.py:357
  49.2 5.0 %collective-permute-start = (bf16[32,8,384]{2,1,0:T(8,128)(2,1)}, bf16[32,8,384]{2,1,0:T(8,128)(2,1)S(1)}, u32[]{:S(2)}, u32[]{:S(2)}) collective-permute-start(bf16[32,8,384]{2,1,0:T(8,128)(2,1)} %all-to-all-done.1.mine), channel_id=1, source_target_pairs={{0,1},{1,0},{2,3},{3,2},{4,5},{5,4},{6,7},{7,6},{8,9},{9,8},{10,11... | collective-permute-start | bytes 589832 | tf_op jit(solution)/shard_map/ppermute | solution.py:278
  55.5 6.6 %collective-permute-start.9 = (bf16[128,768]{1,0:T(8,128)(2,1)S(1)}, bf16[128,768]{1,0:T(8,128)(2,1)S(1)}, u32[]{:S(2)}, u32[]{:S(2)}) collective-permute-start(bf16[128,768]{1,0:T(8,128)(2,1)S(1)} %get-tuple-element.27.normed), channel_id=1, source_target_pairs={{0,6},{2,0},{4,2},{6,4},{1,7},{3,1},{5,3},{7,5},{8,14},{10,8},{12,... | collective-permute-start | bytes 589832 | tf_op jit(solution)/shard_map/ppermute | solution.py:283
  57.5 7.3 %collective-permute-start.8 = (bf16[128,768]{1,0:T(8,128)(2,1)S(1)}, bf16[128,768]{1,0:T(8,128)(2,1)S(1)}, u32[]{:S(2)}, u32[]{:S(2)}) collective-permute-start(bf16[128,768]{1,0:T(8,128)(2,1)S(1)} %get-tuple-element.27.normed), channel_id=1, source_target_pairs={{0,4},{2,6},{4,0},{6,2},{1,5},{3,7},{5,1},{7,3},{8,12},{10,14},{12... | collective-permute-start | bytes 589832 | tf_op jit(solution)/shard_map/ppermute | solution.py:283
  58.9 11.1 %collective-permute-start.2 = (bf16[128,768]{1,0:T(8,128)(2,1)S(1)}, bf16[128,768]{1,0:T(8,128)(2,1)S(1)}, u32[]{:S(2)}, u32[]{:S(2)}) collective-permute-start(bf16[128,768]{1,0:T(8,128)(2,1)S(1)} %get-tuple-element.27.normed), channel_id=1, source_target_pairs={{0,2},{2,4},{4,6},{6,0},{1,3},{3,5},{5,7},{7,1},{8,10},{10,12},{12... | collective-permute-start | bytes 589832 | tf_op jit(solution)/shard_map/ppermute | solution.py:283
  66.9 12.5 %collective-permute-start.11 = (bf16[1,288,768]{2,1,0:T(8,128)(2,1)S(1)}, bf16[1,288,768]{2,1,0:T(8,128)(2,1)S(1)}, u32[]{:S(2)}, u32[]{:S(2)}) collective-permute-start(bf16[1,288,768]{2,1,0:T(8,128)(2,1)S(1)} %get-tuple-element.31.refs_0_._left), channel_id=1, source_target_pairs={{0,64},{64,128},{128,192},{192,0},{1,65},{65,129},{129,193},{193,1... | collective-permute-start | bytes 1327112 | tf_op jit(solution)/shard_map/ppermute | solution.py:392
  67.0 3.6 %copy-start.1 = (bf16[768,768]{1,0:T(8,128)(2,1)S(1)}, bf16[768,768]{1,0:T(8,128)(2,1)}, u32[]{:S(2)}) copy-start(bf16[768,768]{1,0:T(8,128)(2,1)} %w_o.1) | copy-start | bytes 3538948
  67.0 3.6 %copy-start.3 = (f32[768]{0:T(1024)S(1)}, f32[768]{0:T(1024)}, u32[]{:S(2)}) copy-start(f32[768]{0:T(1024)} %gain_ff.1) | copy-start | bytes 9220
  67.0 3.6 %copy-start.4 = (s32[512]{0:T(512)S(1)}, s32[512]{0:T(512)}, u32[]{:S(2)}) copy-start(s32[512]{0:T(512)} %mask.1) | copy-start | bytes 6148
  67.0 3.6 %copy-start.5 = (bf16[768,768]{1,0:T(8,128)(2,1)S(1)}, bf16[768,768]{1,0:T(8,128)(2,1)}, u32[]{:S(2)}) copy-start(bf16[768,768]{1,0:T(8,128)(2,1)} %constant.2.clone.order) | copy-start | bytes 3538948
  67.0 12.4 %collective-permute-start.12 = (bf16[1,288,768]{2,1,0:T(8,128)(2,1)S(1)}, bf16[1,288,768]{2,1,0:T(8,128)(2,1)S(1)}, u32[]{:S(2)}, u32[]{:S(2)}) collective-permute-start(bf16[1,288,768]{2,1,0:T(8,128)(2,1)S(1)} %get-tuple-element.32.refs_1_._right), channel_id=1, source_target_pairs={{0,192},{64,0},{128,64},{192,128},{1,193},{65,1},{129,65},{193,129... | collective-permute-start | bytes 1327112 | tf_op jit(solution)/shard_map/ppermute | solution.py:392
  75.0 4.4 %collective-permute-start.10 = (bf16[128,768]{1,0:T(8,128)(2,1)S(1)}, bf16[128,768]{1,0:T(8,128)(2,1)S(1)}, u32[]{:S(2)}, u32[]{:S(2)}) collective-permute-start(bf16[128,768]{1,0:T(8,128)(2,1)S(1)} %get-tuple-element.41.own), channel_id=1, source_target_pairs={{0,1},{1,0},{2,3},{3,2},{4,5},{5,4},{6,7},{7,6},{8,9},{9,8},{10,11... | collective-permute-start | bytes 589832 | tf_op jit(solution)/shard_map/ppermute | solution.py:278
  82.7 2.5 %collective-permute-start.13 = (bf16[2,64,768]{2,1,0:T(8,128)(2,1)S(1)}, bf16[2,64,768]{2,1,0:T(8,128)(2,1)S(1)}, u32[]{:S(2)}, u32[]{:S(2)}) collective-permute-start(bf16[2,64,768]{2,1,0:T(8,128)(2,1)S(1)} %get-tuple-element.44), channel_id=1, source_target_pairs={{0,1},{1,0},{2,3},{3,2},{4,5},{5,4},{6,7},{7,6},{8,9},{9,8},{10,11... | collective-permute-start | bytes 589832 | tf_op jit(solution)/shard_map/ppermute | solution.py:278

commit v7 on v6

--- a/solution.py
+++ b/solution.py
@@ -241,24 +241,50 @@
     c, x = lax.axis_index("c"), lax.axis_index("x")
     half = own.shape[0] // 2
     width = own.shape[1]
-    parts = [(block.at[i], across, i) for block, across in ((here, 0), (left, 3), (right, 1)) for i in range(2)]
-    parts += [(far_0.at[0], 2, 0), (far_1.at[0], 2, 1)]
-    copies = []
-    for k, (part, across, i) in enumerate(parts):
-        e = lax.rem(x + across, NX) * 2 + i
-        copies.append(pltpu.make_async_copy(part.at[:GROUP], weights.at[e], arrived.at[2 * k]))
-        copies.append(pltpu.make_async_copy(part.at[GROUP:], extras.at[e], arrived.at[2 * k + 1]))
-    for copy in copies:
-        copy.start()
+    columns = (
+        (here.at[0], here.at[1]),
+        (right.at[0], right.at[1]),
+        (far_0.at[0], far_1.at[0]),
+        (left.at[0], left.at[1]),
+    )
+
+    def copies(source, column):
+        return [
+            copy
+            for i, part in enumerate(column)
+            for copy in (
+                pltpu.make_async_copy(
+                    part.at[:GROUP], weights.at[2 * source + i], arrived.at[4 * source + 2 * i]
+                ),
+                pltpu.make_async_copy(
+                    part.at[GROUP:], extras.at[2 * source + i], arrived.at[4 * source + 2 * i + 1]
+                ),
+            )
+        ]
+
+    def wait(source):
+        for copy in copies(source, columns[0]):
+            copy.wait()
+
+    for source in range(NX):
+        for across, column in enumerate(columns):
+
+            @pl.when(lax.rem(x + across, NX) == source)
+            def _():
+                for copy in copies(source, column):
+                    copy.start()
+
     rows = jnp.concatenate([own[...], other[...]], axis=0)
-    for copy in copies:
-        copy.wait()
+    wait(0)
+    wait(1)
 
     def plain(tiles):
         return tiles.astype(jnp.float32).reshape(-1, width).astype(jnp.bfloat16)
 
     gate = jnp.dot(rows, weights[0:3].reshape(width, width), preferred_element_type=jnp.float32)
+    wait(2)
     up = jnp.dot(rows, weights[3:6].reshape(width, width), preferred_element_type=jnp.float32)
+    wait(3)
     out_row, in_row = iotas((GROUP * TILE, GROUP * TILE))
     onehot = in_row == out_row % TILE * GROUP + out_row // TILE
     last = reorder(onehot, plain(extras[...])).reshape(GROUP, 1, TILE, width)

time: 87.3 us -> 87.3 us (level)
  no operation moved by 1% of the time
where the time goes in v7:
time: 87.3 us; the launch traced here: 86.2 us
  starting transfers between devices  41.1 us (47%)
  waiting for transfers between devices  27.5 us (32%)
  Pallas kernels  16.7 us (19%)
    pallas_call x12, Pallas kernels, kernel(): pl.pallas_call(f, grid=(1,), out_shape=outs, in_specs=specs, out_specs=tu...  16.7 us
    all_to_all x1, waiting for transfers between devices, body(): lax.all_to_all(pieces.reshape(GROUP, both, width + 128), PARTICLE, 0, 0)  11.9 us
    all_to_all x1, starting transfers between devices, body(): lax.all_to_all(pieces.reshape(GROUP, both, width + 128), PARTICLE, 0, 0)  11.9 us
    ppermute x4, starting transfers between devices, swap_cores(): return lax.ppermute(value, 'c', [(0, 1), (1, 0)])  9.59 us
    all_to_all x1, starting transfers between devices, body(): mine = lax.all_to_all(picked, PARTICLE, 0, 0)  7.9 us
    ppermute x6, starting transfers between devices, others(): lax.ppermute(value, axis, [(i, (i + k) % size) for i in range(size)])  7.33 us
    ppermute x6, waiting for transfers between devices, others(): lax.ppermute(value, axis, [(i, (i + k) % size) for i in range(size)])  6.68 us
    all_to_all x1, waiting for transfers between devices, body(): mine = lax.all_to_all(picked, PARTICLE, 0, 0)  5.14 us
  transfers between devices with their start and end apart: 16, of which 10 were waited for; matrix products, arithmetic and copies ran while one was open for 0% of the time, Pallas kernels for 13%

profile of v7, /device:TPU:1, one launch (start us, length us, event | category | flops | bytes accessed | tf_op | source)
XLA Modules:
  0.0 86.2 jit_solution(13042297982245364787)
XLA Ops:
  0.0 2.1 %spread.1 = bf16[16,2,8,896]{3,2,1,0:T(8,128)(2,1)} custom-call(s32[2]{0:T(128)} %ancestors.1, bf16[2,64,768]{2,1,0:T(8,128)(2,1)} %states.1, bf16[2,24,1536]{2,1,0:T(8,128)(2,1)} %w_in.1, bf16[24,1536]{1,0:T(8,128)(2,1)} %w_out.1), custom_call_target="tpu_custom_call" | custom-call | flops 1000000000 | tf_op jit(solution)/shard_map/spread/pallas_call | solution.py:319
  2.1 11.9 %all-to-all-start = ((bf16[32,8,896]{2,1,0:T(8,128)(2,1)}), bf16[32,8,896]{2,1,0:T(8,128)(2,1)S(1)}, u32[]{:S(2)}, u32[]{:S(2)}) async-start(bf16[32,8,896]{2,1,0:T(8,128)(2,1)} %bitcast.8), calls=%async_computation | async-start | bytes 917504 | tf_op jit(solution)/shard_map/all_to_all | solution.py:353
  13.9 1.0 %collective-permute-start.1 = (bf16[16,64,512]{2,1,0:T(8,128)(2,1)}, bf16[16,64,512]{2,1,0:T(8,128)(2,1)}, u32[]{:S(2)}, u32[]{:S(2)}) collective-permute-start(bf16[16,64,512]{2,1,0:T(8,128)(2,1)} %bias_own.1), channel_id=1, source_target_pairs={{0,1},{1,0},{2,3},{3,2},{4,5},{5,4},{6,7},{7,6},{8,9},{9,8},{10,11... | collective-permute-start | bytes 3145736 | tf_op jit(solution)/shard_map/ppermute | solution.py:304
  15.0 11.9 %all-to-all-done.pieces = bf16[32,8,896]{2,1,0:T(8,128)(2,1)S(1)} async-done(((bf16[32,8,896]{2,1,0:T(8,128)(2,1)}), bf16[32,8,896]{2,1,0:T(8,128)(2,1)S(1)}, u32[]{:S(2)}, u32[]{:S(2)}) %all-to-all-start) | async-done | bytes 458784 | tf_op jit(solution)/shard_map/all_to_all | solution.py:353
  26.8 0.3 unpack.1
  27.1 2.8 %collective-permute-start.5 = (bf16[288,384]{1,0:T(8,128)(2,1)S(1)}, bf16[288,384]{1,0:T(8,128)(2,1)S(1)}, u32[]{:S(2)}, u32[]{:S(2)}) collective-permute-start(bf16[288,384]{1,0:T(8,128)(2,1)S(1)} %get-tuple-element.29.w0), channel_id=1, source_target_pairs={{0,6},{2,0},{4,2},{6,4},{1,7},{3,1},{5,3},{7,5},{8,14},{10,8},{12,... | collective-permute-start | bytes 663560 | tf_op jit(solution)/shard_map/ppermute | solution.py:309
  30.0 0.4 collective-permute-start.4
  30.3 0.7 collective-permute-start.3
  31.0 0.9 %pick.1 = bf16[32,8,384]{2,1,0:T(8,128)(2,1)} custom-call(bf16[256,256]{1,0:T(8,128)(2,1)S(1)} %get-tuple-element.25.onehot, bf16[256,384]{1,0:T(8,128)(2,1)S(1)} %get-tuple-element.26.states), custom_call_target="tpu_custom_call" | custom-call | flops 1000000000 | tf_op jit(solution)/shard_map/pick/pallas_call | solution.py:319
  31.9 7.9 %all-to-all-start.1 = ((bf16[32,8,384]{2,1,0:T(8,128)(2,1)}), bf16[32,8,384]{2,1,0:T(8,128)(2,1)}, u32[]{:S(2)}, u32[]{:S(2)}) async-start(bf16[32,8,384]{2,1,0:T(8,128)(2,1)} %pick.1), calls=%async_computation.1 | async-start | bytes 393216 | tf_op jit(solution)/shard_map/all_to_all | solution.py:385
  39.8 0.0 copy-start.2
  39.8 0.0 collective-permute-done.5.w3
  39.8 0.0 collective-permute-done.4.w2
  39.8 1.7 %collective-permute-done.3.w1 = bf16[288,384]{1,0:T(8,128)(2,1)S(1)} collective-permute-done((bf16[288,384]{1,0:T(8,128)(2,1)S(1)}, bf16[288,384]{1,0:T(8,128)(2,1)S(1)}, u32[]{:S(2)}, u32[]{:S(2)}) %collective-permute-start.3) | collective-permute-done | bytes 221216 | tf_op jit(solution)/shard_map/ppermute | solution.py:309
  41.6 1.0 %column.1 = bf16[2,288,768]{2,1,0:T(8,128)(2,1)} custom-call(bf16[288,384]{1,0:T(8,128)(2,1)S(1)} %get-tuple-element.29.w0, bf16[288,384]{1,0:T(8,128)(2,1)S(1)} %collective-permute-done.3.w1, bf16[288,384]{1,0:T(8,128)(2,1)S(1)} %collective-permute-done.4.w2, bf16[288,384]{1,0:T(8,128)(2,1)S(1)} %collective-permute-done.5.w3), custom_call_target="tpu_custom_call" | custom-call | flops 1000000000 | tf_op jit(solution)/shard_map/column/pallas_call | solution.py:319
  42.6 0.0 copy-start
  42.6 1.4 %collective-permute-start.7 = (bf16[2,288,768]{2,1,0:T(8,128)(2,1)}, bf16[2,288,768]{2,1,0:T(8,128)(2,1)}, u32[]{:S(2)}, u32[]{:S(2)}) collective-permute-start(bf16[2,288,768]{2,1,0:T(8,128)(2,1)} %column.1), channel_id=1, source_target_pairs={{0,192},{64,0},{128,64},{192,128},{1,193},{65,1},{129,65},{193,129... | collective-permute-start | bytes 2654216 | tf_op jit(solution)/shard_map/ppermute | solution.py:383
  44.0 0.1 collective-permute-start.6
  44.1 5.1 %all-to-all-done.1.mine = bf16[32,8,384]{2,1,0:T(8,128)(2,1)} async-done(((bf16[32,8,384]{2,1,0:T(8,128)(2,1)}), bf16[32,8,384]{2,1,0:T(8,128)(2,1)}, u32[]{:S(2)}, u32[]{:S(2)}) %all-to-all-start.1) | async-done | bytes 196640 | tf_op jit(solution)/shard_map/all_to_all | solution.py:385
  49.2 3.8 %collective-permute-start = (bf16[32,8,384]{2,1,0:T(8,128)(2,1)}, bf16[32,8,384]{2,1,0:T(8,128)(2,1)S(1)}, u32[]{:S(2)}, u32[]{:S(2)}) collective-permute-start(bf16[32,8,384]{2,1,0:T(8,128)(2,1)} %all-to-all-done.1.mine), channel_id=1, source_target_pairs={{0,1},{1,0},{2,3},{3,2},{4,5},{5,4},{6,7},{7,6},{8,9},{9,8},{10,11... | collective-permute-start | bytes 589832 | tf_op jit(solution)/shard_map/ppermute | solution.py:304
  52.9 0.0 collective-permute-done.1._bias.bias_other
  52.9 1.3 %collective-permute-done.theirs = bf16[32,8,384]{2,1,0:T(8,128)(2,1)S(1)} collective-permute-done((bf16[32,8,384]{2,1,0:T(8,128)(2,1)}, bf16[32,8,384]{2,1,0:T(8,128)(2,1)S(1)}, u32[]{:S(2)}, u32[]{:S(2)}) %collective-permute-start) | collective-permute-done | bytes 196640 | tf_op jit(solution)/shard_map/ppermute | solution.py:304
  54.2 0.0 copy-done.2
  54.2 1.2 %own.1 = (bf16[128,768]{1,0:T(8,128)(2,1)S(1)}, bf16[128,768]{1,0:T(8,128)(2,1)S(1)}) custom-call(bf16[32,8,384]{2,1,0:T(8,128)(2,1)} %all-to-all-done.1.mine, bf16[32,8,384]{2,1,0:T(8,128)(2,1)S(1)} %collective-permute-done.theirs, f32[768]{0:T(1024)S(1)} %copy-done.2, bf16[16,64,512]{2,1,0:T(8,128)(2,1)} %collective-permute-done.1._bias.bias_other), custom_call_target="tpu_custom_call" | custom-call | flops 1000000000 | tf_op jit(solution)/shard_map/own/pallas_call | solution.py:319
  55.5 2.1 %collective-permute-start.9 = (bf16[128,768]{1,0:T(8,128)(2,1)S(1)}, bf16[128,768]{1,0:T(8,128)(2,1)S(1)}, u32[]{:S(2)}, u32[]{:S(2)}) collective-permute-start(bf16[128,768]{1,0:T(8,128)(2,1)S(1)} %get-tuple-element.27.normed), channel_id=1, source_target_pairs={{0,6},{2,0},{4,2},{6,4},{1,7},{3,1},{5,3},{7,5},{8,14},{10,8},{12,... | collective-permute-start | bytes 589832 | tf_op jit(solution)/shard_map/ppermute | solution.py:309
  57.5 1.4 %collective-permute-start.8 = (bf16[128,768]{1,0:T(8,128)(2,1)S(1)}, bf16[128,768]{1,0:T(8,128)(2,1)S(1)}, u32[]{:S(2)}, u32[]{:S(2)}) collective-permute-start(bf16[128,768]{1,0:T(8,128)(2,1)S(1)} %get-tuple-element.27.normed), channel_id=1, source_target_pairs={{0,4},{2,6},{4,0},{6,2},{1,5},{3,7},{5,1},{7,3},{8,12},{10,14},{12... | collective-permute-start | bytes 589832 | tf_op jit(solution)/shard_map/ppermute | solution.py:309
  58.9 0.0 collective-permute-start.2
  58.9 0.0 copy-done
  58.9 0.6 project.1
  59.6 2.5 %collective-permute-done.9.normed = bf16[128,768]{1,0:T(8,128)(2,1)S(1)} collective-permute-done((bf16[128,768]{1,0:T(8,128)(2,1)S(1)}, bf16[128,768]{1,0:T(8,128)(2,1)S(1)}, u32[]{:S(2)}, u32[]{:S(2)}) %collective-permute-start.9) | collective-permute-done | bytes 196640 | tf_op jit(solution)/shard_map/ppermute | solution.py:309
  62.1 0.5 other.5
  62.6 2.3 %collective-permute-done.8.normed = bf16[128,768]{1,0:T(8,128)(2,1)S(1)} collective-permute-done((bf16[128,768]{1,0:T(8,128)(2,1)S(1)}, bf16[128,768]{1,0:T(8,128)(2,1)S(1)}, u32[]{:S(2)}, u32[]{:S(2)}) %collective-permute-start.8) | collective-permute-done | bytes 196640 | tf_op jit(solution)/shard_map/ppermute | solution.py:309
  64.9 0.5 other.3
  65.4 0.0 collective-permute-done.7.right
  65.4 0.4 collective-permute-done.6.left
  65.7 1.2 %halves.1 = (bf16[1,288,768]{2,1,0:T(8,128)(2,1)S(1)}, bf16[1,288,768]{2,1,0:T(8,128)(2,1)S(1)}) custom-call(bf16[2,288,768]{2,1,0:T(8,128)(2,1)} %collective-permute-done.6.left, bf16[2,288,768]{2,1,0:T(8,128)(2,1)} %collective-permute-done.7.right, bf16[128,768]{1,0:T(8,128)(2,1)S(1)} %get-tuple-element.30._after.k2), custom_call_target="tpu_custom_call" | custom-call | flops 1000000000 | tf_op jit(solution)/shard_map/halves/pallas_call | solution.py:319
  66.9 0.1 collective-permute-start.11
  67.0 0.0 copy-start.1
  67.0 0.0 copy-start.3
  67.0 0.0 copy-start.4
  67.0 0.0 copy-start.5
  67.0 2.9 %collective-permute-start.12 = (bf16[1,288,768]{2,1,0:T(8,128)(2,1)S(1)}, bf16[1,288,768]{2,1,0:T(8,128)(2,1)S(1)}, u32[]{:S(2)}, u32[]{:S(2)}) collective-permute-start(bf16[1,288,768]{2,1,0:T(8,128)(2,1)S(1)} %get-tuple-element.32.refs_1_._right), channel_id=1, source_target_pairs={{0,192},{64,0},{128,64},{192,128},{1,193},{65,1},{129,65},{193,129... | collective-permute-start | bytes 1327112 | tf_op jit(solution)/shard_map/ppermute | solution.py:418
  69.9 0.1 collective-permute-done.2.normed
  70.1 0.5 other.4
  70.6 0.0 copy-done.1
  70.6 0.0 copy-done.3
  70.6 0.0 copy-done.4
  70.6 0.0 copy-done.5
  70.6 4.4 %attention.1 = (f32[128,768]{1,0:T(8,128)S(1)}, bf16[128,768]{1,0:T(8,128)(2,1)S(1)}) custom-call(bf16[128,768]{1,0:T(8,128)(2,1)S(1)} %get-tuple-element.28.k0, bf16[128,768]{1,0:T(8,128)(2,1)S(1)} %get-tuple-element.33.k1, bf16[128,768]{1,0:T(8,128)(2,1)S(1)} %get-tuple-element.30._after.k2, bf16[128,768]{1,0:T(8,128)(2,1)S(1)} %get-tuple-element.34.k3, ...), custom_call_target="tpu_custom_call" | custom-call | flops 4000000000 | tf_op jit(solution)/shard_map/attention/pallas_call | solution.py:319
  75.0 3.3 %collective-permute-start.10 = (bf16[128,768]{1,0:T(8,128)(2,1)S(1)}, bf16[128,768]{1,0:T(8,128)(2,1)S(1)}, u32[]{:S(2)}, u32[]{:S(2)}) collective-permute-start(bf16[128,768]{1,0:T(8,128)(2,1)S(1)} %get-tuple-element.41.own), channel_id=1, source_target_pairs={{0,1},{1,0},{2,3},{3,2},{4,5},{5,4},{6,7},{7,6},{8,9},{9,8},{10,11... | collective-permute-start | bytes 589832 | tf_op jit(solution)/shard_map/ppermute | solution.py:304
  78.3 1.1 %collective-permute-done.10.other = bf16[128,768]{1,0:T(8,128)(2,1)S(1)} collective-permute-done((bf16[128,768]{1,0:T(8,128)(2,1)S(1)}, bf16[128,768]{1,0:T(8,128)(2,1)S(1)}, u32[]{:S(2)}, u32[]{:S(2)}) %collective-permute-start.10) | collective-permute-done | bytes 196640 | tf_op jit(solution)/shard_map/ppermute | solution.py:304
  79.4 0.0 collective-permute-done.11
  79.4 0.0 collective-permute-done.12
  79.4 3.5 %transition.1 = (f32[2,64,768]{2,1,0:T(8,128)S(1)}, bf16[2,64,768]{2,1,0:T(8,128)(2,1)S(1)}) custom-call(bf16[128,768]{1,0:T(8,128)(2,1)S(1)} %get-tuple-element.41.own, bf16[128,768]{1,0:T(8,128)(2,1)S(1)} %collective-permute-done.10.other, f32[128,768]{1,0:T(8,128)S(1)} %get-tuple-element.42.stream, bf16[2,36,8,768]{3,2,1,0:T(8,128)(2,1)} %bitcast.1.here, ...), custom_call_target="tpu_custom_call" | custom-call | flops 1000000000 | tf_op jit(solution)/shard_map/transition/pallas_call | solution.py:319
  83.0 1.5 %collective-permute-start.13 = (bf16[2,64,768]{2,1,0:T(8,128)(2,1)S(1)}, bf16[2,64,768]{2,1,0:T(8,128)(2,1)S(1)}, u32[]{:S(2)}, u32[]{:S(2)}) collective-permute-start(bf16[2,64,768]{2,1,0:T(8,128)(2,1)S(1)} %get-tuple-element.44), channel_id=1, source_target_pairs={{0,1},{1,0},{2,3},{3,2},{4,5},{5,4},{6,7},{7,6},{8,9},{9,8},{10,11... | collective-permute-start | bytes 589832 | tf_op jit(solution)/shard_map/ppermute | solution.py:304
  84.4 1.1 %collective-permute-done.13 = bf16[2,64,768]{2,1,0:T(8,128)(2,1)S(1)} collective-permute-done((bf16[2,64,768]{2,1,0:T(8,128)(2,1)S(1)}, bf16[2,64,768]{2,1,0:T(8,128)(2,1)S(1)}, u32[]{:S(2)}, u32[]{:S(2)}) %collective-permute-start.13) | collective-permute-done | bytes 196640 | tf_op jit(solution)/shard_map/ppermute | solution.py:304
  85.5 0.7 add_convert_fusion
Async XLA Ops:
  2.1 24.8 %all-to-all-start = ((bf16[32,8,896]{2,1,0:T(8,128)(2,1)}), bf16[32,8,896]{2,1,0:T(8,128)(2,1)S(1)}, u32[]{:S(2)}, u32[]{:S(2)}) async-start(bf16[32,8,896]{2,1,0:T(8,128)(2,1)} %bitcast.8), calls=%async_computation | async-start | bytes 917504 | tf_op jit(solution)/shard_map/all_to_all | solution.py:353
  13.9 39.0 %collective-permute-start.1 = (bf16[16,64,512]{2,1,0:T(8,128)(2,1)}, bf16[16,64,512]{2,1,0:T(8,128)(2,1)}, u32[]{:S(2)}, u32[]{:S(2)}) collective-permute-start(bf16[16,64,512]{2,1,0:T(8,128)(2,1)} %bias_own.1), channel_id=1, source_target_pairs={{0,1},{1,0},{2,3},{3,2},{4,5},{5,4},{6,7},{7,6},{8,9},{9,8},{10,11... | collective-permute-start | bytes 3145736 | tf_op jit(solution)/shard_map/ppermute | solution.py:304
  27.1 12.7 %collective-permute-start.5 = (bf16[288,384]{1,0:T(8,128)(2,1)S(1)}, bf16[288,384]{1,0:T(8,128)(2,1)S(1)}, u32[]{:S(2)}, u32[]{:S(2)}) collective-permute-start(bf16[288,384]{1,0:T(8,128)(2,1)S(1)} %get-tuple-element.29.w0), channel_id=1, source_target_pairs={{0,6},{2,0},{4,2},{6,4},{1,7},{3,1},{5,3},{7,5},{8,14},{10,8},{12,... | collective-permute-start | bytes 663560 | tf_op jit(solution)/shard_map/ppermute | solution.py:309
  30.0 9.9 %collective-permute-start.4 = (bf16[288,384]{1,0:T(8,128)(2,1)S(1)}, bf16[288,384]{1,0:T(8,128)(2,1)S(1)}, u32[]{:S(2)}, u32[]{:S(2)}) collective-permute-start(bf16[288,384]{1,0:T(8,128)(2,1)S(1)} %get-tuple-element.29.w0), channel_id=1, source_target_pairs={{0,4},{2,6},{4,0},{6,2},{1,5},{3,7},{5,1},{7,3},{8,12},{10,14},{12... | collective-permute-start | bytes 663560 | tf_op jit(solution)/shard_map/ppermute | solution.py:309
  30.3 11.2 %collective-permute-start.3 = (bf16[288,384]{1,0:T(8,128)(2,1)S(1)}, bf16[288,384]{1,0:T(8,128)(2,1)S(1)}, u32[]{:S(2)}, u32[]{:S(2)}) collective-permute-start(bf16[288,384]{1,0:T(8,128)(2,1)S(1)} %get-tuple-element.29.w0), channel_id=1, source_target_pairs={{0,2},{2,4},{4,6},{6,0},{1,3},{3,5},{5,7},{7,1},{8,10},{10,12},{12... | collective-permute-start | bytes 663560 | tf_op jit(solution)/shard_map/ppermute | solution.py:309
  31.9 17.3 %all-to-all-start.1 = ((bf16[32,8,384]{2,1,0:T(8,128)(2,1)}), bf16[32,8,384]{2,1,0:T(8,128)(2,1)}, u32[]{:S(2)}, u32[]{:S(2)}) async-start(bf16[32,8,384]{2,1,0:T(8,128)(2,1)} %pick.1), calls=%async_computation.1 | async-start | bytes 393216 | tf_op jit(solution)/shard_map/all_to_all | solution.py:385
  39.8 14.4 %copy-start.2 = (f32[768]{0:T(1024)S(1)}, f32[768]{0:T(1024)}, u32[]{:S(2)}) copy-start(f32[768]{0:T(1024)} %gain.1) | copy-start | bytes 9220
  42.6 16.4 %copy-start = (bf16[768,2304]{1,0:T(8,128)(2,1)S(1)}, bf16[768,2304]{1,0:T(8,128)(2,1)}, u32[]{:S(2)}) copy-start(bf16[768,2304]{1,0:T(8,128)(2,1)} %w_qkv.7) | copy-start | bytes 10616836
  42.6 22.8 %collective-permute-start.7 = (bf16[2,288,768]{2,1,0:T(8,128)(2,1)}, bf16[2,288,768]{2,1,0:T(8,128)(2,1)}, u32[]{:S(2)}, u32[]{:S(2)}) collective-permute-start(bf16[2,288,768]{2,1,0:T(8,128)(2,1)} %column.1), channel_id=1, source_target_pairs={{0,192},{64,0},{128,64},{192,128},{1,193},{65,1},{129,65},{193,129... | collective-permute-start | bytes 2654216 | tf_op jit(solution)/shard_map/ppermute | solution.py:383
  44.0 21.8 %collective-permute-start.6 = (bf16[2,288,768]{2,1,0:T(8,128)(2,1)}, bf16[2,288,768]{2,1,0:T(8,128)(2,1)}, u32[]{:S(2)}, u32[]{:S(2)}) collective-permute-start(bf16[2,288,768]{2,1,0:T(8,128)(2,1)} %column.1), channel_id=1, source_target_pairs={{0,64},{64,128},{128,192},{192,0},{1,65},{65,129},{129,193},{193,1... | collective-permute-start | bytes 2654216 | tf_op jit(solution)/shard_map/ppermute | solution.py:383
  49.2 5.0 %collective-permute-start = (bf16[32,8,384]{2,1,0:T(8,128)(2,1)}, bf16[32,8,384]{2,1,0:T(8,128)(2,1)S(1)}, u32[]{:S(2)}, u32[]{:S(2)}) collective-permute-start(bf16[32,8,384]{2,1,0:T(8,128)(2,1)} %all-to-all-done.1.mine), channel_id=1, source_target_pairs={{0,1},{1,0},{2,3},{3,2},{4,5},{5,4},{6,7},{7,6},{8,9},{9,8},{10,11... | collective-permute-start | bytes 589832 | tf_op jit(solution)/shard_map/ppermute | solution.py:304
  55.5 6.6 %collective-permute-start.9 = (bf16[128,768]{1,0:T(8,128)(2,1)S(1)}, bf16[128,768]{1,0:T(8,128)(2,1)S(1)}, u32[]{:S(2)}, u32[]{:S(2)}) collective-permute-start(bf16[128,768]{1,0:T(8,128)(2,1)S(1)} %get-tuple-element.27.normed), channel_id=1, source_target_pairs={{0,6},{2,0},{4,2},{6,4},{1,7},{3,1},{5,3},{7,5},{8,14},{10,8},{12,... | collective-permute-start | bytes 589832 | tf_op jit(solution)/shard_map/ppermute | solution.py:309
  57.5 7.3 %collective-permute-start.8 = (bf16[128,768]{1,0:T(8,128)(2,1)S(1)}, bf16[128,768]{1,0:T(8,128)(2,1)S(1)}, u32[]{:S(2)}, u32[]{:S(2)}) collective-permute-start(bf16[128,768]{1,0:T(8,128)(2,1)S(1)} %get-tuple-element.27.normed), channel_id=1, source_target_pairs={{0,4},{2,6},{4,0},{6,2},{1,5},{3,7},{5,1},{7,3},{8,12},{10,14},{12... | collective-permute-start | bytes 589832 | tf_op jit(solution)/shard_map/ppermute | solution.py:309
  58.9 11.1 %collective-permute-start.2 = (bf16[128,768]{1,0:T(8,128)(2,1)S(1)}, bf16[128,768]{1,0:T(8,128)(2,1)S(1)}, u32[]{:S(2)}, u32[]{:S(2)}) collective-permute-start(bf16[128,768]{1,0:T(8,128)(2,1)S(1)} %get-tuple-element.27.normed), channel_id=1, source_target_pairs={{0,2},{2,4},{4,6},{6,0},{1,3},{3,5},{5,7},{7,1},{8,10},{10,12},{12... | collective-permute-start | bytes 589832 | tf_op jit(solution)/shard_map/ppermute | solution.py:309
  66.9 12.5 %collective-permute-start.11 = (bf16[1,288,768]{2,1,0:T(8,128)(2,1)S(1)}, bf16[1,288,768]{2,1,0:T(8,128)(2,1)S(1)}, u32[]{:S(2)}, u32[]{:S(2)}) collective-permute-start(bf16[1,288,768]{2,1,0:T(8,128)(2,1)S(1)} %get-tuple-element.31.refs_0_._left), channel_id=1, source_target_pairs={{0,64},{64,128},{128,192},{192,0},{1,65},{65,129},{129,193},{193,1... | collective-permute-start | bytes 1327112 | tf_op jit(solution)/shard_map/ppermute | solution.py:418
  67.0 3.6 %copy-start.1 = (bf16[768,768]{1,0:T(8,128)(2,1)S(1)}, bf16[768,768]{1,0:T(8,128)(2,1)}, u32[]{:S(2)}) copy-start(bf16[768,768]{1,0:T(8,128)(2,1)} %w_o.1) | copy-start | bytes 3538948
  67.0 3.6 %copy-start.3 = (f32[768]{0:T(1024)S(1)}, f32[768]{0:T(1024)}, u32[]{:S(2)}) copy-start(f32[768]{0:T(1024)} %gain_ff.1) | copy-start | bytes 9220
  67.0 3.6 %copy-start.4 = (s32[512]{0:T(512)S(1)}, s32[512]{0:T(512)}, u32[]{:S(2)}) copy-start(s32[512]{0:T(512)} %mask.1) | copy-start | bytes 6148
  67.0 3.6 %copy-start.5 = (bf16[768,768]{1,0:T(8,128)(2,1)S(1)}, bf16[768,768]{1,0:T(8,128)(2,1)}, u32[]{:S(2)}) copy-start(bf16[768,768]{1,0:T(8,128)(2,1)} %constant.2.clone.order) | copy-start | bytes 3538948
  67.0 12.4 %collective-permute-start.12 = (bf16[1,288,768]{2,1,0:T(8,128)(2,1)S(1)}, bf16[1,288,768]{2,1,0:T(8,128)(2,1)S(1)}, u32[]{:S(2)}, u32[]{:S(2)}) collective-permute-start(bf16[1,288,768]{2,1,0:T(8,128)(2,1)S(1)} %get-tuple-element.32.refs_1_._right), channel_id=1, source_target_pairs={{0,192},{64,0},{128,64},{192,128},{1,193},{65,1},{129,65},{193,129... | collective-permute-start | bytes 1327112 | tf_op jit(solution)/shard_map/ppermute | solution.py:418
  75.0 4.4 %collective-permute-start.10 = (bf16[128,768]{1,0:T(8,128)(2,1)S(1)}, bf16[128,768]{1,0:T(8,128)(2,1)S(1)}, u32[]{:S(2)}, u32[]{:S(2)}) collective-permute-start(bf16[128,768]{1,0:T(8,128)(2,1)S(1)} %get-tuple-element.41.own), channel_id=1, source_target_pairs={{0,1},{1,0},{2,3},{3,2},{4,5},{5,4},{6,7},{7,6},{8,9},{9,8},{10,11... | collective-permute-start | bytes 589832 | tf_op jit(solution)/shard_map/ppermute | solution.py:304
  83.0 2.5 %collective-permute-start.13 = (bf16[2,64,768]{2,1,0:T(8,128)(2,1)S(1)}, bf16[2,64,768]{2,1,0:T(8,128)(2,1)S(1)}, u32[]{:S(2)}, u32[]{:S(2)}) collective-permute-start(bf16[2,64,768]{2,1,0:T(8,128)(2,1)S(1)} %get-tuple-element.44), channel_id=1, source_target_pairs={{0,1},{1,0},{2,3},{3,2},{4,5},{5,4},{6,7},{7,6},{8,9},{9,8},{10,11... | collective-permute-start | bytes 589832 | tf_op jit(solution)/shard_map/ppermute | solution.py:304

commit v8 on v6

--- a/solution.py
+++ b/solution.py
@@ -376,7 +376,7 @@
         halves_kernel,
         "halves",
         [ANY] * 3,
-        (left, right, made[0][0]),
+        (left, right, made[1][0]),
         [((1,) + column.shape[1:], bf16)] * 2,
         out_spec=ANY,
         scratch=[pltpu.SemaphoreType.DMA((2,))],

time: 87.3 us -> 88.2 us (1.010); the launches traced: 85.9 us -> 87.8 us
  waiting for transfers between devices: 27.5 us -> 29.7 us
    ppermute x6, waiting for transfers between devices: 6.68 us -> 8.16 us  [others(): lax.ppermute(value, axis, [(i, (i + k) % size) for i in range(size)])]
    ppermute x1, waiting for transfers between devices: 0.01 us -> 1.09 us  [body(): lax.ppermute(left_half, 'x', forward)]
    ppermute x4, starting transfers between devices: 9.59 us -> 8.65 us  [swap_cores(): return lax.ppermute(value, 'c', [(0, 1), (1, 0)])]
  transfers between devices with their start and end apart: 16 -> 16, of which waited for: 10 -> 9; matrix products, arithmetic and copies ran while one was open for 0% -> 0% of each run, Pallas kernels for 13% -> 13%
where the time goes in v8:
time: 88.2 us; the launch traced here: 87.8 us
  starting transfers between devices  40.8 us (46%)
  waiting for transfers between devices  29.7 us (34%)
  Pallas kernels  16.4 us (19%)
    pallas_call x12, Pallas kernels, kernel(): pl.pallas_call(f, grid=(1,), out_shape=outs, in_specs=specs, out_specs=tu...  16.4 us
    all_to_all x1, waiting for transfers between devices, body(): lax.all_to_all(pieces.reshape(GROUP, both, width + 128), PARTICLE, 0, 0)  11.9 us
    all_to_all x1, starting transfers between devices, body(): lax.all_to_all(pieces.reshape(GROUP, both, width + 128), PARTICLE, 0, 0)  11.9 us
    ppermute x4, starting transfers between devices, swap_cores(): return lax.ppermute(value, 'c', [(0, 1), (1, 0)])  8.65 us
    ppermute x6, waiting for transfers between devices, others(): lax.ppermute(value, axis, [(i, (i + k) % size) for i in range(size)])  8.16 us
    ppermute x6, starting transfers between devices, others(): lax.ppermute(value, axis, [(i, (i + k) % size) for i in range(size)])  7.94 us
    all_to_all x1, starting transfers between devices, body(): mine = lax.all_to_all(picked, PARTICLE, 0, 0)  7.9 us
    all_to_all x1, waiting for transfers between devices, body(): mine = lax.all_to_all(picked, PARTICLE, 0, 0)  5.14 us
  transfers between devices with their start and end apart: 16, of which 9 were waited for; matrix products, arithmetic and copies ran while one was open for 0% of the time, Pallas kernels for 13%

profile of v8, /device:TPU:1, one launch (start us, length us, event | category | flops | bytes accessed | tf_op | source)
XLA Modules:
  0.0 87.8 jit_solution(6415483425256551520)
XLA Ops:
  0.0 2.1 %spread.1 = bf16[16,2,8,896]{3,2,1,0:T(8,128)(2,1)} custom-call(s32[2]{0:T(128)} %ancestors.1, bf16[2,64,768]{2,1,0:T(8,128)(2,1)} %states.1, bf16[2,24,1536]{2,1,0:T(8,128)(2,1)} %w_in.1, bf16[24,1536]{1,0:T(8,128)(2,1)} %w_out.1), custom_call_target="tpu_custom_call" | custom-call | flops 1000000000 | tf_op jit(solution)/shard_map/spread/pallas_call | solution.py:293
  2.1 11.9 %all-to-all-start = ((bf16[32,8,896]{2,1,0:T(8,128)(2,1)}), bf16[32,8,896]{2,1,0:T(8,128)(2,1)S(1)}, u32[]{:S(2)}, u32[]{:S(2)}) async-start(bf16[32,8,896]{2,1,0:T(8,128)(2,1)} %bitcast.8), calls=%async_computation | async-start | bytes 917504 | tf_op jit(solution)/shard_map/all_to_all | solution.py:327
  13.9 1.0 %collective-permute-start.1 = (bf16[16,64,512]{2,1,0:T(8,128)(2,1)}, bf16[16,64,512]{2,1,0:T(8,128)(2,1)}, u32[]{:S(2)}, u32[]{:S(2)}) collective-permute-start(bf16[16,64,512]{2,1,0:T(8,128)(2,1)} %bias_own.1), channel_id=1, source_target_pairs={{0,1},{1,0},{2,3},{3,2},{4,5},{5,4},{6,7},{7,6},{8,9},{9,8},{10,11... | collective-permute-start | bytes 3145736 | tf_op jit(solution)/shard_map/ppermute | solution.py:278
  15.0 11.9 %all-to-all-done.pieces = bf16[32,8,896]{2,1,0:T(8,128)(2,1)S(1)} async-done(((bf16[32,8,896]{2,1,0:T(8,128)(2,1)}), bf16[32,8,896]{2,1,0:T(8,128)(2,1)S(1)}, u32[]{:S(2)}, u32[]{:S(2)}) %all-to-all-start) | async-done | bytes 458784 | tf_op jit(solution)/shard_map/all_to_all | solution.py:327
  26.8 0.3 unpack.1
  27.1 2.8 %collective-permute-start.5 = (bf16[288,384]{1,0:T(8,128)(2,1)S(1)}, bf16[288,384]{1,0:T(8,128)(2,1)S(1)}, u32[]{:S(2)}, u32[]{:S(2)}) collective-permute-start(bf16[288,384]{1,0:T(8,128)(2,1)S(1)} %get-tuple-element.29.w0), channel_id=1, source_target_pairs={{0,6},{2,0},{4,2},{6,4},{1,7},{3,1},{5,3},{7,5},{8,14},{10,8},{12,... | collective-permute-start | bytes 663560 | tf_op jit(solution)/shard_map/ppermute | solution.py:283
  30.0 0.4 collective-permute-start.4
  30.3 0.7 collective-permute-start.3
  31.0 0.9 %pick.1 = bf16[32,8,384]{2,1,0:T(8,128)(2,1)} custom-call(bf16[256,256]{1,0:T(8,128)(2,1)S(1)} %get-tuple-element.25.onehot, bf16[256,384]{1,0:T(8,128)(2,1)S(1)} %get-tuple-element.26.states), custom_call_target="tpu_custom_call" | custom-call | flops 1000000000 | tf_op jit(solution)/shard_map/pick/pallas_call | solution.py:293
  31.9 7.9 %all-to-all-start.1 = ((bf16[32,8,384]{2,1,0:T(8,128)(2,1)}), bf16[32,8,384]{2,1,0:T(8,128)(2,1)}, u32[]{:S(2)}, u32[]{:S(2)}) async-start(bf16[32,8,384]{2,1,0:T(8,128)(2,1)} %pick.1), calls=%async_computation.1 | async-start | bytes 393216 | tf_op jit(solution)/shard_map/all_to_all | solution.py:359
  39.8 0.0 copy-start.2
  39.8 0.0 collective-permute-done.5.w3
  39.8 0.0 collective-permute-done.4.w2
  39.8 1.7 %collective-permute-done.3.w1 = bf16[288,384]{1,0:T(8,128)(2,1)S(1)} collective-permute-done((bf16[288,384]{1,0:T(8,128)(2,1)S(1)}, bf16[288,384]{1,0:T(8,128)(2,1)S(1)}, u32[]{:S(2)}, u32[]{:S(2)}) %collective-permute-start.3) | collective-permute-done | bytes 221216 | tf_op jit(solution)/shard_map/ppermute | solution.py:283
  41.6 1.0 %column.1 = bf16[2,288,768]{2,1,0:T(8,128)(2,1)} custom-call(bf16[288,384]{1,0:T(8,128)(2,1)S(1)} %get-tuple-element.29.w0, bf16[288,384]{1,0:T(8,128)(2,1)S(1)} %collective-permute-done.3.w1, bf16[288,384]{1,0:T(8,128)(2,1)S(1)} %collective-permute-done.4.w2, bf16[288,384]{1,0:T(8,128)(2,1)S(1)} %collective-permute-done.5.w3), custom_call_target="tpu_custom_call" | custom-call | flops 1000000000 | tf_op jit(solution)/shard_map/column/pallas_call | solution.py:293
  42.6 0.0 copy-start
  42.6 1.4 %collective-permute-start.7 = (bf16[2,288,768]{2,1,0:T(8,128)(2,1)}, bf16[2,288,768]{2,1,0:T(8,128)(2,1)}, u32[]{:S(2)}, u32[]{:S(2)}) collective-permute-start(bf16[2,288,768]{2,1,0:T(8,128)(2,1)} %column.1), channel_id=1, source_target_pairs={{0,192},{64,0},{128,64},{192,128},{1,193},{65,1},{129,65},{193,129... | collective-permute-start | bytes 2654216 | tf_op jit(solution)/shard_map/ppermute | solution.py:357
  44.0 0.1 collective-permute-start.6
  44.1 5.1 %all-to-all-done.1.mine = bf16[32,8,384]{2,1,0:T(8,128)(2,1)} async-done(((bf16[32,8,384]{2,1,0:T(8,128)(2,1)}), bf16[32,8,384]{2,1,0:T(8,128)(2,1)}, u32[]{:S(2)}, u32[]{:S(2)}) %all-to-all-start.1) | async-done | bytes 196640 | tf_op jit(solution)/shard_map/all_to_all | solution.py:359
  49.2 3.8 %collective-permute-start = (bf16[32,8,384]{2,1,0:T(8,128)(2,1)}, bf16[32,8,384]{2,1,0:T(8,128)(2,1)S(1)}, u32[]{:S(2)}, u32[]{:S(2)}) collective-permute-start(bf16[32,8,384]{2,1,0:T(8,128)(2,1)} %all-to-all-done.1.mine), channel_id=1, source_target_pairs={{0,1},{1,0},{2,3},{3,2},{4,5},{5,4},{6,7},{7,6},{8,9},{9,8},{10,11... | collective-permute-start | bytes 589832 | tf_op jit(solution)/shard_map/ppermute | solution.py:278
  52.9 0.0 collective-permute-done.1._bias.bias_other
  52.9 1.3 %collective-permute-done.theirs = bf16[32,8,384]{2,1,0:T(8,128)(2,1)S(1)} collective-permute-done((bf16[32,8,384]{2,1,0:T(8,128)(2,1)}, bf16[32,8,384]{2,1,0:T(8,128)(2,1)S(1)}, u32[]{:S(2)}, u32[]{:S(2)}) %collective-permute-start) | collective-permute-done | bytes 196640 | tf_op jit(solution)/shard_map/ppermute | solution.py:278
  54.2 0.0 copy-done.2
  54.2 1.2 %own.1 = (bf16[128,768]{1,0:T(8,128)(2,1)S(1)}, bf16[128,768]{1,0:T(8,128)(2,1)S(1)}) custom-call(bf16[32,8,384]{2,1,0:T(8,128)(2,1)} %all-to-all-done.1.mine, bf16[32,8,384]{2,1,0:T(8,128)(2,1)S(1)} %collective-permute-done.theirs, f32[768]{0:T(1024)S(1)} %copy-done.2, bf16[16,64,512]{2,1,0:T(8,128)(2,1)} %collective-permute-done.1._bias.bias_other), custom_call_target="tpu_custom_call" | custom-call | flops 1000000000 | tf_op jit(solution)/shard_map/own/pallas_call | solution.py:293
  55.5 1.5 %collective-permute-start.9 = (bf16[128,768]{1,0:T(8,128)(2,1)S(1)}, bf16[128,768]{1,0:T(8,128)(2,1)S(1)}, u32[]{:S(2)}, u32[]{:S(2)}) collective-permute-start(bf16[128,768]{1,0:T(8,128)(2,1)S(1)} %get-tuple-element.27.normed), channel_id=1, source_target_pairs={{0,4},{2,6},{4,0},{6,2},{1,5},{3,7},{5,1},{7,3},{8,12},{10,14},{12... | collective-permute-start | bytes 589832 | tf_op jit(solution)/shard_map/ppermute | solution.py:283
  57.0 2.5 %collective-permute-start.8 = (bf16[128,768]{1,0:T(8,128)(2,1)S(1)}, bf16[128,768]{1,0:T(8,128)(2,1)S(1)}, u32[]{:S(2)}, u32[]{:S(2)}) collective-permute-start(bf16[128,768]{1,0:T(8,128)(2,1)S(1)} %get-tuple-element.27.normed), channel_id=1, source_target_pairs={{0,6},{2,0},{4,2},{6,4},{1,7},{3,1},{5,3},{7,5},{8,14},{10,8},{12,... | collective-permute-start | bytes 589832 | tf_op jit(solution)/shard_map/ppermute | solution.py:283
  59.6 0.0 collective-permute-start.2
  59.6 0.0 copy-done
  59.6 0.6 project.1
  60.2 3.0 %collective-permute-done.9.normed = bf16[128,768]{1,0:T(8,128)(2,1)S(1)} collective-permute-done((bf16[128,768]{1,0:T(8,128)(2,1)S(1)}, bf16[128,768]{1,0:T(8,128)(2,1)S(1)}, u32[]{:S(2)}, u32[]{:S(2)}) %collective-permute-start.9) | collective-permute-done | bytes 196640 | tf_op jit(solution)/shard_map/ppermute | solution.py:283
  63.2 0.5 other.5
  63.7 3.5 %collective-permute-done.8.normed = bf16[128,768]{1,0:T(8,128)(2,1)S(1)} collective-permute-done((bf16[128,768]{1,0:T(8,128)(2,1)S(1)}, bf16[128,768]{1,0:T(8,128)(2,1)S(1)}, u32[]{:S(2)}, u32[]{:S(2)}) %collective-permute-start.8) | collective-permute-done | bytes 196640 | tf_op jit(solution)/shard_map/ppermute | solution.py:283
  67.1 0.5 other.3
  67.6 0.0 collective-permute-done.7.right
  67.6 0.0 collective-permute-done.6.left
  67.6 1.2 %halves.1 = (bf16[1,288,768]{2,1,0:T(8,128)(2,1)S(1)}, bf16[1,288,768]{2,1,0:T(8,128)(2,1)S(1)}) custom-call(bf16[2,288,768]{2,1,0:T(8,128)(2,1)} %collective-permute-done.6.left, bf16[2,288,768]{2,1,0:T(8,128)(2,1)} %collective-permute-done.7.right, bf16[128,768]{1,0:T(8,128)(2,1)S(1)} %get-tuple-element.30._after.k3), custom_call_target="tpu_custom_call" | custom-call | flops 1000000000 | tf_op jit(solution)/shard_map/halves/pallas_call | solution.py:293
  68.8 0.3 collective-permute-start.11
  69.1 0.0 copy-start.1
  69.1 0.0 copy-start.3
  69.1 0.0 copy-start.4
  69.1 0.0 copy-start.5
  69.1 2.7 %collective-permute-start.12 = (bf16[1,288,768]{2,1,0:T(8,128)(2,1)S(1)}, bf16[1,288,768]{2,1,0:T(8,128)(2,1)S(1)}, u32[]{:S(2)}, u32[]{:S(2)}) collective-permute-start(bf16[1,288,768]{2,1,0:T(8,128)(2,1)S(1)} %get-tuple-element.32.refs_1_._right), channel_id=1, source_target_pairs={{0,192},{64,0},{128,64},{192,128},{1,193},{65,1},{129,65},{193,129... | collective-permute-start | bytes 1327112 | tf_op jit(solution)/shard_map/ppermute | solution.py:392
  71.8 0.0 collective-permute-done.2.normed
  71.8 0.5 other.4
  72.3 0.0 copy-done.1
  72.3 0.0 copy-done.3
  72.3 0.0 copy-done.4
  72.3 0.0 copy-done.5
  72.3 4.4 %attention.1 = (f32[128,768]{1,0:T(8,128)S(1)}, bf16[128,768]{1,0:T(8,128)(2,1)S(1)}) custom-call(bf16[128,768]{1,0:T(8,128)(2,1)S(1)} %get-tuple-element.28.k0, bf16[128,768]{1,0:T(8,128)(2,1)S(1)} %get-tuple-element.33.k1, bf16[128,768]{1,0:T(8,128)(2,1)S(1)} %get-tuple-element.34.k2, bf16[128,768]{1,0:T(8,128)(2,1)S(1)} %get-tuple-element.30._after.k3, ...), custom_call_target="tpu_custom_call" | custom-call | flops 4000000000 | tf_op jit(solution)/shard_map/attention/pallas_call | solution.py:293
  76.7 1.7 %collective-permute-start.10 = (bf16[128,768]{1,0:T(8,128)(2,1)S(1)}, bf16[128,768]{1,0:T(8,128)(2,1)S(1)}, u32[]{:S(2)}, u32[]{:S(2)}) collective-permute-start(bf16[128,768]{1,0:T(8,128)(2,1)S(1)} %get-tuple-element.41.own), channel_id=1, source_target_pairs={{0,1},{1,0},{2,3},{3,2},{4,5},{5,4},{6,7},{7,6},{8,9},{9,8},{10,11... | collective-permute-start | bytes 589832 | tf_op jit(solution)/shard_map/ppermute | solution.py:278
  78.5 1.1 %collective-permute-done.10.other = bf16[128,768]{1,0:T(8,128)(2,1)S(1)} collective-permute-done((bf16[128,768]{1,0:T(8,128)(2,1)S(1)}, bf16[128,768]{1,0:T(8,128)(2,1)S(1)}, u32[]{:S(2)}, u32[]{:S(2)}) %collective-permute-start.10) | collective-permute-done | bytes 196640 | tf_op jit(solution)/shard_map/ppermute | solution.py:278
  79.6 1.1 %collective-permute-done.11 = bf16[1,288,768]{2,1,0:T(8,128)(2,1)S(1)} collective-permute-done((bf16[1,288,768]{2,1,0:T(8,128)(2,1)S(1)}, bf16[1,288,768]{2,1,0:T(8,128)(2,1)S(1)}, u32[]{:S(2)}, u32[]{:S(2)}) %collective-permute-start.11) | collective-permute-done | bytes 442400 | tf_op jit(solution)/shard_map/ppermute | solution.py:392
  80.6 0.0 collective-permute-done.12
  80.6 3.3 %transition.1 = (f32[2,64,768]{2,1,0:T(8,128)S(1)}, bf16[2,64,768]{2,1,0:T(8,128)(2,1)S(1)}) custom-call(bf16[128,768]{1,0:T(8,128)(2,1)S(1)} %get-tuple-element.41.own, bf16[128,768]{1,0:T(8,128)(2,1)S(1)} %collective-permute-done.10.other, f32[128,768]{1,0:T(8,128)S(1)} %get-tuple-element.42.stream, bf16[2,36,8,768]{3,2,1,0:T(8,128)(2,1)} %bitcast.1.here, ...), custom_call_target="tpu_custom_call" | custom-call | flops 1000000000 | tf_op jit(solution)/shard_map/transition/pallas_call | solution.py:293
  83.9 2.1 %collective-permute-start.13 = (bf16[2,64,768]{2,1,0:T(8,128)(2,1)S(1)}, bf16[2,64,768]{2,1,0:T(8,128)(2,1)S(1)}, u32[]{:S(2)}, u32[]{:S(2)}) collective-permute-start(bf16[2,64,768]{2,1,0:T(8,128)(2,1)S(1)} %get-tuple-element.44), channel_id=1, source_target_pairs={{0,1},{1,0},{2,3},{3,2},{4,5},{5,4},{6,7},{7,6},{8,9},{9,8},{10,11... | collective-permute-start | bytes 589832 | tf_op jit(solution)/shard_map/ppermute | solution.py:278
  86.0 1.1 %collective-permute-done.13 = bf16[2,64,768]{2,1,0:T(8,128)(2,1)S(1)} collective-permute-done((bf16[2,64,768]{2,1,0:T(8,128)(2,1)S(1)}, bf16[2,64,768]{2,1,0:T(8,128)(2,1)S(1)}, u32[]{:S(2)}, u32[]{:S(2)}) %collective-permute-start.13) | collective-permute-done | bytes 196640 | tf_op jit(solution)/shard_map/ppermute | solution.py:278
  87.1 0.7 add_convert_fusion
Async XLA Ops:
  2.1 24.8 %all-to-all-start = ((bf16[32,8,896]{2,1,0:T(8,128)(2,1)}), bf16[32,8,896]{2,1,0:T(8,128)(2,1)S(1)}, u32[]{:S(2)}, u32[]{:S(2)}) async-start(bf16[32,8,896]{2,1,0:T(8,128)(2,1)} %bitcast.8), calls=%async_computation | async-start | bytes 917504 | tf_op jit(solution)/shard_map/all_to_all | solution.py:327
  13.9 39.0 %collective-permute-start.1 = (bf16[16,64,512]{2,1,0:T(8,128)(2,1)}, bf16[16,64,512]{2,1,0:T(8,128)(2,1)}, u32[]{:S(2)}, u32[]{:S(2)}) collective-permute-start(bf16[16,64,512]{2,1,0:T(8,128)(2,1)} %bias_own.1), channel_id=1, source_target_pairs={{0,1},{1,0},{2,3},{3,2},{4,5},{5,4},{6,7},{7,6},{8,9},{9,8},{10,11... | collective-permute-start | bytes 3145736 | tf_op jit(solution)/shard_map/ppermute | solution.py:278
  27.1 12.7 %collective-permute-start.5 = (bf16[288,384]{1,0:T(8,128)(2,1)S(1)}, bf16[288,384]{1,0:T(8,128)(2,1)S(1)}, u32[]{:S(2)}, u32[]{:S(2)}) collective-permute-start(bf16[288,384]{1,0:T(8,128)(2,1)S(1)} %get-tuple-element.29.w0), channel_id=1, source_target_pairs={{0,6},{2,0},{4,2},{6,4},{1,7},{3,1},{5,3},{7,5},{8,14},{10,8},{12,... | collective-permute-start | bytes 663560 | tf_op jit(solution)/shard_map/ppermute | solution.py:283
  30.0 9.9 %collective-permute-start.4 = (bf16[288,384]{1,0:T(8,128)(2,1)S(1)}, bf16[288,384]{1,0:T(8,128)(2,1)S(1)}, u32[]{:S(2)}, u32[]{:S(2)}) collective-permute-start(bf16[288,384]{1,0:T(8,128)(2,1)S(1)} %get-tuple-element.29.w0), channel_id=1, source_target_pairs={{0,4},{2,6},{4,0},{6,2},{1,5},{3,7},{5,1},{7,3},{8,12},{10,14},{12... | collective-permute-start | bytes 663560 | tf_op jit(solution)/shard_map/ppermute | solution.py:283
  30.3 11.2 %collective-permute-start.3 = (bf16[288,384]{1,0:T(8,128)(2,1)S(1)}, bf16[288,384]{1,0:T(8,128)(2,1)S(1)}, u32[]{:S(2)}, u32[]{:S(2)}) collective-permute-start(bf16[288,384]{1,0:T(8,128)(2,1)S(1)} %get-tuple-element.29.w0), channel_id=1, source_target_pairs={{0,2},{2,4},{4,6},{6,0},{1,3},{3,5},{5,7},{7,1},{8,10},{10,12},{12... | collective-permute-start | bytes 663560 | tf_op jit(solution)/shard_map/ppermute | solution.py:283
  31.9 17.3 %all-to-all-start.1 = ((bf16[32,8,384]{2,1,0:T(8,128)(2,1)}), bf16[32,8,384]{2,1,0:T(8,128)(2,1)}, u32[]{:S(2)}, u32[]{:S(2)}) async-start(bf16[32,8,384]{2,1,0:T(8,128)(2,1)} %pick.1), calls=%async_computation.1 | async-start | bytes 393216 | tf_op jit(solution)/shard_map/all_to_all | solution.py:359
  39.8 14.4 %copy-start.2 = (f32[768]{0:T(1024)S(1)}, f32[768]{0:T(1024)}, u32[]{:S(2)}) copy-start(f32[768]{0:T(1024)} %gain.1) | copy-start | bytes 9220
  42.6 17.0 %copy-start = (bf16[768,2304]{1,0:T(8,128)(2,1)S(1)}, bf16[768,2304]{1,0:T(8,128)(2,1)}, u32[]{:S(2)}) copy-start(bf16[768,2304]{1,0:T(8,128)(2,1)} %w_qkv.7) | copy-start | bytes 10616836
  42.6 25.0 %collective-permute-start.7 = (bf16[2,288,768]{2,1,0:T(8,128)(2,1)}, bf16[2,288,768]{2,1,0:T(8,128)(2,1)}, u32[]{:S(2)}, u32[]{:S(2)}) collective-permute-start(bf16[2,288,768]{2,1,0:T(8,128)(2,1)} %column.1), channel_id=1, source_target_pairs={{0,192},{64,0},{128,64},{192,128},{1,193},{65,1},{129,65},{193,129... | collective-permute-start | bytes 2654216 | tf_op jit(solution)/shard_map/ppermute | solution.py:357
  44.0 23.7 %collective-permute-start.6 = (bf16[2,288,768]{2,1,0:T(8,128)(2,1)}, bf16[2,288,768]{2,1,0:T(8,128)(2,1)}, u32[]{:S(2)}, u32[]{:S(2)}) collective-permute-start(bf16[2,288,768]{2,1,0:T(8,128)(2,1)} %column.1), channel_id=1, source_target_pairs={{0,64},{64,128},{128,192},{192,0},{1,65},{65,129},{129,193},{193,1... | collective-permute-start | bytes 2654216 | tf_op jit(solution)/shard_map/ppermute | solution.py:357
  49.2 5.0 %collective-permute-start = (bf16[32,8,384]{2,1,0:T(8,128)(2,1)}, bf16[32,8,384]{2,1,0:T(8,128)(2,1)S(1)}, u32[]{:S(2)}, u32[]{:S(2)}) collective-permute-start(bf16[32,8,384]{2,1,0:T(8,128)(2,1)} %all-to-all-done.1.mine), channel_id=1, source_target_pairs={{0,1},{1,0},{2,3},{3,2},{4,5},{5,4},{6,7},{7,6},{8,9},{9,8},{10,11... | collective-permute-start | bytes 589832 | tf_op jit(solution)/shard_map/ppermute | solution.py:278
  55.5 7.7 %collective-permute-start.9 = (bf16[128,768]{1,0:T(8,128)(2,1)S(1)}, bf16[128,768]{1,0:T(8,128)(2,1)S(1)}, u32[]{:S(2)}, u32[]{:S(2)}) collective-permute-start(bf16[128,768]{1,0:T(8,128)(2,1)S(1)} %get-tuple-element.27.normed), channel_id=1, source_target_pairs={{0,4},{2,6},{4,0},{6,2},{1,5},{3,7},{5,1},{7,3},{8,12},{10,14},{12... | collective-permute-start | bytes 589832 | tf_op jit(solution)/shard_map/ppermute | solution.py:283
  57.0 10.1 %collective-permute-start.8 = (bf16[128,768]{1,0:T(8,128)(2,1)S(1)}, bf16[128,768]{1,0:T(8,128)(2,1)S(1)}, u32[]{:S(2)}, u32[]{:S(2)}) collective-permute-start(bf16[128,768]{1,0:T(8,128)(2,1)S(1)} %get-tuple-element.27.normed), channel_id=1, source_target_pairs={{0,6},{2,0},{4,2},{6,4},{1,7},{3,1},{5,3},{7,5},{8,14},{10,8},{12,... | collective-permute-start | bytes 589832 | tf_op jit(solution)/shard_map/ppermute | solution.py:283
  59.6 12.3 %collective-permute-start.2 = (bf16[128,768]{1,0:T(8,128)(2,1)S(1)}, bf16[128,768]{1,0:T(8,128)(2,1)S(1)}, u32[]{:S(2)}, u32[]{:S(2)}) collective-permute-start(bf16[128,768]{1,0:T(8,128)(2,1)S(1)} %get-tuple-element.27.normed), channel_id=1, source_target_pairs={{0,2},{2,4},{4,6},{6,0},{1,3},{3,5},{5,7},{7,1},{8,10},{10,12},{12... | collective-permute-start | bytes 589832 | tf_op jit(solution)/shard_map/ppermute | solution.py:283
  68.8 11.9 %collective-permute-start.11 = (bf16[1,288,768]{2,1,0:T(8,128)(2,1)S(1)}, bf16[1,288,768]{2,1,0:T(8,128)(2,1)S(1)}, u32[]{:S(2)}, u32[]{:S(2)}) collective-permute-start(bf16[1,288,768]{2,1,0:T(8,128)(2,1)S(1)} %get-tuple-element.31.refs_0_._left), channel_id=1, source_target_pairs={{0,64},{64,128},{128,192},{192,0},{1,65},{65,129},{129,193},{193,1... | collective-permute-start | bytes 1327112 | tf_op jit(solution)/shard_map/ppermute | solution.py:392
  69.1 3.2 %copy-start.1 = (bf16[768,768]{1,0:T(8,128)(2,1)S(1)}, bf16[768,768]{1,0:T(8,128)(2,1)}, u32[]{:S(2)}) copy-start(bf16[768,768]{1,0:T(8,128)(2,1)} %w_o.1) | copy-start | bytes 3538948
  69.1 3.2 %copy-start.3 = (f32[768]{0:T(1024)S(1)}, f32[768]{0:T(1024)}, u32[]{:S(2)}) copy-start(f32[768]{0:T(1024)} %gain_ff.1) | copy-start | bytes 9220
  69.1 3.2 %copy-start.4 = (s32[512]{0:T(512)S(1)}, s32[512]{0:T(512)}, u32[]{:S(2)}) copy-start(s32[512]{0:T(512)} %mask.1) | copy-start | bytes 6148
  69.1 3.2 %copy-start.5 = (bf16[768,768]{1,0:T(8,128)(2,1)S(1)}, bf16[768,768]{1,0:T(8,128)(2,1)}, u32[]{:S(2)}) copy-start(bf16[768,768]{1,0:T(8,128)(2,1)} %constant.2.clone.order) | copy-start | bytes 3538948
  69.1 11.5 %collective-permute-start.12 = (bf16[1,288,768]{2,1,0:T(8,128)(2,1)S(1)}, bf16[1,288,768]{2,1,0:T(8,128)(2,1)S(1)}, u32[]{:S(2)}, u32[]{:S(2)}) collective-permute-start(bf16[1,288,768]{2,1,0:T(8,128)(2,1)S(1)} %get-tuple-element.32.refs_1_._right), channel_id=1, source_target_pairs={{0,192},{64,0},{128,64},{192,128},{1,193},{65,1},{129,65},{193,129... | collective-permute-start | bytes 1327112 | tf_op jit(solution)/shard_map/ppermute | solution.py:392
  76.7 2.8 %collective-permute-start.10 = (bf16[128,768]{1,0:T(8,128)(2,1)S(1)}, bf16[128,768]{1,0:T(8,128)(2,1)S(1)}, u32[]{:S(2)}, u32[]{:S(2)}) collective-permute-start(bf16[128,768]{1,0:T(8,128)(2,1)S(1)} %get-tuple-element.41.own), channel_id=1, source_target_pairs={{0,1},{1,0},{2,3},{3,2},{4,5},{5,4},{6,7},{7,6},{8,9},{9,8},{10,11... | collective-permute-start | bytes 589832 | tf_op jit(solution)/shard_map/ppermute | solution.py:278
  83.9 3.2 %collective-permute-start.13 = (bf16[2,64,768]{2,1,0:T(8,128)(2,1)S(1)}, bf16[2,64,768]{2,1,0:T(8,128)(2,1)S(1)}, u32[]{:S(2)}, u32[]{:S(2)}) collective-permute-start(bf16[2,64,768]{2,1,0:T(8,128)(2,1)S(1)} %get-tuple-element.44), channel_id=1, source_target_pairs={{0,1},{1,0},{2,3},{3,2},{4,5},{5,4},{6,7},{7,6},{8,9},{9,8},{10,11... | collective-permute-start | bytes 589832 | tf_op jit(solution)/shard_map/ppermute | solution.py:278
